TPU v7x, 32 devices: a whole 2x2x4 slice. The times are simulated.
32 devices in a mesh: hit: 8 (over z, core), head: 4 (over y, x).
Axes of the slice: x: 2, y: 2, z: 4, core: 2. Of those that a mesh axis runs over, the one named last changes fastest.
Arguments:
- slots: bfloat16 [1024, 1024], replicated, may hold values from -700 to 700
- hits: bfloat16 [16384, 1024], P(('hit', 'head')), may hold values from -15 to 15
- hit_mask: int32 [16384], P('hit'), may hold values from 0 to 1, as said below
- q_weight: bfloat16 [1024, 1024], P(None, 'head'), may hold values from -0.1875 to 0.1875
- k_weight: bfloat16 [1024, 1024], replicated, may hold values from -0.1875 to 0.1875
- v_weight: bfloat16 [1024, 1024], replicated, may hold values from -0.1875 to 0.1875
- o_weight: bfloat16 [1024, 1024], P('head'), may hold values from -0.1875 to 0.1875
Outputs:
- attended: bfloat16 [1024, 1024], P('hit', 'head')
Inputs may be any that keep to these rules, and one draw needn't show every extreme that they name: `hit_mask`: within each group of 2048 hits the real hits form a prefix of 512 hits or more; in some group every hit is real.
All inputs are finite; a program needn't handle non-finite values.
Results may differ from a plain program's by a relative error of at most 0.0098.
Values may be sent and summed in bfloat16 or wider, within the bound.
No kernel may reach another device: no remote copies, remote signals or barrier semaphores. Data moves between devices by JAX's collectives and lax.ppermute only.
A program may use at most 128 MiB of HBM per device.

v0:
```python
import jax
import jax.numpy as jnp
from jax import lax
from jax.sharding import PartitionSpec as P

HEAD_DIM = 64


def attend(queries_head, keys_head, values_head, valid):
    scores = jnp.dot(queries_head, keys_head.T, preferred_element_type=jnp.float32) * HEAD_DIM ** (
        -0.5
    )
    scores = jnp.where(valid[None, :] > 0, scores, jnp.float32(-1e30))
    row_top = jnp.max(scores, axis=1)
    expo = jnp.exp(scores - row_top[:, None])
    totals = jnp.sum(expo, axis=1)
    weights = expo.astype(jnp.bfloat16)
    partial_value = jnp.dot(weights, values_head, preferred_element_type=jnp.float32)
    return (row_top, totals, partial_value)


def local(slots, hits, hit_mask, q_weight, k_weight, v_weight, o_weight):
    heads_here = q_weight.shape[1] // HEAD_DIM
    slot_count = slots.shape[0]
    queries = jnp.dot(slots, q_weight, preferred_element_type=jnp.float32).astype(jnp.bfloat16)
    local_hits = hits.shape[0]
    head_devs = lax.axis_size("head")
    keys = jnp.dot(hits, k_weight, preferred_element_type=jnp.float32).astype(jnp.bfloat16)
    values = jnp.dot(hits, v_weight, preferred_element_type=jnp.float32).astype(jnp.bfloat16)
    keys = keys.reshape(local_hits, head_devs, heads_here, HEAD_DIM)
    values = values.reshape(local_hits, head_devs, heads_here, HEAD_DIM)
    both = jnp.concatenate([keys, values], axis=3)
    moved = lax.all_to_all(both, "head", split_axis=1, concat_axis=0, tiled=True)
    key_vals = moved.reshape(moved.shape[0], heads_here, 2 * HEAD_DIM)
    block = min(512, slot_count)
    block_count = slot_count // block
    row_tops = []
    sums_list = []
    partials = []
    for head_pos in range(heads_here):
        queries_head = queries[:, head_pos * HEAD_DIM : (head_pos + 1) * HEAD_DIM].reshape(
            block_count, block, HEAD_DIM
        )
        keys_head = key_vals[:, head_pos, :HEAD_DIM]
        values_head = key_vals[:, head_pos, HEAD_DIM:]

        def per_block(query_block):
            return attend(query_block, keys_head, values_head, hit_mask)

        head_top, head_sums, head_part = lax.map(per_block, queries_head)
        row_tops.append(head_top.reshape(slot_count))
        sums_list.append(head_sums.reshape(slot_count))
        partials.append(head_part.reshape(slot_count, HEAD_DIM))
    row_top = jnp.stack(row_tops, axis=1)
    totals = jnp.stack(sums_list, axis=1)
    partial_value = jnp.concatenate(partials, axis=1)
    overall = lax.pmax(row_top, "hit")
    scale = jnp.exp(row_top - overall)
    numer, denom = (
        lax.psum_scatter(
            partial_value * jnp.repeat(scale, HEAD_DIM, axis=1),
            "hit",
            scatter_dimension=0,
            tiled=True,
        ),
        lax.psum_scatter(totals * scale, "hit", scatter_dimension=0, tiled=True),
    )
    mixed = (numer / jnp.repeat(denom, HEAD_DIM, axis=1)).astype(jnp.bfloat16)
    head_terms = jnp.dot(mixed, o_weight, preferred_element_type=jnp.float32)
    return lax.psum_scatter(head_terms, "head", scatter_dimension=1, tiled=True).astype(
        jnp.bfloat16
    )


def solution(mesh):
    placed = (P(), P(("hit", "head"), None), P("hit"), P(None, "head"), P(), P(), P("head", None))
    return jax.shard_map(
        local, mesh=mesh, in_specs=placed, out_specs=P("hit", "head"), check_vma=False
    )
```

profile of v0, /device:TPU:0, one launch (start us, length us, event | category | flops | bytes accessed | tf_op | source)
XLA Modules:
  0.0 309.2 jit_solution(2727608730771907905)
XLA Ops:
  8.1 3.5 %convolution_convert_fusion = bf16[512,1024]{1,0:T(8,128)(2,1)} fusion(bf16[512,1024]{1,0:T(8,128)(2,1)} %param.16, bf16[1024,1024]{1,0:T(8,128)(2,1)S(1)} %copy-done), kind=kOutput, calls=%fused_computation.61 | convolution fusion | flops 1074266112 | bytes 4194304 | tf_op jit(solution)/shard_map/dot_general | solution.py:29
  13.1 4.2 %convolution_convert_fusion.1 = bf16[512,1024]{1,0:T(8,128)(2,1)} fusion(bf16[512,1024]{1,0:T(8,128)(2,1)} %param.16, bf16[1024,1024]{1,0:T(8,128)(2,1)} %param.19), kind=kOutput, calls=%fused_computation.62 | convolution fusion | flops 1074266112 | bytes 4194304 | tf_op jit(solution)/shard_map/dot_general | solution.py:28
  22.3 5.3 %all-to-all-start = ((bf16[512,4,4,128]{0,3,2,1:T(8,128)(2,1)}), bf16[512,4,4,128]{0,3,2,1:T(8,128)(2,1)}, u32[]{:S(2)}, u32[]{:S(2)}) async-start(bf16[512,4,4,128]{0,3,2,1:T(8,128)(2,1)} %pad_maximum_fusion), calls=%async_computation | async-start | bytes 4194304 | tf_op jit(solution)/shard_map/all_to_all | solution.py:33
  32.7 20.7 %all-to-all-done = bf16[512,4,4,128]{0,3,2,1:T(8,128)(2,1)} async-done(((bf16[512,4,4,128]{0,3,2,1:T(8,128)(2,1)}), bf16[512,4,4,128]{0,3,2,1:T(8,128)(2,1)}, u32[]{:S(2)}, u32[]{:S(2)}) %all-to-all-start) | async-done | bytes 2097184 | tf_op jit(solution)/shard_map/all_to_all | solution.py:33
  53.3 4.1 %copy.38 = bf16[4,512,1,4,128]{4,1,0,3,2:T(8,128)(2,1)} copy(bf16[4,512,1,4,128]{1,4,3,0,2:T(8,128)(2,1)} %bitcast.20) | data formatting | bytes 4194304 | tf_op jit(solution)/shard_map/all_to_all | solution.py:33
  57.5 4.5 %slice_bitcast_fusion.6 = (bf16[2048,64]{1,0:T(8,128)(2,1)}, bf16[2048,64]{1,0:T(8,128)(2,1)}, bf16[2048,64]{1,0:T(8,128)(2,1)}, bf16[2048,64]{1,0:T(8,128)(2,1)...) fusion(bf16[2048,4,128]{2,0,1:T(8,128)(2,1)} %bitcast.181), kind=kLoop, calls=%fused_computation.71 | loop fusion | bytes 4194304 | tf_op jit(solution)/shard_map/squeeze | solution.py:45
  62.8 27.9 %while.59 = (s32[]{:T(128)}, f32[2,512]{1,0:T(2,128)S(1)}, f32[2,512]{1,0:T(2,128)S(1)}, f32[2,512,64]{1,0,2:T(2,128)}, s32[2048]{0:T(1024)S(1)}, /*index=5*/bf1...) while((s32[]{:T(128)}, f32[2,512]{1,0:T(2,128)S(1)}, ...), condition=%wide.region_15.16_spmd, body=%wide.region_12.15_spmd.sunk | while | flops 279970816 | bytes 14188669 | solution.py:50
  62.8 3.8 %fusion.124 = (f32[512]{0:T(512)S(1)}, f32[512,2048]{1,0:T(8,128)}) fusion(pred[2048]{0:T(1024)(128)(4,1)S(1)} %broadcast_compare_fusion.11, bf16[2048,64]{1,0:T(8,128)(2,1)} %get-tuple-element.645, bf16[2,512,64]{2,1,0:T(8,128)(2,1)} %get-tuple-element.644, s32[]{:T(128)S(6)} %copy.97), kind=kOutput, calls=%fused_computation.47.clone.1 | convolution fusion | flops 137362944 | bytes 4853764 | tf_op jit(solution)/shard_map/while/body/eval_jaxpr/dot_general | solution.py:10
  73.3 3.5 %dynamic_update_slice.61 = f32[2,512,64]{1,0,2:T(2,128)} dynamic-update-slice(f32[2,512,64]{1,0,2:T(2,128)} %get-tuple-element.632, f32[1,512,64]{1,0,2:T(1,128)S(1)} %copy.80, s32[]{:T(128)S(6)} %copy.97, s32[]{:T(128)} %constant.78.clone.1..sunk.3, s32[]{:T(128)} %constant.78.clone.1..sunk.3) | dynamic-update-slice | bytes 262148 | tf_op jit(solution)/shard_map/while/body/jit(dynamic_update_index_in_dim)/dynamic_update_slice | solution.py:50
  76.8 3.8 %fusion.124 = (f32[512]{0:T(512)S(1)}, f32[512,2048]{1,0:T(8,128)}) fusion(pred[2048]{0:T(1024)(128)(4,1)S(1)} %broadcast_compare_fusion.11, bf16[2048,64]{1,0:T(8,128)(2,1)} %get-tuple-element.645, bf16[2,512,64]{2,1,0:T(8,128)(2,1)} %get-tuple-element.644, s32[]{:T(128)S(6)} %copy.97), kind=kOutput, calls=%fused_computation.47.clone.1 | convolution fusion | flops 137362944 | bytes 4853764 | tf_op jit(solution)/shard_map/while/body/eval_jaxpr/dot_general | solution.py:10
  87.3 3.5 %dynamic_update_slice.61 = f32[2,512,64]{1,0,2:T(2,128)} dynamic-update-slice(f32[2,512,64]{1,0,2:T(2,128)} %get-tuple-element.632, f32[1,512,64]{1,0,2:T(1,128)S(1)} %copy.80, s32[]{:T(128)S(6)} %copy.97, s32[]{:T(128)} %constant.78.clone.1..sunk.3, s32[]{:T(128)} %constant.78.clone.1..sunk.3) | dynamic-update-slice | bytes 262148 | tf_op jit(solution)/shard_map/while/body/jit(dynamic_update_index_in_dim)/dynamic_update_slice | solution.py:50
  92.7 32.9 %while.58 = (s32[]{:T(128)}, f32[2,512]{1,0:T(2,128)}, f32[2,512]{1,0:T(2,128)}, f32[2,512,64]{1,0,2:T(2,128)}, s32[2048]{0:T(1024)S(1)}, /*index=5*/bf16[2,512,...) while((s32[]{:T(128)}, f32[2,512]{1,0:T(2,128)}, ...), condition=%wide.region_11.12_spmd, body=%wide.region_8.11_spmd.sunk | while | flops 279970816 | bytes 14188669 | solution.py:50
  92.7 3.8 %fusion.118 = (f32[512]{0:T(512)S(1)}, f32[512,2048]{1,0:T(8,128)}) fusion(pred[2048]{0:T(1024)(128)(4,1)S(1)} %broadcast_compare_fusion.10, bf16[2048,64]{1,0:T(8,128)(2,1)} %get-tuple-element.675, bf16[2,512,64]{2,1,0:T(8,128)(2,1)} %get-tuple-element.674, s32[]{:T(128)S(6)} %copy.109), kind=kOutput, calls=%fused_computation.32.clone.1 | convolution fusion | flops 137362944 | bytes 4853764 | tf_op jit(solution)/shard_map/while/body/eval_jaxpr/dot_general | solution.py:10
  109.1 3.8 %fusion.118 = (f32[512]{0:T(512)S(1)}, f32[512,2048]{1,0:T(8,128)}) fusion(pred[2048]{0:T(1024)(128)(4,1)S(1)} %broadcast_compare_fusion.10, bf16[2048,64]{1,0:T(8,128)(2,1)} %get-tuple-element.675, bf16[2,512,64]{2,1,0:T(8,128)(2,1)} %get-tuple-element.674, s32[]{:T(128)S(6)} %copy.109), kind=kOutput, calls=%fused_computation.32.clone.1 | convolution fusion | flops 137362944 | bytes 4853764 | tf_op jit(solution)/shard_map/while/body/eval_jaxpr/dot_general | solution.py:10
  127.5 32.4 %while.57 = (s32[]{:T(128)}, f32[2,512]{1,0:T(2,128)}, f32[2,512]{1,0:T(2,128)}, f32[2,512,64]{1,0,2:T(2,128)}, s32[2048]{0:T(1024)S(1)}, /*index=5*/bf16[2,512,...) while((s32[]{:T(128)}, f32[2,512]{1,0:T(2,128)}, ...), condition=%wide.region_7.8_spmd, body=%wide.region_4.7_spmd.sunk | while | flops 279970816 | bytes 13926525 | solution.py:50
  127.5 3.6 %fusion.112 = (f32[512]{0:T(512)S(1)}, f32[512,2048]{1,0:T(8,128)}) fusion(pred[2048]{0:T(1024)(128)(4,1)S(1)} %broadcast_compare_fusion.9, bf16[2048,64]{1,0:T(8,128)(2,1)S(1)} %get-tuple-element.705, bf16[2,512,64]{2,1,0:T(8,128)(2,1)} %get-tuple-element.704, s32[]{:T(128)S(6)} %copy.121), kind=kOutput, calls=%fused_computation.17.clone.1 | convolution fusion | flops 137362944 | bytes 4591620 | tf_op jit(solution)/shard_map/while/body/eval_jaxpr/dot_general | solution.py:10
  140.3 3.4 %dynamic_update_slice.55 = f32[2,512,64]{1,0,2:T(2,128)} dynamic-update-slice(f32[2,512,64]{1,0,2:T(2,128)} %get-tuple-element.692, f32[1,512,64]{1,0,2:T(1,128)S(1)} %copy.78, s32[]{:T(128)S(6)} %copy.121, s32[]{:T(128)} %constant.78.clone.1..sunk.1, s32[]{:T(128)} %constant.78.clone.1..sunk.1) | dynamic-update-slice | bytes 262148 | tf_op jit(solution)/shard_map/while/body/jit(dynamic_update_index_in_dim)/dynamic_update_slice | solution.py:50
  143.8 3.6 %fusion.112 = (f32[512]{0:T(512)S(1)}, f32[512,2048]{1,0:T(8,128)}) fusion(pred[2048]{0:T(1024)(128)(4,1)S(1)} %broadcast_compare_fusion.9, bf16[2048,64]{1,0:T(8,128)(2,1)S(1)} %get-tuple-element.705, bf16[2,512,64]{2,1,0:T(8,128)(2,1)} %get-tuple-element.704, s32[]{:T(128)S(6)} %copy.121), kind=kOutput, calls=%fused_computation.17.clone.1 | convolution fusion | flops 137362944 | bytes 4591620 | tf_op jit(solution)/shard_map/while/body/eval_jaxpr/dot_general | solution.py:10
  156.6 3.4 %dynamic_update_slice.55 = f32[2,512,64]{1,0,2:T(2,128)} dynamic-update-slice(f32[2,512,64]{1,0,2:T(2,128)} %get-tuple-element.692, f32[1,512,64]{1,0,2:T(1,128)S(1)} %copy.78, s32[]{:T(128)S(6)} %copy.121, s32[]{:T(128)} %constant.78.clone.1..sunk.1, s32[]{:T(128)} %constant.78.clone.1..sunk.1) | dynamic-update-slice | bytes 262148 | tf_op jit(solution)/shard_map/while/body/jit(dynamic_update_index_in_dim)/dynamic_update_slice | solution.py:50
  160.1 21.4 %while.56 = (s32[]{:T(128)}, f32[2,512]{1,0:T(2,128)S(1)}, f32[2,512]{1,0:T(2,128)S(1)}, f32[2,512,64]{1,0,2:T(2,128)S(1)}, s32[2048]{0:T(1024)S(1)}, /*index=5*...) while((s32[]{:T(128)}, f32[2,512]{1,0:T(2,128)S(1)}, ...), condition=%wide.region_3.4_spmd, body=%wide.region_0.3_spmd.sunk | while | flops 279970816 | bytes 14188669 | solution.py:50
  184.3 28.3 %pmax.7 = f32[1024,4]{0,1:T(4,128)S(1)} all-reduce(f32[1024,4]{0,1:T(4,128)S(1)} %pad_maximum_fusion.1), channel_id=1, replica_groups=mesh['hit'=8,'head'=4] {'hit'}, use_global_device_ids=true, to_apply=%region_16.17 | all-reduce | flops 4096 | bytes 32768 | tf_op jit(solution)/shard_map/pmax | solution.py:57
  218.1 24.0 %reduce-scatter.10.cloned.1.call-done = f32[128,4]{1,0:T(8,128)} async-done(((f32[1024,4]{1,0:T(8,128)}), f32[128,4]{1,0:T(8,128)}) %reduce-scatter.10.cloned.1.call-update) | async-done | bytes 2064
  242.9 31.9 %reduce-scatter.6.cloned.1.call-done = f32[128,256]{0,1:T(8,128)} async-done(((f32[1024,256]{0,1:T(8,128)}), f32[128,256]{0,1:T(8,128)}) %reduce-scatter.6.cloned.1.call-update) | async-done | bytes 131088 | tf_op jit(solution)/shard_map/reduce_scatter | solution.py:60
  276.8 24.4 %reduce-scatter.8.cloned.1.call-done = f32[128,256]{1,0:T(8,128)} async-done(((f32[128,1024]{1,0:T(8,128)}), f32[128,256]{1,0:T(8,128)}) %reduce-scatter.8.cloned.1.call-update) | async-done | bytes 131088 | tf_op jit(solution)/shard_map/reduce_scatter | solution.py:70
  (109 shorter events, 108.7 us)
Async XLA Ops:
  6.5 1.6 copy-start
  22.3 5.3 %copy-start.3 = (bf16[1024,256]{1,0:T(8,128)(2,1)S(1)}, bf16[1024,256]{1,0:T(8,128)(2,1)}, u32[]{:S(2)}) copy-start(bf16[1024,256]{1,0:T(8,128)(2,1)} %param.18) | copy-start | bytes 1572868
  22.3 31.0 %all-to-all-start = ((bf16[512,4,4,128]{0,3,2,1:T(8,128)(2,1)}), bf16[512,4,4,128]{0,3,2,1:T(8,128)(2,1)}, u32[]{:S(2)}, u32[]{:S(2)}) async-start(bf16[512,4,4,128]{0,3,2,1:T(8,128)(2,1)} %pad_maximum_fusion), calls=%async_computation | async-start | bytes 4194304 | tf_op jit(solution)/shard_map/all_to_all | solution.py:33
  27.6 214.4 %reduce-scatter.10.cloned.1.call-start = ((), (), s32[]{:S(2)}) async-start(), calls=%async_computation.6 | async-start | bytes 589824
  57.5 5.3 %copy-start.1 = (s32[2048]{0:T(1024)S(1)}, s32[2048]{0:T(1024)}, u32[]{:S(2)}) copy-start(s32[2048]{0:T(1024)} %param.17) | copy-start | bytes 24580
  181.5 94.3 %copy-start.2 = (bf16[256,1024]{1,0:T(8,128)(2,1)S(1)}, bf16[256,1024]{1,0:T(8,128)(2,1)}, u32[]{:S(2)}) copy-start(bf16[256,1024]{1,0:T(8,128)(2,1)} %param.21) | copy-start | bytes 1572868
  213.7 61.1 %reduce-scatter.6.cloned.1.call-start = ((), (), s32[]{:S(2)}) async-start(), calls=%async_computation.4 | async-start | bytes 1179648 | tf_op jit(solution)/shard_map/reduce_scatter | solution.py:60
  218.0 83.2 %reduce-scatter.8.cloned.1.call-start = ((), (), s32[]{:S(2)}) async-start(), calls=%async_computation.5 | async-start | bytes 655360 | tf_op jit(solution)/shard_map/reduce_scatter | solution.py:70
Sparse Core Ops, SparseCore 0:
  213.9 28.1 reduce-scatter.9
  244.4 30.3 reduce-scatter.5
  277.9 23.2 reduce-scatter.7
where the time goes:
time: 312 us; the launch traced here: 309 us
  waiting for transfers between devices  101 us (32%)
  matrix products  65.5 us (21%)
  local copies, waits for them, and re-layouts  64.2 us (21%)
  other arithmetic  31.4 us (10%)
  blocking collectives  28.3 us (9%)
  between operations  13.2 us (4%)
  starting transfers between devices  5.38 us (2%)
    dynamic_update_slice x32, local copies, waits for them, and re-layouts, local(): head_top, head_sums, head_part = lax.map(per_block, queries_head)  34.8 us
    reduce_scatter x1, waiting for transfers between devices, local(): lax.psum_scatter(partial_value * jnp.repeat(scale, HEAD_DIM, axis=1), 'hi...  31.9 us
    pmax x1, blocking collectives, local(): overall = lax.pmax(row_top, 'hit')  28.3 us
    dot_general x8, matrix products, attend(): jnp.dot(queries_head, keys_head.T, preferred_element_type=jnp.float32)  27.7 us
    dot_general x8, matrix products, attend(): jnp.dot(weights, values_head, preferred_element_type=jnp.float32)  26.8 us
    reduce_sum x8, other arithmetic, attend(): totals = jnp.sum(expo, axis=1)  24.9 us
    reduce_scatter x1, waiting for transfers between devices, local(): lax.psum_scatter(head_terms, 'head', scatter_dimension=1, tiled=True)  24.4 us
    unnamed x4, waiting for transfers between devices  24 us
  transfers between devices with their start and end apart: 4, of which 4 were waited for; matrix products, arithmetic and copies ran while one was open for 3% of the time, Pallas kernels for 0%

commit v1 on v0

v1 whole, which is shorter than its diff:
```python
import functools
import math

import jax
import jax.numpy as jnp
from jax import lax
from jax.experimental import pallas as pl
from jax.experimental.pallas import tpu as pltpu
from jax.sharding import PartitionSpec as P

HEAD_DIM = 64
F32 = jnp.float32
BF16 = jnp.bfloat16
NN = (((1,), (0,)), ((), ()))
NT = (((1,), (1,)), ((), ()))
SCALE = HEAD_DIM**-0.5 * math.log2(math.e)
AXES = ("hit", "head")
VMEM = pl.BlockSpec(memory_space=pltpu.VMEM)
SMEM = pl.BlockSpec(memory_space=pltpu.SMEM)
PARAMS = pltpu.CompilerParams(vmem_limit_bytes=40 << 20)


def mul(left, right, dims=NN):
    return lax.dot_general(left, right, dims, preferred_element_type=F32)


def struct(shape, dtype=BF16):
    return jax.ShapeDtypeStruct(shape, dtype)


def split(value, count):
    pieces = []
    for _ in range(count):
        piece = value.astype(BF16).astype(F32)
        pieces.append(piece)
        value = value - piece
    return pieces


def project_kernel(flip, where_ref, hits_ref, k_ref, v_ref, out_ref):
    width = out_ref.shape[1] // 2
    out_ref[:, :width] = mul(hits_ref[...], k_ref[...]).astype(BF16)
    out_ref[:, width:] = mul(hits_ref[...], v_ref[...]).astype(BF16)


def project(flip, where, hits, k_weight, v_weight, width):
    rows, depth = hits.shape
    weight = pl.BlockSpec((depth, width), lambda i, where: (0, where[0] ^ flip))
    return pl.pallas_call(
        functools.partial(project_kernel, flip),
        grid_spec=pltpu.PrefetchScalarGridSpec(
            num_scalar_prefetch=1,
            grid=(1,),
            in_specs=[pl.BlockSpec((rows, depth), lambda i, where: (0, 0)), weight, weight],
            out_specs=pl.BlockSpec((rows, 2 * width), lambda i, where: (0, 0)),
        ),
        out_shape=struct((rows, 2 * width)),
        compiler_params=PARAMS,
        name=f"project{flip}",
    )(where, hits, k_weight, v_weight)


def query_kernel(slots_ref, q_ref, out_ref):
    rows = slots_ref.shape[0]
    queries = mul(slots_ref[...], q_ref[...]).astype(BF16).astype(F32)
    lane = lax.broadcasted_iota(jnp.int32, (rows, 128), 1)
    low = lane < HEAD_DIM
    for pair in range(queries.shape[1] // 128):
        pieces = split(queries[:, pair * 128 : (pair + 1) * 128] * SCALE, 3)
        rolled = [pltpu.roll(piece, HEAD_DIM, 1) for piece in pieces]
        one = jnp.where(lane == HEAD_DIM, 1.0, 0.0)
        out_ref[2 * pair, :, :128] = jnp.where(low, pieces[0], rolled[1]).astype(BF16)
        out_ref[2 * pair, :, 128:] = jnp.where(low, pieces[2], one).astype(BF16)
        out_ref[2 * pair + 1, :, :128] = jnp.where(low, rolled[0], pieces[1]).astype(BF16)
        out_ref[2 * pair + 1, :, 128:] = jnp.where(low, rolled[2], one).astype(BF16)


def query(slots, q_weight):
    rows, depth = slots.shape
    width = q_weight.shape[1]
    heads = width // HEAD_DIM
    block = 256
    return pl.pallas_call(
        query_kernel,
        grid=(rows // block,),
        in_specs=[
            pl.BlockSpec((block, depth), lambda i: (i, 0)),
            pl.BlockSpec((depth, width), lambda i: (0, 0)),
        ],
        out_specs=pl.BlockSpec((heads, block, 256), lambda i: (0, i, 0)),
        out_shape=struct((heads, rows, 256)),
        compiler_params=PARAMS,
        name="query",
    )(slots, q_weight)


def attend_kernel(count, first, last, *refs):
    where_ref, q_ref = refs[:2]
    kv_refs = refs[2 : 2 + count]
    mask_refs = refs[2 + count : 2 + 2 * count]
    rest = list(refs[2 + 2 * count :])
    if not first:
        acc_in, stat_in = rest[:2]
        rest = rest[2:]
    if last:
        keep_ref, send_ref = rest[:2]
        rest = rest[2:]
    else:
        acc_out, stat_out = rest[:2]
        rest = rest[2:]
    ke_ref, ve_ref = rest[:2]
    heads, slots = q_ref.shape[:2]
    pairs = heads // 2
    hits = kv_refs[0].shape[0]
    lane = lax.broadcasted_iota(jnp.int32, (hits, 128), 1)
    low = lane < HEAD_DIM
    for at in range(count):
        rows = pl.ds(at * hits, hits)
        off = jnp.where(mask_refs[at][...] > 0, 0.0, -1e30)
        column = jnp.broadcast_to(off, (128, hits)).T
        tail = jnp.where(lane == HEAD_DIM, column, 0.0)
        for pair in range(pairs):
            keys = kv_refs[at][:, pair * 128 : (pair + 1) * 128].astype(F32)
            rolled = pltpu.roll(keys, HEAD_DIM, 1)
            ke_ref[2 * pair, rows, :128] = jnp.where(low, keys, rolled).astype(BF16)
            ke_ref[2 * pair, rows, 128:] = jnp.where(low, keys, tail).astype(BF16)
            ke_ref[2 * pair + 1, rows, :128] = jnp.where(low, rolled, keys).astype(BF16)
            ke_ref[2 * pair + 1, rows, 128:] = jnp.where(low, rolled, tail).astype(BF16)
            start = (pairs + pair) * 128
            ve_ref[pair, rows, :128] = kv_refs[at][:, start : start + 128]
            ve_ref[pair, rows, 128:] = jnp.ones((hits, 128), BF16)
    block = 256
    half = block // 2
    slot_lane = lax.broadcasted_iota(jnp.int32, (block, 128), 1)
    slot_low = slot_lane < HEAD_DIM
    for step in range(slots // block):
        rows = pl.ds(step * block, block)
        stat = jnp.zeros((block, 128), F32) if first else stat_in[rows, :]
        new_stat = jnp.zeros((block, 128), F32)
        for pair in range(pairs):
            outs = []
            for odd in range(2):
                head = 2 * pair + odd
                scores = mul(q_ref[head, rows, :], ke_ref[head], NT)
                top = jnp.max(scores, axis=1, keepdims=True)
                if not first:
                    old_top = stat[:, head : head + 1]
                    top = jnp.maximum(top, old_top)
                weights = jnp.exp2(scores - top).astype(BF16)
                both = mul(weights, ve_ref[pair])
                total = both[:, 128:]
                value = both[:, :128]
                if not first:
                    keep = jnp.exp2(old_top - top)
                    total = total + stat[:, 8 + head : 9 + head] * keep
                    value = value + acc_in[pair, rows, :] * keep
                if last:
                    value = value / total
                new_stat = jnp.where(slot_lane == head, top, new_stat)
                new_stat = jnp.where(slot_lane == 8 + head, total, new_stat)
                outs.append(value)
            value = jnp.where(slot_low, outs[0], outs[1])
            if last:
                rest[2][:, pair * 128 : (pair + 1) * 128] = value.astype(BF16)
            else:
                acc_out[pair, rows, :] = value
        if last:
            core = where_ref[1]
            rest[3][...] = new_stat
            for target, place in ((keep_ref, core), (send_ref, 1 - core)):
                part = pl.ds(pl.multiple_of(place * half, half), half)
                target[step, :half, :] = rest[2][part, :]
                flat = rest[3][part, :].T
                target[step, half:, :] = pack(flat[:heads], flat[8 : 8 + heads])
        else:
            stat_out[rows, :] = new_stat


def pack(top, total):
    heads, slots = top.shape
    gap = jnp.zeros((heads, slots), F32)
    left = jnp.concatenate(split(top, 3) + [gap], axis=0)
    right = jnp.concatenate(split(total, 2) + [gap, gap], axis=0)
    return jnp.concatenate([left, right], axis=1).astype(BF16)


def unpack(rows, heads):
    rows = rows.astype(F32)
    slots = rows.shape[1] // 2
    left, right = rows[:, :slots], rows[:, slots:]
    top = left[:heads] + left[heads : 2 * heads] + left[2 * heads : 3 * heads]
    total = right[:heads] + right[heads : 2 * heads]
    return top, total


def attend(where, queries, sources, masks, carry, last):
    heads, slots, _ = queries.shape
    pairs = heads // 2
    count = len(sources)
    hits = sources[0].shape[0]
    block = 256
    message = (slots // block, block // 2 + 4 * heads, heads * HEAD_DIM)
    scratch = [pltpu.VMEM((heads, count * hits, 256), BF16), pltpu.VMEM((pairs, count * hits, 256), BF16)]
    if last:
        out_shape = (struct(message), struct(message))
        scratch += [pltpu.VMEM((block, heads * HEAD_DIM), BF16), pltpu.VMEM((block, 128), F32)]
    else:
        out_shape = (struct((pairs, slots, 128), F32), struct((slots, 128), F32))
    args = [where, queries, *sources, *masks, *carry]
    scores = heads * slots * count * hits
    return pl.pallas_call(
        functools.partial(attend_kernel, count, not carry, last),
        in_specs=[SMEM] + [VMEM] * (len(args) - 1),
        out_specs=(VMEM, VMEM),
        out_shape=out_shape,
        scratch_shapes=scratch,
        compiler_params=PARAMS,
        cost_estimate=pl.CostEstimate(
            flops=2 * scores * 512, bytes_accessed=4 << 20, transcendentals=scores
        ),
        name=f"attend{count}",
    )(*args)


def join(messages, heads):
    slots = messages[0].shape[0] - 4 * heads
    stats = [unpack(message[slots:, :], heads) for message in messages]
    top = functools.reduce(jnp.maximum, [one for one, _ in stats])
    shares = [total * jnp.exp2(one - top) for one, total in stats]
    total = functools.reduce(jnp.add, shares)
    rows = [share / total for share in shares]
    rows.append(jnp.zeros((128 - len(messages) * heads, slots), F32))
    columns = jnp.concatenate(rows, axis=0).T
    low = lax.broadcasted_iota(jnp.int32, (slots, 128), 1) < HEAD_DIM
    outs = []
    for pair in range(heads // 2):
        value = jnp.zeros((slots, 128), F32)
        for at, message in enumerate(messages):
            head = at * heads + 2 * pair
            factor = jnp.where(low, columns[:, head : head + 1], columns[:, head + 1 : head + 2])
            value = value + message[:slots, pair * 128 : (pair + 1) * 128].astype(F32) * factor
        outs.append(value)
    return jnp.concatenate(outs, axis=1).astype(BF16), top, total


def core_kernel(heads, where_ref, own_ref, other_ref, *outs):
    slots = own_ref.shape[1] - 4 * heads
    for flip, out in enumerate(outs):
        place = where_ref[2] ^ flip
        value, top, total = join([own_ref.at[place], other_ref.at[place]], heads)
        out[:slots, :] = value
        out[slots:, :] = pack(top, total)


def core_join(where, own, other, heads):
    chips, rows, width = own.shape
    return pl.pallas_call(
        functools.partial(core_kernel, heads),
        in_specs=[SMEM, VMEM, VMEM],
        out_specs=[VMEM] * chips,
        out_shape=[struct((rows, width))] * chips,
        compiler_params=PARAMS,
        name="core_join",
    )(where, own, other)


def out_kernel(heads, where_ref, o_ref, m0, m1, m2, m3, own_ref, *refs):
    outs, full = refs[:-1], refs[-1]
    mixed, _, _ = join([m0, m1, m2, m3], heads)
    full[...] = mul(mixed, o_ref[...])
    width = own_ref.shape[1]
    for flip, out in enumerate((own_ref, *outs)):
        start = pl.multiple_of((where_ref[0] ^ flip) * width, width)
        out[...] = full[:, pl.ds(start, width)].astype(out.dtype)


def out_project(where, o_weight, messages, heads):
    rows = messages[0].shape[0] - 4 * heads
    width = o_weight.shape[1] // 4
    return pl.pallas_call(
        functools.partial(out_kernel, heads),
        in_specs=[SMEM] + [VMEM] * 5,
        out_specs=[VMEM] * 4,
        out_shape=[struct((rows, width), F32)] + [struct((rows, width))] * 3,
        scratch_shapes=[pltpu.VMEM((rows, o_weight.shape[1]), F32)],
        compiler_params=PARAMS,
        name="out_project",
    )(where, o_weight, *messages)


def move(value, hit_flip, head_flip):
    hits, heads = lax.axis_size("hit"), lax.axis_size("head")
    pairs = [
        (hit * heads + head, (hit ^ hit_flip) * heads + (head ^ head_flip))
        for hit in range(hits)
        for head in range(heads)
    ]
    return lax.ppermute(value, AXES, pairs)


def local_plane(slots, hits, hit_mask, q_weight, k_weight, v_weight, o_weight):
    width = q_weight.shape[1]
    heads = width // HEAD_DIM
    hit, head = lax.axis_index("hit"), lax.axis_index("head")
    where = jnp.stack([head, hit % 2, hit // 2, hit]).astype(jnp.int32)
    masks = hit_mask.reshape(4, 1, hits.shape[0])

    def mask_of(flip):
        return lax.dynamic_index_in_dim(masks, head ^ flip, 0, keepdims=False)

    ours = {flip: project(flip, where, hits, k_weight, v_weight, width) for flip in (3, 1, 2, 0)}
    theirs = {flip: move(ours[flip], 0, flip) for flip in (3, 1, 2)}
    queries = query(slots, q_weight)
    carry = attend(where, queries, [ours[0]], [mask_of(0)], (), False)
    carry = attend(where, queries, [theirs[3]], [mask_of(3)], carry, False)
    kept, sent = attend(
        where, queries, [theirs[1], theirs[2]], [mask_of(1), mask_of(2)], carry, True
    )
    other = move(sent, 1, 0)
    parts = core_join(where, kept, other, heads)
    messages = [parts[0]] + [move(parts[flip], 2 * flip, 0) for flip in (1, 2, 3)]
    shares = out_project(where, o_weight, messages, heads)
    total = shares[0]
    for flip in (1, 2, 3):
        total = total + move(shares[flip], 0, flip).astype(F32)
    return total.astype(BF16)


def attend_group(queries_head, keys_head, values_head, valid):
    scores = mul(queries_head, keys_head, NT) * HEAD_DIM ** (-0.5)
    scores = jnp.where(valid[None, :] > 0, scores, F32(-1e30))
    row_top = jnp.max(scores, axis=1)
    expo = jnp.exp(scores - row_top[:, None])
    totals = jnp.sum(expo, axis=1)
    return row_top, totals, mul(expo.astype(BF16), values_head)


def local_any(slots, hits, hit_mask, q_weight, k_weight, v_weight, o_weight):
    heads_here = q_weight.shape[1] // HEAD_DIM
    slot_count = slots.shape[0]
    queries = mul(slots, q_weight).astype(BF16)
    local_hits = hits.shape[0]
    head_devs = lax.axis_size("head")
    keys = mul(hits, k_weight).astype(BF16)
    values = mul(hits, v_weight).astype(BF16)
    keys = keys.reshape(local_hits, head_devs, heads_here, HEAD_DIM)
    values = values.reshape(local_hits, head_devs, heads_here, HEAD_DIM)
    both = jnp.concatenate([keys, values], axis=3)
    moved = lax.all_to_all(both, "head", split_axis=1, concat_axis=0, tiled=True)
    key_vals = moved.reshape(moved.shape[0], heads_here, 2 * HEAD_DIM)
    block = min(512, slot_count)
    row_tops, sums_list, partials = [], [], []
    for at in range(heads_here):
        queries_head = queries[:, at * HEAD_DIM : (at + 1) * HEAD_DIM]
        queries_head = queries_head.reshape(slot_count // block, block, HEAD_DIM)
        keys_head = key_vals[:, at, :HEAD_DIM]
        values_head = key_vals[:, at, HEAD_DIM:]
        head_top, head_sums, head_part = lax.map(
            lambda part: attend_group(part, keys_head, values_head, hit_mask), queries_head
        )
        row_tops.append(head_top.reshape(slot_count))
        sums_list.append(head_sums.reshape(slot_count))
        partials.append(head_part.reshape(slot_count, HEAD_DIM))
    row_top = jnp.stack(row_tops, axis=1)
    totals = jnp.stack(sums_list, axis=1)
    partial_value = jnp.concatenate(partials, axis=1)
    scale = jnp.exp(row_top - lax.pmax(row_top, "hit"))
    numer = lax.psum_scatter(
        partial_value * jnp.repeat(scale, HEAD_DIM, axis=1), "hit", scatter_dimension=0, tiled=True
    )
    denom = lax.psum_scatter(totals * scale, "hit", scatter_dimension=0, tiled=True)
    mixed = (numer / jnp.repeat(denom, HEAD_DIM, axis=1)).astype(BF16)
    head_terms = mul(mixed, o_weight)
    return lax.psum_scatter(head_terms, "head", scatter_dimension=1, tiled=True).astype(BF16)


def solution(mesh):
    placed = (P(), P(("hit", "head"), None), P("hit"), P(None, "head"), P(), P(), P("head", None))
    plane = mesh.shape["hit"] == 8 and mesh.shape["head"] == 4
    return jax.shard_map(
        local_plane if plane else local_any,
        mesh=mesh,
        in_specs=placed,
        out_specs=P("hit", "head"),
        check_vma=False,
    )
```

time: 312 us -> 67.3 us (0.22)
  waiting for transfers between devices: 101 us -> 16.4 us
  matrix products: 65.5 us -> 0 us
  local copies, waits for them, and re-layouts: 64.2 us -> 5.23 us
  Pallas kernels: 0 us -> 31.9 us
  other arithmetic: 31.4 us -> 0.74 us
  blocking collectives: 28.3 us -> 0 us
  between operations: 13.2 us -> 0.12 us
  starting transfers between devices: 5.38 us -> 12.6 us
    dot_general x20 -> x0, matrix products: 65.5 us -> none  [the longest x8 27.7 us: attend(): jnp.dot(queries_head, keys_head.T, preferred_element_type=jnp.float32)]
    reduce_scatter x2 -> x0, waiting for transfers between devices: 56.3 us -> none  [the longest x1 31.9 us: local(): lax.psum_scatter(partial_value * jnp.repeat(scale, HEAD_DIM, axis=1), 'hi...]
    dynamic_update_slice x32 -> x0, local copies, waits for them, and re-layouts: 34.8 us -> none  [local(): head_top, head_sums, head_part = lax.map(per_block, queries_head)]
    pallas_call x0 -> x10, Pallas kernels: none -> 31.9 us  [the longest x3 20.5 us: attend(): pl.pallas_call(functools.partial(attend_kernel, count, not carry, last),...]
    pmax x1 -> x0, blocking collectives: 28.3 us -> none  [local(): overall = lax.pmax(row_top, 'hit')]
    reduce_sum x8 -> x0, other arithmetic: 24.9 us -> none  [attend(): totals = jnp.sum(expo, axis=1)]
    unnamed x4 -> x0, waiting for transfers between devices: 24 us -> none
    all_to_all x1 -> x0, waiting for transfers between devices: 20.7 us -> none  [local(): lax.all_to_all(both, 'head', split_axis=1, concat_axis=0, tiled=True)]
  transfers between devices with their start and end apart: 4 -> 10, of which waited for: 4 -> 7; matrix products, arithmetic and copies ran while one was open for 3% -> 0% of each run, Pallas kernels for 0% -> 27%
where the time goes in v1:
time: 67.3 us; the launch traced here: 67.1 us
  Pallas kernels  31.9 us (47%)
  waiting for transfers between devices  16.4 us (24%)
  starting transfers between devices  12.6 us (19%)
  local copies, waits for them, and re-layouts  5.23 us (8%)
  other arithmetic  0.74 us (1%)
    pallas_call x3, Pallas kernels, attend(): pl.pallas_call(functools.partial(attend_kernel, count, not carry, last),...  20.5 us
    ppermute x10, waiting for transfers between devices, move(): return lax.ppermute(value, AXES, pairs)  16.4 us
    ppermute x10, starting transfers between devices, move(): return lax.ppermute(value, AXES, pairs)  12.6 us
    pallas_call x4, Pallas kernels, project(): pl.pallas_call(functools.partial(project_kernel, flip), grid_spec=pltpu.P...  6.65 us
    unnamed x18, local copies, waits for them, and re-layouts  5.22 us
    pallas_call x1, Pallas kernels, query(): pl.pallas_call(query_kernel, grid=(rows // block,), in_specs=[pl.BlockSpe...  2.13 us
    pallas_call x1, Pallas kernels, core_join(): pl.pallas_call(functools.partial(core_kernel, heads), in_specs=[SMEM, VME...  1.41 us
  transfers between devices with their start and end apart: 10, of which 7 were waited for; matrix products, arithmetic and copies ran while one was open for 0% of the time, Pallas kernels for 27%

profile of v1, /device:TPU:0, one launch (start us, length us, event | category | flops | bytes accessed | tf_op | source)
XLA Modules:
  0.0 67.1 jit_solution(9130570479969484494)
XLA Ops:
  0.1 1.6 %copy-done = bf16[1024,1024]{1,0:T(8,128)(2,1)S(1)} copy-done((bf16[1024,1024]{1,0:T(8,128)(2,1)S(1)}, bf16[1024,1024]{1,0:T(8,128)(2,1)}, u32[]{:S(2)}) %copy-start) | copy-done | bytes 2097176
  1.7 1.6 %copy-done.1 = bf16[1024,1024]{1,0:T(8,128)(2,1)S(1)} copy-done((bf16[1024,1024]{1,0:T(8,128)(2,1)S(1)}, bf16[1024,1024]{1,0:T(8,128)(2,1)}, u32[]{:S(2)}) %copy-start.1) | copy-done | bytes 2097176
  3.3 1.2 %copy-done.2 = bf16[512,1024]{1,0:T(8,128)(2,1)S(1)} copy-done((bf16[512,1024]{1,0:T(8,128)(2,1)S(1)}, bf16[512,1024]{1,0:T(8,128)(2,1)}, u32[]{:S(2)}) %copy-start.2) | copy-done | bytes 1048600
  4.5 2.1 %project3.1 = bf16[512,512]{1,0:T(8,128)(2,1)} custom-call(s32[4]{0:T(128)S(1)} %pad_add_fusion.where_ref.refs_0_, bf16[512,1024]{1,0:T(8,128)(2,1)S(1)} %copy-done.2, bf16[1024,1024]{1,0:T(8,128)(2,1)S(1)} %copy-done, bf16[1024,1024]{1,0:T(8,128)(2,1)S(1)} %copy-done.1), custom_call_target="tpu_custom_call" | custom-call | tf_op jit(solution)/shard_map/project3/pallas_call | solution.py:49
  6.5 3.9 %collective-permute-start.2 = (bf16[512,512]{1,0:T(8,128)(2,1)}, bf16[512,512]{1,0:T(8,128)(2,1)}, u32[]{:S(2)}, u32[]{:S(2)}) collective-permute-start(bf16[512,512]{1,0:T(8,128)(2,1)} %project3.1), channel_id=1, source_target_pairs={{0,3},{1,2},{2,1},{3,0},{4,7},{5,6},{6,5},{7,4},{8,11},{9,10},{10,... | collective-permute-start | bytes 1572872 | tf_op jit(solution)/shard_map/ppermute | solution.py:298
  10.4 1.3 %project1.1 = bf16[512,512]{1,0:T(8,128)(2,1)S(1)} custom-call(s32[4]{0:T(128)S(1)} %pad_add_fusion.where_ref.refs_0_, bf16[512,1024]{1,0:T(8,128)(2,1)S(1)} %copy-done.2, bf16[1024,1024]{1,0:T(8,128)(2,1)S(1)} %copy-done, bf16[1024,1024]{1,0:T(8,128)(2,1)S(1)} %copy-done.1), custom_call_target="tpu_custom_call" | custom-call | tf_op jit(solution)/shard_map/project1/pallas_call | solution.py:49
  12.3 2.1 %project2.1 = bf16[512,512]{1,0:T(8,128)(2,1)} custom-call(s32[4]{0:T(128)S(1)} %pad_add_fusion.where_ref.refs_0_, bf16[512,1024]{1,0:T(8,128)(2,1)S(1)} %copy-done.2, bf16[1024,1024]{1,0:T(8,128)(2,1)S(1)} %copy-done, bf16[1024,1024]{1,0:T(8,128)(2,1)S(1)} %copy-done.1), custom_call_target="tpu_custom_call" | custom-call | tf_op jit(solution)/shard_map/project2/pallas_call | solution.py:49
  14.4 1.3 %project0.1.refs_2_ = bf16[512,512]{1,0:T(8,128)(2,1)S(1)} custom-call(s32[4]{0:T(128)S(1)} %pad_add_fusion.where_ref.refs_0_, bf16[512,1024]{1,0:T(8,128)(2,1)S(1)} %copy-done.2, bf16[1024,1024]{1,0:T(8,128)(2,1)S(1)} %copy-done, bf16[1024,1024]{1,0:T(8,128)(2,1)S(1)} %copy-done.1), custom_call_target="tpu_custom_call" | custom-call | tf_op jit(solution)/shard_map/project0/pallas_call | solution.py:49
  16.5 2.1 %query.1.refs_1_ = bf16[4,1024,256]{2,1,0:T(8,128)(2,1)S(1)} custom-call(bf16[1024,1024]{1,0:T(8,128)(2,1)S(1)} %copy-done.3, bf16[1024,256]{1,0:T(8,128)(2,1)S(1)} %copy-done.4), custom_call_target="tpu_custom_call" | custom-call | tf_op jit(solution)/shard_map/query/pallas_call | solution.py:83
  18.7 3.6 %attend1.2 = (f32[2,1024,128]{2,1,0:T(8,128)S(1)}, f32[1024,128]{1,0:T(8,128)S(1)}) custom-call(s32[4]{0:T(128)S(1)} %pad_add_fusion.where_ref.refs_0_, bf16[4,1024,256]{2,1,0:T(8,128)(2,1)S(1)} %query.1.refs_1_, bf16[512,512]{1,0:T(8,128)(2,1)S(1)} %copy-done.6, s32[1,512]{1,0:T(1,128)S(1)} %get-tuple-element.33.refs_3_), custom_call_target="tpu_custom_call" | custom-call | flops 2147483648 | bytes 4194304 | tf_op jit(solution)/shard_map/attend1/pallas_call | solution.py:211
  22.3 1.2 %collective-permute-done.2.refs_2_ = bf16[512,512]{1,0:T(8,128)(2,1)} collective-permute-done((bf16[512,512]{1,0:T(8,128)(2,1)}, bf16[512,512]{1,0:T(8,128)(2,1)}, u32[]{:S(2)}, u32[]{:S(2)}) %collective-permute-start.2) | collective-permute-done | bytes 524320 | tf_op jit(solution)/shard_map/ppermute | solution.py:298
  23.5 7.6 %attend1.3 = (f32[2,1024,128]{2,1,0:T(8,128)S(1)}, f32[1024,128]{1,0:T(8,128)S(1)}) custom-call(s32[4]{0:T(128)S(1)} %pad_add_fusion.where_ref.refs_0_, bf16[4,1024,256]{2,1,0:T(8,128)(2,1)S(1)} %query.1.refs_1_, bf16[512,512]{1,0:T(8,128)(2,1)} %collective-permute-done.2.refs_2_, s32[1,512]{1,0:T(1,128)S(1)} %get-tuple-element.34.refs_3_, ...), custom_call_target="tpu_custom_call" | custom-call | flops 2147483648 | bytes 4194304 | tf_op jit(solution)/shard_map/attend1/pallas_call | solution.py:211
  31.2 3.0 %collective-permute-done.refs_2_ = bf16[512,512]{1,0:T(8,128)(2,1)} collective-permute-done((bf16[512,512]{1,0:T(8,128)(2,1)S(1)}, bf16[512,512]{1,0:T(8,128)(2,1)}, u32[]{:S(2)}, u32[]{:S(2)}) %collective-permute-start) | collective-permute-done | bytes 524320 | tf_op jit(solution)/shard_map/ppermute | solution.py:298
  34.2 9.2 %attend2.1 = (bf16[4,144,256]{2,1,0:T(8,128)(2,1)S(1)}, bf16[4,144,256]{2,1,0:T(8,128)(2,1)S(1)}) custom-call(s32[4]{0:T(128)S(1)} %pad_add_fusion.where_ref.refs_0_, bf16[4,1024,256]{2,1,0:T(8,128)(2,1)S(1)} %query.1.refs_1_, bf16[512,512]{1,0:T(8,128)(2,1)} %collective-permute-done.refs_2_, bf16[512,512]{1,0:T(8,128)(2,1)} %collective-permute-done.1.refs_3_, ...), custom_call_target="tpu_custom_call" | custom-call | flops 4294967296 | bytes 4194304 | tf_op jit(solution)/shard_map/attend2/pallas_call | solution.py:211
  43.5 1.6 %collective-permute-done.3.other_ref = bf16[4,144,256]{2,1,0:T(8,128)(2,1)S(1)} collective-permute-done((bf16[4,144,256]{2,1,0:T(8,128)(2,1)S(1)}, bf16[4,144,256]{2,1,0:T(8,128)(2,1)S(1)}, u32[]{:S(2)}, u32[]{:S(2)}) %collective-permute-start.3) | collective-permute-done | bytes 294944 | tf_op jit(solution)/shard_map/ppermute | solution.py:298
  45.1 1.4 %core_join.1 = (bf16[144,256]{1,0:T(8,128)(2,1)S(1)}, bf16[144,256]{1,0:T(8,128)(2,1)S(1)}, bf16[144,256]{1,0:T(8,128)(2,1)S(1)}, bf16[144,256]{1,0:T(8,128)(2,1)S(1)}) custom-call(s32[4]{0:T(128)S(1)} %pad_add_fusion.where_ref.refs_0_, bf16[4,144,256]{2,1,0:T(8,128)(2,1)S(1)} %get-tuple-element.23.own_ref, ...), custom_call_target="tpu_custom_call" | custom-call | tf_op jit(solution)/shard_map/core_join/pallas_call | solution.py:257
  46.5 1.6 %collective-permute-start.4 = (bf16[144,256]{1,0:T(8,128)(2,1)S(1)}, bf16[144,256]{1,0:T(8,128)(2,1)S(1)}, u32[]{:S(2)}, u32[]{:S(2)}) collective-permute-start(bf16[144,256]{1,0:T(8,128)(2,1)S(1)} %get-tuple-element.26), channel_id=1, source_target_pairs={{0,8},{1,9},{2,10},{3,11},{4,12},{5,13},{6,14},{7,15},{8,0},{9,1},... | collective-permute-start | bytes 221192 | tf_op jit(solution)/shard_map/ppermute | solution.py:298
  48.1 2.6 %collective-permute-start.5 = (bf16[144,256]{1,0:T(8,128)(2,1)S(1)}, bf16[144,256]{1,0:T(8,128)(2,1)S(1)}, u32[]{:S(2)}, u32[]{:S(2)}) collective-permute-start(bf16[144,256]{1,0:T(8,128)(2,1)S(1)} %get-tuple-element.27), channel_id=1, source_target_pairs={{0,16},{1,17},{2,18},{3,19},{4,20},{5,21},{6,22},{7,23},{8,24},{9,... | collective-permute-start | bytes 221192 | tf_op jit(solution)/shard_map/ppermute | solution.py:298
  50.9 6.0 %collective-permute-done.5.m2 = bf16[144,256]{1,0:T(8,128)(2,1)S(1)} collective-permute-done((bf16[144,256]{1,0:T(8,128)(2,1)S(1)}, bf16[144,256]{1,0:T(8,128)(2,1)S(1)}, u32[]{:S(2)}, u32[]{:S(2)}) %collective-permute-start.5) | collective-permute-done | bytes 73760 | tf_op jit(solution)/shard_map/ppermute | solution.py:298
  57.0 1.3 %out_project.1 = (f32[128,256]{1,0:T(8,128)S(1)}, bf16[128,256]{1,0:T(8,128)(2,1)S(1)}, bf16[128,256]{1,0:T(8,128)(2,1)S(1)}, bf16[128,256]{1,0:T(8,128)(2,1)S(1)}) custom-call(s32[4]{0:T(128)S(1)} %pad_add_fusion.where_ref.refs_0_, bf16[256,1024]{1,0:T(8,128)(2,1)S(1)} %copy-done.7, bf16[144,256]{1,0:T(8,128)(2,1)S(1)} %get-tuple-element.25.m0, ...), custom_call_target="tpu_custom_call" | custom-call | tf_op jit(solution)/shard_map/out_project/pallas_call | solution.py:280
  58.3 1.5 %collective-permute-start.7 = (bf16[128,256]{1,0:T(8,128)(2,1)S(1)}, bf16[128,256]{1,0:T(8,128)(2,1)S(1)}, u32[]{:S(2)}, u32[]{:S(2)}) collective-permute-start(bf16[128,256]{1,0:T(8,128)(2,1)S(1)} %get-tuple-element.30), channel_id=1, source_target_pairs={{0,1},{1,0},{2,3},{3,2},{4,5},{5,4},{6,7},{7,6},{8,9},{9,8},{10,11... | collective-permute-start | bytes 196616 | tf_op jit(solution)/shard_map/ppermute | solution.py:298
  59.8 1.4 %collective-permute-start.8 = (bf16[128,256]{1,0:T(8,128)(2,1)S(1)}, bf16[128,256]{1,0:T(8,128)(2,1)S(1)}, u32[]{:S(2)}, u32[]{:S(2)}) collective-permute-start(bf16[128,256]{1,0:T(8,128)(2,1)S(1)} %get-tuple-element.31), channel_id=1, source_target_pairs={{0,2},{1,3},{2,0},{3,1},{4,6},{5,7},{6,4},{7,5},{8,10},{9,11},{10,... | collective-permute-start | bytes 196616 | tf_op jit(solution)/shard_map/ppermute | solution.py:298
  61.8 1.2 %collective-permute-done.7 = bf16[128,256]{1,0:T(8,128)(2,1)S(1)} collective-permute-done((bf16[128,256]{1,0:T(8,128)(2,1)S(1)}, bf16[128,256]{1,0:T(8,128)(2,1)S(1)}, u32[]{:S(2)}, u32[]{:S(2)}) %collective-permute-start.7) | collective-permute-done | bytes 65568 | tf_op jit(solution)/shard_map/ppermute | solution.py:298
  64.2 2.2 %collective-permute-done.9 = bf16[128,256]{1,0:T(8,128)(2,1)S(1)} collective-permute-done((bf16[128,256]{1,0:T(8,128)(2,1)S(1)}, bf16[128,256]{1,0:T(8,128)(2,1)S(1)}, u32[]{:S(2)}, u32[]{:S(2)}) %collective-permute-start.9) | collective-permute-done | bytes 65568 | tf_op jit(solution)/shard_map/ppermute | solution.py:298
  (27 shorter events, 4.3 us)
Async XLA Ops:
  0.1 1.6 %copy-start = (bf16[1024,1024]{1,0:T(8,128)(2,1)S(1)}, bf16[1024,1024]{1,0:T(8,128)(2,1)}, u32[]{:S(2)}) copy-start(bf16[1024,1024]{1,0:T(8,128)(2,1)} %k_ref.7) | copy-start | bytes 6291460
  1.7 1.6 %copy-start.1 = (bf16[1024,1024]{1,0:T(8,128)(2,1)S(1)}, bf16[1024,1024]{1,0:T(8,128)(2,1)}, u32[]{:S(2)}) copy-start(bf16[1024,1024]{1,0:T(8,128)(2,1)} %v_ref.7) | copy-start | bytes 6291460
  3.3 1.2 %copy-start.2 = (bf16[512,1024]{1,0:T(8,128)(2,1)S(1)}, bf16[512,1024]{1,0:T(8,128)(2,1)}, u32[]{:S(2)}) copy-start(bf16[512,1024]{1,0:T(8,128)(2,1)} %hits_ref.7) | copy-start | bytes 3145732
  6.5 17.0 %collective-permute-start.2 = (bf16[512,512]{1,0:T(8,128)(2,1)}, bf16[512,512]{1,0:T(8,128)(2,1)}, u32[]{:S(2)}, u32[]{:S(2)}) collective-permute-start(bf16[512,512]{1,0:T(8,128)(2,1)} %project3.1), channel_id=1, source_target_pairs={{0,3},{1,2},{2,1},{3,0},{4,7},{5,6},{6,5},{7,4},{8,11},{9,10},{10,... | collective-permute-start | bytes 1572872 | tf_op jit(solution)/shard_map/ppermute | solution.py:298
  11.7 22.5 %collective-permute-start = (bf16[512,512]{1,0:T(8,128)(2,1)S(1)}, bf16[512,512]{1,0:T(8,128)(2,1)}, u32[]{:S(2)}, u32[]{:S(2)}) collective-permute-start(bf16[512,512]{1,0:T(8,128)(2,1)S(1)} %project1.1), channel_id=1, source_target_pairs={{0,1},{1,0},{2,3},{3,2},{4,5},{5,4},{6,7},{7,6},{8,9},{9,8},{10,11... | collective-permute-start | bytes 1572872 | tf_op jit(solution)/shard_map/ppermute | solution.py:298
  14.4 2.1 %copy-start.3 = (bf16[1024,1024]{1,0:T(8,128)(2,1)S(1)}, bf16[1024,1024]{1,0:T(8,128)(2,1)}, u32[]{:S(2)}) copy-start(bf16[1024,1024]{1,0:T(8,128)(2,1)} %slots_ref.1) | copy-start | bytes 6291460
  14.4 2.1 %copy-start.4 = (bf16[1024,256]{1,0:T(8,128)(2,1)S(1)}, bf16[1024,256]{1,0:T(8,128)(2,1)}, u32[]{:S(2)}) copy-start(bf16[1024,256]{1,0:T(8,128)(2,1)} %q_ref.1) | copy-start | bytes 1572868
  14.4 19.8 %collective-permute-start.1 = (bf16[512,512]{1,0:T(8,128)(2,1)}, bf16[512,512]{1,0:T(8,128)(2,1)}, u32[]{:S(2)}, u32[]{:S(2)}) collective-permute-start(bf16[512,512]{1,0:T(8,128)(2,1)} %project2.1), channel_id=1, source_target_pairs={{0,2},{1,3},{2,0},{3,1},{4,6},{5,7},{6,4},{7,5},{8,10},{9,11},{10,... | collective-permute-start | bytes 1572872 | tf_op jit(solution)/shard_map/ppermute | solution.py:298
  15.7 0.8 %copy-start.5 = (bf16[512,512]{1,0:T(8,128)(2,1)}, bf16[512,512]{1,0:T(8,128)(2,1)S(1)}, u32[]{:S(2)}) copy-start(bf16[512,512]{1,0:T(8,128)(2,1)S(1)} %project0.1.refs_2_) | copy-start | bytes 1572868
  16.5 2.1 %copy-start.8 = (s32[2048]{0:T(1024)S(1)}, s32[2048]{0:T(1024)}, u32[]{:S(2)}) copy-start(s32[2048]{0:T(1024)} %param.9) | copy-start | bytes 24580
  16.5 2.2 %copy-start.6 = (bf16[512,512]{1,0:T(8,128)(2,1)S(1)}, bf16[512,512]{1,0:T(8,128)(2,1)}, u32[]{:S(2)}) copy-start(bf16[512,512]{1,0:T(8,128)(2,1)} %copy-done.5) | copy-start | bytes 1572868
  34.2 22.8 %copy-start.7 = (bf16[256,1024]{1,0:T(8,128)(2,1)S(1)}, bf16[256,1024]{1,0:T(8,128)(2,1)}, u32[]{:S(2)}) copy-start(bf16[256,1024]{1,0:T(8,128)(2,1)} %o_ref.1) | copy-start | bytes 1572868
  43.4 1.6 %collective-permute-start.3 = (bf16[4,144,256]{2,1,0:T(8,128)(2,1)S(1)}, bf16[4,144,256]{2,1,0:T(8,128)(2,1)S(1)}, u32[]{:S(2)}, u32[]{:S(2)}) collective-permute-start(bf16[4,144,256]{2,1,0:T(8,128)(2,1)S(1)} %get-tuple-element.24), channel_id=1, source_target_pairs={{0,4},{1,5},{2,6},{3,7},{4,0},{5,1},{6,2},{7,3},{8,12},{9,13},{10,... | collective-permute-start | bytes 884744 | tf_op jit(solution)/shard_map/ppermute | solution.py:298
  46.5 4.5 %collective-permute-start.4 = (bf16[144,256]{1,0:T(8,128)(2,1)S(1)}, bf16[144,256]{1,0:T(8,128)(2,1)S(1)}, u32[]{:S(2)}, u32[]{:S(2)}) collective-permute-start(bf16[144,256]{1,0:T(8,128)(2,1)S(1)} %get-tuple-element.26), channel_id=1, source_target_pairs={{0,8},{1,9},{2,10},{3,11},{4,12},{5,13},{6,14},{7,15},{8,0},{9,1},... | collective-permute-start | bytes 221192 | tf_op jit(solution)/shard_map/ppermute | solution.py:298
  48.1 8.9 %collective-permute-start.5 = (bf16[144,256]{1,0:T(8,128)(2,1)S(1)}, bf16[144,256]{1,0:T(8,128)(2,1)S(1)}, u32[]{:S(2)}, u32[]{:S(2)}) collective-permute-start(bf16[144,256]{1,0:T(8,128)(2,1)S(1)} %get-tuple-element.27), channel_id=1, source_target_pairs={{0,16},{1,17},{2,18},{3,19},{4,20},{5,21},{6,22},{7,23},{8,24},{9,... | collective-permute-start | bytes 221192 | tf_op jit(solution)/shard_map/ppermute | solution.py:298
  50.7 6.3 %collective-permute-start.6 = (bf16[144,256]{1,0:T(8,128)(2,1)S(1)}, bf16[144,256]{1,0:T(8,128)(2,1)S(1)}, u32[]{:S(2)}, u32[]{:S(2)}) collective-permute-start(bf16[144,256]{1,0:T(8,128)(2,1)S(1)} %get-tuple-element.28), channel_id=1, source_target_pairs={{0,24},{1,25},{2,26},{3,27},{4,28},{5,29},{6,30},{7,31},{8,16},{9,... | collective-permute-start | bytes 221192 | tf_op jit(solution)/shard_map/ppermute | solution.py:298
  58.3 4.7 %collective-permute-start.7 = (bf16[128,256]{1,0:T(8,128)(2,1)S(1)}, bf16[128,256]{1,0:T(8,128)(2,1)S(1)}, u32[]{:S(2)}, u32[]{:S(2)}) collective-permute-start(bf16[128,256]{1,0:T(8,128)(2,1)S(1)} %get-tuple-element.30), channel_id=1, source_target_pairs={{0,1},{1,0},{2,3},{3,2},{4,5},{5,4},{6,7},{7,6},{8,9},{9,8},{10,11... | collective-permute-start | bytes 196616 | tf_op jit(solution)/shard_map/ppermute | solution.py:298
  59.8 4.4 %collective-permute-start.8 = (bf16[128,256]{1,0:T(8,128)(2,1)S(1)}, bf16[128,256]{1,0:T(8,128)(2,1)S(1)}, u32[]{:S(2)}, u32[]{:S(2)}) collective-permute-start(bf16[128,256]{1,0:T(8,128)(2,1)S(1)} %get-tuple-element.31), channel_id=1, source_target_pairs={{0,2},{1,3},{2,0},{3,1},{4,6},{5,7},{6,4},{7,5},{8,10},{9,11},{10,... | collective-permute-start | bytes 196616 | tf_op jit(solution)/shard_map/ppermute | solution.py:298
  61.2 5.2 %collective-permute-start.9 = (bf16[128,256]{1,0:T(8,128)(2,1)S(1)}, bf16[128,256]{1,0:T(8,128)(2,1)S(1)}, u32[]{:S(2)}, u32[]{:S(2)}) collective-permute-start(bf16[128,256]{1,0:T(8,128)(2,1)S(1)} %get-tuple-element.32), channel_id=1, source_target_pairs={{0,3},{1,2},{2,1},{3,0},{4,7},{5,6},{6,5},{7,4},{8,11},{9,10},{10,... | collective-permute-start | bytes 196616 | tf_op jit(solution)/shard_map/ppermute | solution.py:298

commit v2 on v1

--- a/solution.py
+++ b/solution.py
@@ -17,6 +17,7 @@
 AXES = ("hit", "head")
 VMEM = pl.BlockSpec(memory_space=pltpu.VMEM)
 SMEM = pl.BlockSpec(memory_space=pltpu.SMEM)
+HBM = pl.BlockSpec(memory_space=pltpu.HBM)
 PARAMS = pltpu.CompilerParams(vmem_limit_bytes=40 << 20)
 
 
@@ -37,26 +38,50 @@
     return pieces
 
 
-def project_kernel(flip, where_ref, hits_ref, k_ref, v_ref, out_ref):
-    width = out_ref.shape[1] // 2
-    out_ref[:, :width] = mul(hits_ref[...], k_ref[...]).astype(BF16)
-    out_ref[:, width:] = mul(hits_ref[...], v_ref[...]).astype(BF16)
-
-
-def project(flip, where, hits, k_weight, v_weight, width):
+def project_kernel(flips, where_ref, hits_ref, k_ref, v_ref, *refs):
+    outs = refs[: len(flips)]
+    hits_here, weights, both, in_sems, out_sems = refs[len(flips) :]
+    width = weights.shape[2] // 2
+    hits_copy = pltpu.make_async_copy(hits_ref, hits_here, in_sems.at[0, 0])
+    hits_copy.start()
+    copies = []
+    for at, flip in enumerate(flips):
+        columns = pl.ds(pl.multiple_of((where_ref[0] ^ flip) * width, width), width)
+        for side, source in enumerate((k_ref, v_ref)):
+            target = weights.at[at, :, pl.ds(side * width, width)]
+            copies.append(
+                pltpu.make_async_copy(source.at[:, columns], target, in_sems.at[at + 1, side])
+            )
+            copies[-1].start()
+    hits_copy.wait()
+    out_copies = []
+    for at, out in enumerate(outs):
+        copies[2 * at].wait()
+        copies[2 * at + 1].wait()
+        both[at] = mul(hits_here[...], weights[at]).astype(BF16)
+        out_copies.append(pltpu.make_async_copy(both.at[at], out, out_sems.at[at]))
+        out_copies[-1].start()
+    for copy in out_copies:
+        copy.wait()
+
+
+def project(flips, where, hits, k_weight, v_weight, width):
     rows, depth = hits.shape
-    weight = pl.BlockSpec((depth, width), lambda i, where: (0, where[0] ^ flip))
-    return pl.pallas_call(
-        functools.partial(project_kernel, flip),
-        grid_spec=pltpu.PrefetchScalarGridSpec(
-            num_scalar_prefetch=1,
-            grid=(1,),
-            in_specs=[pl.BlockSpec((rows, depth), lambda i, where: (0, 0)), weight, weight],
-            out_specs=pl.BlockSpec((rows, 2 * width), lambda i, where: (0, 0)),
-        ),
-        out_shape=struct((rows, 2 * width)),
-        compiler_params=PARAMS,
-        name=f"project{flip}",
+    count = len(flips)
+    return pl.pallas_call(
+        functools.partial(project_kernel, flips),
+        in_specs=[SMEM, HBM, HBM, HBM],
+        out_specs=[HBM] * count,
+        out_shape=[struct((rows, 2 * width))] * count,
+        scratch_shapes=[
+            pltpu.VMEM((rows, depth), BF16),
+            pltpu.VMEM((count, depth, 2 * width), BF16),
+            pltpu.VMEM((count, rows, 2 * width), BF16),
+            pltpu.SemaphoreType.DMA((count + 1, 2)),
+            pltpu.SemaphoreType.DMA((count,)),
+        ],
+        compiler_params=pltpu.CompilerParams(vmem_limit_bytes=60 << 20),
+        name="project" + "".join(map(str, flips)),
     )(where, hits, k_weight, v_weight)
 
 
@@ -94,21 +119,11 @@
     )(slots, q_weight)
 
 
-def attend_kernel(count, first, last, *refs):
+def attend_kernel(count, *refs):
     where_ref, q_ref = refs[:2]
     kv_refs = refs[2 : 2 + count]
     mask_refs = refs[2 + count : 2 + 2 * count]
-    rest = list(refs[2 + 2 * count :])
-    if not first:
-        acc_in, stat_in = rest[:2]
-        rest = rest[2:]
-    if last:
-        keep_ref, send_ref = rest[:2]
-        rest = rest[2:]
-    else:
-        acc_out, stat_out = rest[:2]
-        rest = rest[2:]
-    ke_ref, ve_ref = rest[:2]
+    keep_ref, send_ref, ke_ref, ve_ref, value_ref, stat_ref = refs[2 + 2 * count :]
     heads, slots = q_ref.shape[:2]
     pairs = heads // 2
     hits = kv_refs[0].shape[0]
@@ -135,45 +150,27 @@
     slot_low = slot_lane < HEAD_DIM
     for step in range(slots // block):
         rows = pl.ds(step * block, block)
-        stat = jnp.zeros((block, 128), F32) if first else stat_in[rows, :]
-        new_stat = jnp.zeros((block, 128), F32)
+        stat = jnp.zeros((block, 128), F32)
         for pair in range(pairs):
             outs = []
-            for odd in range(2):
-                head = 2 * pair + odd
+            for head in (2 * pair, 2 * pair + 1):
                 scores = mul(q_ref[head, rows, :], ke_ref[head], NT)
                 top = jnp.max(scores, axis=1, keepdims=True)
-                if not first:
-                    old_top = stat[:, head : head + 1]
-                    top = jnp.maximum(top, old_top)
                 weights = jnp.exp2(scores - top).astype(BF16)
                 both = mul(weights, ve_ref[pair])
-                total = both[:, 128:]
-                value = both[:, :128]
-                if not first:
-                    keep = jnp.exp2(old_top - top)
-                    total = total + stat[:, 8 + head : 9 + head] * keep
-                    value = value + acc_in[pair, rows, :] * keep
-                if last:
-                    value = value / total
-                new_stat = jnp.where(slot_lane == head, top, new_stat)
-                new_stat = jnp.where(slot_lane == 8 + head, total, new_stat)
-                outs.append(value)
+                outs.append(both[:, :128] / both[:, 128:])
+                stat = jnp.where(slot_lane == head, top, stat)
+                stat = jnp.where(slot_lane == 8 + head, both[:, 128:], stat)
             value = jnp.where(slot_low, outs[0], outs[1])
-            if last:
-                rest[2][:, pair * 128 : (pair + 1) * 128] = value.astype(BF16)
-            else:
-                acc_out[pair, rows, :] = value
-        if last:
-            core = where_ref[1]
-            rest[3][...] = new_stat
-            for target, place in ((keep_ref, core), (send_ref, 1 - core)):
-                part = pl.ds(pl.multiple_of(place * half, half), half)
-                target[step, :half, :] = rest[2][part, :]
-                flat = rest[3][part, :].T
-                target[step, half:, :] = pack(flat[:heads], flat[8 : 8 + heads])
-        else:
-            stat_out[rows, :] = new_stat
+            value_ref[rows, pair * 128 : (pair + 1) * 128] = value.astype(BF16)
+        stat_ref[rows, :] = stat
+    core = where_ref[1]
+    for step in range(slots // block):
+        for target, place in ((keep_ref, core), (send_ref, 1 - core)):
+            part = pl.ds(pl.multiple_of(step * block + place * half, half), half)
+            target[step, :half, :] = value_ref[part, :]
+            flat = stat_ref[part, :].T
+            target[step, half:, :] = pack(flat[:heads], flat[8 : 8 + heads])
 
 
 def pack(top, total):
@@ -193,33 +190,31 @@
     return top, total
 
 
-def attend(where, queries, sources, masks, carry, last):
+def attend(where, queries, sources, masks):
     heads, slots, _ = queries.shape
     pairs = heads // 2
     count = len(sources)
     hits = sources[0].shape[0]
     block = 256
-    message = (slots // block, block // 2 + 4 * heads, heads * HEAD_DIM)
-    scratch = [pltpu.VMEM((heads, count * hits, 256), BF16), pltpu.VMEM((pairs, count * hits, 256), BF16)]
-    if last:
-        out_shape = (struct(message), struct(message))
-        scratch += [pltpu.VMEM((block, heads * HEAD_DIM), BF16), pltpu.VMEM((block, 128), F32)]
-    else:
-        out_shape = (struct((pairs, slots, 128), F32), struct((slots, 128), F32))
-    args = [where, queries, *sources, *masks, *carry]
+    message = struct((slots // block, block // 2 + 4 * heads, heads * HEAD_DIM))
     scores = heads * slots * count * hits
     return pl.pallas_call(
-        functools.partial(attend_kernel, count, not carry, last),
-        in_specs=[SMEM] + [VMEM] * (len(args) - 1),
+        functools.partial(attend_kernel, count),
+        in_specs=[SMEM] + [VMEM] * (1 + 2 * count),
         out_specs=(VMEM, VMEM),
-        out_shape=out_shape,
-        scratch_shapes=scratch,
+        out_shape=(message, message),
+        scratch_shapes=[
+            pltpu.VMEM((heads, count * hits, 256), BF16),
+            pltpu.VMEM((pairs, count * hits, 256), BF16),
+            pltpu.VMEM((slots, heads * HEAD_DIM), BF16),
+            pltpu.VMEM((slots, 128), F32),
+        ],
         compiler_params=PARAMS,
         cost_estimate=pl.CostEstimate(
             flops=2 * scores * 512, bytes_accessed=4 << 20, transcendentals=scores
         ),
         name=f"attend{count}",
-    )(*args)
+    )(where, queries, *sources, *masks)
 
 
 def join(messages, heads):
@@ -243,25 +238,26 @@
     return jnp.concatenate(outs, axis=1).astype(BF16), top, total
 
 
-def core_kernel(heads, where_ref, own_ref, other_ref, *outs):
-    slots = own_ref.shape[1] - 4 * heads
+def core_kernel(heads, count, where_ref, *refs):
+    given, outs = refs[:count], refs[count:]
+    slots = given[0].shape[1] - 4 * heads
     for flip, out in enumerate(outs):
         place = where_ref[2] ^ flip
-        value, top, total = join([own_ref.at[place], other_ref.at[place]], heads)
+        value, top, total = join([one.at[place] for one in given], heads)
         out[:slots, :] = value
         out[slots:, :] = pack(top, total)
 
 
-def core_join(where, own, other, heads):
-    chips, rows, width = own.shape
-    return pl.pallas_call(
-        functools.partial(core_kernel, heads),
-        in_specs=[SMEM, VMEM, VMEM],
+def core_join(where, given, heads):
+    chips, rows, width = given[0].shape
+    return pl.pallas_call(
+        functools.partial(core_kernel, heads, len(given)),
+        in_specs=[SMEM] + [VMEM] * len(given),
         out_specs=[VMEM] * chips,
         out_shape=[struct((rows, width))] * chips,
         compiler_params=PARAMS,
         name="core_join",
-    )(where, own, other)
+    )(where, *given)
 
 
 def out_kernel(heads, where_ref, o_ref, m0, m1, m2, m3, own_ref, *refs):
@@ -308,16 +304,22 @@
     def mask_of(flip):
         return lax.dynamic_index_in_dim(masks, head ^ flip, 0, keepdims=False)
 
-    ours = {flip: project(flip, where, hits, k_weight, v_weight, width) for flip in (3, 1, 2, 0)}
-    theirs = {flip: move(ours[flip], 0, flip) for flip in (3, 1, 2)}
+    ours = {}
+    for flips in ((1, 2), (3, 0)):
+        ours.update(zip(flips, project(flips, where, hits, k_weight, v_weight, width)))
     queries = query(slots, q_weight)
-    carry = attend(where, queries, [ours[0]], [mask_of(0)], (), False)
-    carry = attend(where, queries, [theirs[3]], [mask_of(3)], carry, False)
-    kept, sent = attend(
-        where, queries, [theirs[1], theirs[2]], [mask_of(1), mask_of(2)], carry, True
-    )
-    other = move(sent, 1, 0)
-    parts = core_join(where, kept, other, heads)
+    theirs = {0: ours[0]}
+    theirs.update((flip, move(ours[flip], 0, flip)) for flip in (1, 2))
+    parts = []
+    for flips in ((0,), (1, 2), (3,)):
+        kept, sent = attend(
+            where, queries, [theirs[flip] for flip in flips], [mask_of(flip) for flip in flips]
+        )
+        parts += [kept, move(sent, 1, 0)]
+        if flips == (0,):
+            ours[3], sent = lax.optimization_barrier((ours[3], sent))
+            theirs[3] = move(ours[3], 0, 3)
+    parts = core_join(where, parts, heads)
     messages = [parts[0]] + [move(parts[flip], 2 * flip, 0) for flip in (1, 2, 3)]
     shares = out_project(where, o_weight, messages, heads)
     total = shares[0]

time: 67.3 us -> 61.5 us (0.914)
  local copies, waits for them, and re-layouts: 5.23 us -> 0.05 us
  Pallas kernels: 31.9 us -> 29.9 us
  waiting for transfers between devices: 16.4 us -> 17.1 us
    unnamed x18 -> x14, local copies, waits for them, and re-layouts: 5.22 us -> 0.03 us
    pallas_call x8 -> x6, Pallas kernels: 28.5 us -> 26.6 us  [the longest x3 14.9 us: attend(): pl.pallas_call(functools.partial(attend_kernel, count), in_specs=[SMEM] +...]
    ppermute x10 -> x12, waiting for transfers between devices: 16.4 us -> 17.1 us  [move(): return lax.ppermute(value, AXES, pairs)]
    ppermute x10 -> x12, starting transfers between devices: 12.6 us -> 12.8 us  [move(): return lax.ppermute(value, AXES, pairs)]
  transfers between devices with their start and end apart: 10 -> 12, of which waited for: 7 -> 7; matrix products, arithmetic and copies ran while one was open for 0% -> 0% of each run, Pallas kernels for 27% -> 35%
where the time goes in v2:
time: 61.5 us; the launch traced here: 61.3 us
  Pallas kernels  29.9 us (49%)
  waiting for transfers between devices  17.1 us (28%)
  starting transfers between devices  12.8 us (21%)
  other arithmetic  1.25 us (2%)
    ppermute x12, waiting for transfers between devices, move(): return lax.ppermute(value, AXES, pairs)  17.1 us
    pallas_call x3, Pallas kernels, attend(): pl.pallas_call(functools.partial(attend_kernel, count), in_specs=[SMEM] +...  14.9 us
    ppermute x12, starting transfers between devices, move(): return lax.ppermute(value, AXES, pairs)  12.8 us
    pallas_call x2, Pallas kernels, project(): pl.pallas_call(functools.partial(project_kernel, flips), in_specs=[SMEM,...  9.09 us
    pallas_call x1, Pallas kernels, core_join(): pl.pallas_call(functools.partial(core_kernel, heads, len(given)), in_spec...  2.67 us
    pallas_call x1, Pallas kernels, query(): pl.pallas_call(query_kernel, grid=(rows // block,), in_specs=[pl.BlockSpe...  1.95 us
    pallas_call x1, Pallas kernels, out_project(): pl.pallas_call(functools.partial(out_kernel, heads), in_specs=[SMEM] + [V...  1.3 us
  transfers between devices with their start and end apart: 12, of which 7 were waited for; matrix products, arithmetic and copies ran while one was open for 0% of the time, Pallas kernels for 35%

profile of v2, /device:TPU:0, one launch (start us, length us, event | category | flops | bytes accessed | tf_op | source)
XLA Modules:
  0.0 61.3 jit_solution(17072699203105419974)
XLA Ops:
  0.0 0.6 pad_add_fusion.where_ref.refs_0_
  0.6 4.5 %project12.1 = (bf16[512,512]{1,0:T(8,128)(2,1)}, bf16[512,512]{1,0:T(8,128)(2,1)}) custom-call(s32[4]{0:T(128)} %pad_add_fusion.where_ref.refs_0_, bf16[512,1024]{1,0:T(8,128)(2,1)} %hits_ref.3, bf16[1024,1024]{1,0:T(8,128)(2,1)} %k_ref.3, bf16[1024,1024]{1,0:T(8,128)(2,1)} %v_ref.3), custom_call_target="tpu_custom_call" | custom-call | tf_op jit(solution)/shard_map/project12/pallas_call | solution.py:71
  5.1 3.0 %collective-permute-start.1 = (bf16[512,512]{1,0:T(8,128)(2,1)}, bf16[512,512]{1,0:T(8,128)(2,1)S(1)}, u32[]{:S(2)}, u32[]{:S(2)}) collective-permute-start(bf16[512,512]{1,0:T(8,128)(2,1)} %get-tuple-element.27), channel_id=1, source_target_pairs={{0,1},{1,0},{2,3},{3,2},{4,5},{5,4},{6,7},{7,6},{8,9},{9,8},{10,11... | collective-permute-start | bytes 1572872 | tf_op jit(solution)/shard_map/ppermute | solution.py:294
  8.1 1.5 %collective-permute-start.2 = (bf16[512,512]{1,0:T(8,128)(2,1)}, bf16[512,512]{1,0:T(8,128)(2,1)}, u32[]{:S(2)}, u32[]{:S(2)}) collective-permute-start(bf16[512,512]{1,0:T(8,128)(2,1)} %get-tuple-element.28), channel_id=1, source_target_pairs={{0,2},{1,3},{2,0},{3,1},{4,6},{5,7},{6,4},{7,5},{8,10},{9,11},{10,... | collective-permute-start | bytes 1572872 | tf_op jit(solution)/shard_map/ppermute | solution.py:294
  9.6 4.6 %project30.1 = (bf16[512,512]{1,0:T(8,128)(2,1)}, bf16[512,512]{1,0:T(8,128)(2,1)}) custom-call(s32[4]{0:T(128)} %pad_add_fusion.where_ref.refs_0_, bf16[512,1024]{1,0:T(8,128)(2,1)} %hits_ref.3, bf16[1024,1024]{1,0:T(8,128)(2,1)} %k_ref.3, bf16[1024,1024]{1,0:T(8,128)(2,1)} %v_ref.3), custom_call_target="tpu_custom_call" | custom-call | tf_op jit(solution)/shard_map/project30/pallas_call | solution.py:71
  14.3 2.0 %query.1.refs_1_ = bf16[4,1024,256]{2,1,0:T(8,128)(2,1)S(1)} custom-call(bf16[1024,1024]{1,0:T(8,128)(2,1)S(1)} %copy-done, bf16[1024,256]{1,0:T(8,128)(2,1)S(1)} %copy-done.1), custom_call_target="tpu_custom_call" | custom-call | tf_op jit(solution)/shard_map/query/pallas_call | solution.py:108
  16.3 3.8 %attend1.2 = (bf16[4,144,256]{2,1,0:T(8,128)(2,1)S(1)}, bf16[4,144,256]{2,1,0:T(8,128)(2,1)S(1)}) custom-call(s32[4]{0:T(128)S(1)} %copy-done.3, bf16[4,1024,256]{2,1,0:T(8,128)(2,1)S(1)} %query.1.refs_1_, bf16[512,512]{1,0:T(8,128)(2,1)S(1)} %copy-done.4, s32[1,512]{1,0:T(1,128)S(1)} %get-tuple-element.46.refs_3_), custom_call_target="tpu_custom_call" | custom-call | flops 2147483648 | bytes 4194304 | tf_op jit(solution)/shard_map/attend1/pallas_call | solution.py:201
  20.3 1.5 %collective-permute-done.2.refs_3_ = bf16[512,512]{1,0:T(8,128)(2,1)} collective-permute-done((bf16[512,512]{1,0:T(8,128)(2,1)}, bf16[512,512]{1,0:T(8,128)(2,1)}, u32[]{:S(2)}, u32[]{:S(2)}) %collective-permute-start.2) | collective-permute-done | bytes 524320 | tf_op jit(solution)/shard_map/ppermute | solution.py:294
  21.8 7.1 %attend2.1 = (bf16[4,144,256]{2,1,0:T(8,128)(2,1)S(1)}, bf16[4,144,256]{2,1,0:T(8,128)(2,1)S(1)}) custom-call(s32[4]{0:T(128)S(1)} %copy-done.3, bf16[4,1024,256]{2,1,0:T(8,128)(2,1)S(1)} %query.1.refs_1_, bf16[512,512]{1,0:T(8,128)(2,1)S(1)} %collective-permute-done.1.refs_2_, bf16[512,512]{1,0:T(8,128)(2,1)} %collective-permute-done.2.refs_3_, ...), custom_call_target="tpu_custom_call" | custom-call | flops 4294967296 | bytes 4194304 | tf_op jit(solution)/shard_map/attend2/pallas_call | solution.py:201
  28.9 5.3 %collective-permute-done.4.refs_2_ = bf16[512,512]{1,0:T(8,128)(2,1)S(1)} collective-permute-done((bf16[512,512]{1,0:T(8,128)(2,1)S(1)}, bf16[512,512]{1,0:T(8,128)(2,1)S(1)}, u32[]{:S(2)}, u32[]{:S(2)}) %collective-permute-start.4) | collective-permute-done | bytes 524320 | tf_op jit(solution)/shard_map/ppermute | solution.py:294
  34.2 4.0 %attend1.3 = (bf16[4,144,256]{2,1,0:T(8,128)(2,1)S(1)}, bf16[4,144,256]{2,1,0:T(8,128)(2,1)S(1)}) custom-call(s32[4]{0:T(128)S(1)} %copy-done.3, bf16[4,1024,256]{2,1,0:T(8,128)(2,1)S(1)} %query.1.refs_1_, bf16[512,512]{1,0:T(8,128)(2,1)S(1)} %collective-permute-done.4.refs_2_, s32[1,512]{1,0:T(1,128)S(1)} %get-tuple-element.43.refs_3_), custom_call_target="tpu_custom_call" | custom-call | flops 2147483648 | bytes 4194304 | tf_op jit(solution)/shard_map/attend1/pallas_call | solution.py:201
  38.3 1.5 %collective-permute-done.5.refs_5_ = bf16[4,144,256]{2,1,0:T(8,128)(2,1)S(1)} collective-permute-done((bf16[4,144,256]{2,1,0:T(8,128)(2,1)S(1)}, bf16[4,144,256]{2,1,0:T(8,128)(2,1)S(1)}, u32[]{:S(2)}, u32[]{:S(2)}) %collective-permute-start.5) | collective-permute-done | bytes 294944 | tf_op jit(solution)/shard_map/ppermute | solution.py:294
  39.9 2.7 %core_join.1 = (bf16[144,256]{1,0:T(8,128)(2,1)S(1)}, bf16[144,256]{1,0:T(8,128)(2,1)S(1)}, bf16[144,256]{1,0:T(8,128)(2,1)S(1)}, bf16[144,256]{1,0:T(8,128)(2,1)S(1)}) custom-call(s32[4]{0:T(128)S(1)} %copy-done.3, bf16[4,144,256]{2,1,0:T(8,128)(2,1)S(1)} %get-tuple-element.25.refs_0_, bf16[4,144,256]{2,1,0:T(8,128)(2,1)S(1)} %collective-permute-done.refs_1_, ...), custom_call_target="tpu_custom_call" | custom-call | tf_op jit(solution)/shard_map/core_join/pallas_call | solution.py:253
  42.5 1.7 %collective-permute-start.6 = (bf16[144,256]{1,0:T(8,128)(2,1)S(1)}, bf16[144,256]{1,0:T(8,128)(2,1)S(1)}, u32[]{:S(2)}, u32[]{:S(2)}) collective-permute-start(bf16[144,256]{1,0:T(8,128)(2,1)S(1)} %get-tuple-element.36), channel_id=1, source_target_pairs={{0,8},{1,9},{2,10},{3,11},{4,12},{5,13},{6,14},{7,15},{8,0},{9,1},... | collective-permute-start | bytes 221192 | tf_op jit(solution)/shard_map/ppermute | solution.py:294
  44.2 2.6 %collective-permute-start.7 = (bf16[144,256]{1,0:T(8,128)(2,1)S(1)}, bf16[144,256]{1,0:T(8,128)(2,1)S(1)}, u32[]{:S(2)}, u32[]{:S(2)}) collective-permute-start(bf16[144,256]{1,0:T(8,128)(2,1)S(1)} %get-tuple-element.37), channel_id=1, source_target_pairs={{0,16},{1,17},{2,18},{3,19},{4,20},{5,21},{6,22},{7,23},{8,24},{9,... | collective-permute-start | bytes 221192 | tf_op jit(solution)/shard_map/ppermute | solution.py:294
  47.0 6.1 %collective-permute-done.7.m2 = bf16[144,256]{1,0:T(8,128)(2,1)S(1)} collective-permute-done((bf16[144,256]{1,0:T(8,128)(2,1)S(1)}, bf16[144,256]{1,0:T(8,128)(2,1)S(1)}, u32[]{:S(2)}, u32[]{:S(2)}) %collective-permute-start.7) | collective-permute-done | bytes 73760 | tf_op jit(solution)/shard_map/ppermute | solution.py:294
  53.1 1.3 %out_project.1 = (f32[128,256]{1,0:T(8,128)S(1)}, bf16[128,256]{1,0:T(8,128)(2,1)S(1)}, bf16[128,256]{1,0:T(8,128)(2,1)S(1)}, bf16[128,256]{1,0:T(8,128)(2,1)S(1)}) custom-call(s32[4]{0:T(128)S(1)} %copy-done.3, bf16[256,1024]{1,0:T(8,128)(2,1)S(1)} %copy-done.2, bf16[144,256]{1,0:T(8,128)(2,1)S(1)} %get-tuple-element.35.m0, ...), custom_call_target="tpu_custom_call" | custom-call | tf_op jit(solution)/shard_map/out_project/pallas_call | solution.py:276
  54.4 0.6 collective-permute-start.9
  55.0 0.5 collective-permute-start.10
  55.5 2.4 %collective-permute-start.11 = (bf16[128,256]{1,0:T(8,128)(2,1)S(1)}, bf16[128,256]{1,0:T(8,128)(2,1)S(1)}, u32[]{:S(2)}, u32[]{:S(2)}) collective-permute-start(bf16[128,256]{1,0:T(8,128)(2,1)S(1)} %get-tuple-element.42), channel_id=1, source_target_pairs={{0,3},{1,2},{2,1},{3,0},{4,7},{5,6},{6,5},{7,4},{8,11},{9,10},{10,... | collective-permute-start | bytes 196616 | tf_op jit(solution)/shard_map/ppermute | solution.py:294
  57.9 0.8 %collective-permute-done.9 = bf16[128,256]{1,0:T(8,128)(2,1)S(1)} collective-permute-done((bf16[128,256]{1,0:T(8,128)(2,1)S(1)}, bf16[128,256]{1,0:T(8,128)(2,1)S(1)}, u32[]{:S(2)}, u32[]{:S(2)}) %collective-permute-start.9) | collective-permute-done | bytes 65568 | tf_op jit(solution)/shard_map/ppermute | solution.py:294
  58.7 0.5 collective-permute-done.10
  59.2 1.4 %collective-permute-done.11 = bf16[128,256]{1,0:T(8,128)(2,1)S(1)} collective-permute-done((bf16[128,256]{1,0:T(8,128)(2,1)S(1)}, bf16[128,256]{1,0:T(8,128)(2,1)S(1)}, u32[]{:S(2)}, u32[]{:S(2)}) %collective-permute-start.11) | collective-permute-done | bytes 65568 | tf_op jit(solution)/shard_map/ppermute | solution.py:294
  60.6 0.7 %add_convert_fusion = bf16[128,256]{1,0:T(8,128)(2,1)} fusion(bf16[128,256]{1,0:T(8,128)(2,1)S(1)} %collective-permute-done.11, bf16[128,256]{1,0:T(8,128)(2,1)S(1)} %collective-permute-done.10, f32[128,256]{1,0:T(8,128)S(1)} %get-tuple-element.39, bf16[128,256]{1,0:T(8,128)(2,1)S(1)} %collective-permute-done.9), kind=kLoop, calls=%fused_computation | loop fusion | flops 229376 | bytes 393216 | tf_op jit(solution)/shard_map/convert_element_type | solution.py:328
  (25 shorter events, 0.6 us)
Async XLA Ops:
  5.1 15.2 %collective-permute-start.1 = (bf16[512,512]{1,0:T(8,128)(2,1)}, bf16[512,512]{1,0:T(8,128)(2,1)S(1)}, u32[]{:S(2)}, u32[]{:S(2)}) collective-permute-start(bf16[512,512]{1,0:T(8,128)(2,1)} %get-tuple-element.27), channel_id=1, source_target_pairs={{0,1},{1,0},{2,3},{3,2},{4,5},{5,4},{6,7},{7,6},{8,9},{9,8},{10,11... | collective-permute-start | bytes 1572872 | tf_op jit(solution)/shard_map/ppermute | solution.py:294
  8.1 13.7 %collective-permute-start.2 = (bf16[512,512]{1,0:T(8,128)(2,1)}, bf16[512,512]{1,0:T(8,128)(2,1)}, u32[]{:S(2)}, u32[]{:S(2)}) collective-permute-start(bf16[512,512]{1,0:T(8,128)(2,1)} %get-tuple-element.28), channel_id=1, source_target_pairs={{0,2},{1,3},{2,0},{3,1},{4,6},{5,7},{6,4},{7,5},{8,10},{9,11},{10,... | collective-permute-start | bytes 1572872 | tf_op jit(solution)/shard_map/ppermute | solution.py:294
  9.6 4.6 %copy-start = (bf16[1024,1024]{1,0:T(8,128)(2,1)S(1)}, bf16[1024,1024]{1,0:T(8,128)(2,1)}, u32[]{:S(2)}) copy-start(bf16[1024,1024]{1,0:T(8,128)(2,1)} %slots_ref.1) | copy-start | bytes 6291460
  9.6 4.7 %copy-start.1 = (bf16[1024,256]{1,0:T(8,128)(2,1)S(1)}, bf16[1024,256]{1,0:T(8,128)(2,1)}, u32[]{:S(2)}) copy-start(bf16[1024,256]{1,0:T(8,128)(2,1)} %q_ref.1) | copy-start | bytes 1572868
  14.3 2.0 %copy-start.5 = (s32[2048]{0:T(1024)S(1)}, s32[2048]{0:T(1024)}, u32[]{:S(2)}) copy-start(s32[2048]{0:T(1024)} %param.9) | copy-start | bytes 24580
  14.3 2.0 %copy-start.3 = (s32[4]{0:T(128)S(1)}, s32[4]{0:T(128)}, u32[]{:S(2)}) copy-start(s32[4]{0:T(128)} %pad_add_fusion.where_ref.refs_0_) | copy-start | bytes 52
  14.3 2.0 %copy-start.4 = (bf16[512,512]{1,0:T(8,128)(2,1)S(1)}, bf16[512,512]{1,0:T(8,128)(2,1)}, u32[]{:S(2)}) copy-start(bf16[512,512]{1,0:T(8,128)(2,1)} %get-tuple-element.24.refs_2_) | copy-start | bytes 1572868
  16.3 3.8 %copy-start.6 = (bf16[512,512]{1,0:T(8,128)(2,1)S(1)}, bf16[512,512]{1,0:T(8,128)(2,1)}, u32[]{:S(2)}) copy-start(bf16[512,512]{1,0:T(8,128)(2,1)} %get-tuple-element.32) | copy-start | bytes 1572868
  20.1 14.1 %collective-permute-start.4 = (bf16[512,512]{1,0:T(8,128)(2,1)S(1)}, bf16[512,512]{1,0:T(8,128)(2,1)S(1)}, u32[]{:S(2)}, u32[]{:S(2)}) collective-permute-start(bf16[512,512]{1,0:T(8,128)(2,1)S(1)} %copy-done.6), channel_id=1, source_target_pairs={{0,3},{1,2},{2,1},{3,0},{4,7},{5,6},{6,5},{7,4},{8,11},{9,10},{10,... | collective-permute-start | bytes 1572872 | tf_op jit(solution)/shard_map/ppermute | solution.py:294
  20.2 18.1 %collective-permute-start = (bf16[4,144,256]{2,1,0:T(8,128)(2,1)S(1)}, bf16[4,144,256]{2,1,0:T(8,128)(2,1)S(1)}, u32[]{:S(2)}, u32[]{:S(2)}) collective-permute-start(bf16[4,144,256]{2,1,0:T(8,128)(2,1)S(1)} %get-tuple-element.26), channel_id=1, source_target_pairs={{0,4},{1,5},{2,6},{3,7},{4,0},{5,1},{6,2},{7,3},{8,12},{9,13},{10,... | collective-permute-start | bytes 884744 | tf_op jit(solution)/shard_map/ppermute | solution.py:294
  28.9 9.5 %collective-permute-start.3 = (bf16[4,144,256]{2,1,0:T(8,128)(2,1)S(1)}, bf16[4,144,256]{2,1,0:T(8,128)(2,1)S(1)}, u32[]{:S(2)}, u32[]{:S(2)}) collective-permute-start(bf16[4,144,256]{2,1,0:T(8,128)(2,1)S(1)} %get-tuple-element.30), channel_id=1, source_target_pairs={{0,4},{1,5},{2,6},{3,7},{4,0},{5,1},{6,2},{7,3},{8,12},{9,13},{10,... | collective-permute-start | bytes 884744 | tf_op jit(solution)/shard_map/ppermute | solution.py:294
  38.2 14.9 %copy-start.2 = (bf16[256,1024]{1,0:T(8,128)(2,1)S(1)}, bf16[256,1024]{1,0:T(8,128)(2,1)}, u32[]{:S(2)}) copy-start(bf16[256,1024]{1,0:T(8,128)(2,1)} %o_ref.1) | copy-start | bytes 1572868
  38.2 1.6 %collective-permute-start.5 = (bf16[4,144,256]{2,1,0:T(8,128)(2,1)S(1)}, bf16[4,144,256]{2,1,0:T(8,128)(2,1)S(1)}, u32[]{:S(2)}, u32[]{:S(2)}) collective-permute-start(bf16[4,144,256]{2,1,0:T(8,128)(2,1)S(1)} %get-tuple-element.34), channel_id=1, source_target_pairs={{0,4},{1,5},{2,6},{3,7},{4,0},{5,1},{6,2},{7,3},{8,12},{9,13},{10,... | collective-permute-start | bytes 884744 | tf_op jit(solution)/shard_map/ppermute | solution.py:294
  42.5 4.5 %collective-permute-start.6 = (bf16[144,256]{1,0:T(8,128)(2,1)S(1)}, bf16[144,256]{1,0:T(8,128)(2,1)S(1)}, u32[]{:S(2)}, u32[]{:S(2)}) collective-permute-start(bf16[144,256]{1,0:T(8,128)(2,1)S(1)} %get-tuple-element.36), channel_id=1, source_target_pairs={{0,8},{1,9},{2,10},{3,11},{4,12},{5,13},{6,14},{7,15},{8,0},{9,1},... | collective-permute-start | bytes 221192 | tf_op jit(solution)/shard_map/ppermute | solution.py:294
  44.2 8.9 %collective-permute-start.7 = (bf16[144,256]{1,0:T(8,128)(2,1)S(1)}, bf16[144,256]{1,0:T(8,128)(2,1)S(1)}, u32[]{:S(2)}, u32[]{:S(2)}) collective-permute-start(bf16[144,256]{1,0:T(8,128)(2,1)S(1)} %get-tuple-element.37), channel_id=1, source_target_pairs={{0,16},{1,17},{2,18},{3,19},{4,20},{5,21},{6,22},{7,23},{8,24},{9,... | collective-permute-start | bytes 221192 | tf_op jit(solution)/shard_map/ppermute | solution.py:294
  46.8 6.3 %collective-permute-start.8 = (bf16[144,256]{1,0:T(8,128)(2,1)S(1)}, bf16[144,256]{1,0:T(8,128)(2,1)S(1)}, u32[]{:S(2)}, u32[]{:S(2)}) collective-permute-start(bf16[144,256]{1,0:T(8,128)(2,1)S(1)} %get-tuple-element.38), channel_id=1, source_target_pairs={{0,24},{1,25},{2,26},{3,27},{4,28},{5,29},{6,30},{7,31},{8,16},{9,... | collective-permute-start | bytes 221192 | tf_op jit(solution)/shard_map/ppermute | solution.py:294
  54.4 4.3 %collective-permute-start.9 = (bf16[128,256]{1,0:T(8,128)(2,1)S(1)}, bf16[128,256]{1,0:T(8,128)(2,1)S(1)}, u32[]{:S(2)}, u32[]{:S(2)}) collective-permute-start(bf16[128,256]{1,0:T(8,128)(2,1)S(1)} %get-tuple-element.40), channel_id=1, source_target_pairs={{0,1},{1,0},{2,3},{3,2},{4,5},{5,4},{6,7},{7,6},{8,9},{9,8},{10,11... | collective-permute-start | bytes 196616 | tf_op jit(solution)/shard_map/ppermute | solution.py:294
  55.0 4.3 %collective-permute-start.10 = (bf16[128,256]{1,0:T(8,128)(2,1)S(1)}, bf16[128,256]{1,0:T(8,128)(2,1)S(1)}, u32[]{:S(2)}, u32[]{:S(2)}) collective-permute-start(bf16[128,256]{1,0:T(8,128)(2,1)S(1)} %get-tuple-element.41), channel_id=1, source_target_pairs={{0,2},{1,3},{2,0},{3,1},{4,6},{5,7},{6,4},{7,5},{8,10},{9,11},{10,... | collective-permute-start | bytes 196616 | tf_op jit(solution)/shard_map/ppermute | solution.py:294
  55.5 5.2 %collective-permute-start.11 = (bf16[128,256]{1,0:T(8,128)(2,1)S(1)}, bf16[128,256]{1,0:T(8,128)(2,1)S(1)}, u32[]{:S(2)}, u32[]{:S(2)}) collective-permute-start(bf16[128,256]{1,0:T(8,128)(2,1)S(1)} %get-tuple-element.42), channel_id=1, source_target_pairs={{0,3},{1,2},{2,1},{3,0},{4,7},{5,6},{6,5},{7,4},{8,11},{9,10},{10,... | collective-permute-start | bytes 196616 | tf_op jit(solution)/shard_map/ppermute | solution.py:294

commit v3 on v2

--- a/solution.py
+++ b/solution.py
@@ -16,7 +16,6 @@
 SCALE = HEAD_DIM**-0.5 * math.log2(math.e)
 AXES = ("hit", "head")
 VMEM = pl.BlockSpec(memory_space=pltpu.VMEM)
-SMEM = pl.BlockSpec(memory_space=pltpu.SMEM)
 HBM = pl.BlockSpec(memory_space=pltpu.HBM)
 PARAMS = pltpu.CompilerParams(vmem_limit_bytes=40 << 20)
 
@@ -38,15 +37,15 @@
     return pieces
 
 
-def project_kernel(flips, where_ref, hits_ref, k_ref, v_ref, *refs):
-    outs = refs[: len(flips)]
-    hits_here, weights, both, in_sems, out_sems = refs[len(flips) :]
+def project_kernel(flips, hits_ref, k_ref, v_ref, *refs):
+    outs = refs[: -len(PROJECT_SCRATCH)]
+    hits_here, weights, in_sems = refs[-len(PROJECT_SCRATCH) :]
     width = weights.shape[2] // 2
     hits_copy = pltpu.make_async_copy(hits_ref, hits_here, in_sems.at[0, 0])
     hits_copy.start()
     copies = []
-    for at, flip in enumerate(flips):
-        columns = pl.ds(pl.multiple_of((where_ref[0] ^ flip) * width, width), width)
+    for at, (flip, _) in enumerate(flips):
+        columns = pl.ds(pl.multiple_of((lax.axis_index("head") ^ flip) * width, width), width)
         for side, source in enumerate((k_ref, v_ref)):
             target = weights.at[at, :, pl.ds(side * width, width)]
             copies.append(
@@ -54,35 +53,36 @@
             )
             copies[-1].start()
     hits_copy.wait()
-    out_copies = []
     for at, out in enumerate(outs):
         copies[2 * at].wait()
         copies[2 * at + 1].wait()
-        both[at] = mul(hits_here[...], weights[at]).astype(BF16)
-        out_copies.append(pltpu.make_async_copy(both.at[at], out, out_sems.at[at]))
-        out_copies[-1].start()
-    for copy in out_copies:
-        copy.wait()
-
-
-def project(flips, where, hits, k_weight, v_weight, width):
+        out[...] = mul(hits_here[...], weights[at]).astype(BF16)
+
+
+PROJECT_SCRATCH = ("hits", "weights", "in")
+
+
+def project(flips, hits, k_weight, v_weight, width):
     rows, depth = hits.shape
     count = len(flips)
-    return pl.pallas_call(
+    shapes = [struct((rows // pieces, 2 * width)) for _, pieces in flips for _ in range(pieces)]
+    outs = pl.pallas_call(
         functools.partial(project_kernel, flips),
-        in_specs=[SMEM, HBM, HBM, HBM],
-        out_specs=[HBM] * count,
-        out_shape=[struct((rows, 2 * width))] * count,
+        in_specs=[HBM, HBM, HBM],
+        out_specs=[VMEM] * len(shapes),
+        out_shape=shapes,
         scratch_shapes=[
             pltpu.VMEM((rows, depth), BF16),
             pltpu.VMEM((count, depth, 2 * width), BF16),
-            pltpu.VMEM((count, rows, 2 * width), BF16),
             pltpu.SemaphoreType.DMA((count + 1, 2)),
-            pltpu.SemaphoreType.DMA((count,)),
         ],
-        compiler_params=pltpu.CompilerParams(vmem_limit_bytes=60 << 20),
-        name="project" + "".join(map(str, flips)),
-    )(where, hits, k_weight, v_weight)
+        compiler_params=pltpu.CompilerParams(vmem_limit_bytes=58 << 20),
+        name="project" + "".join(str(flip) for flip, _ in flips),
+    )(hits, k_weight, v_weight)
+    taken = {}
+    for flip, pieces in flips:
+        taken[flip], outs = outs[:pieces], outs[pieces:]
+    return taken
 
 
 def query_kernel(slots_ref, q_ref, out_ref):
@@ -120,10 +120,10 @@
 
 
 def attend_kernel(count, *refs):
-    where_ref, q_ref = refs[:2]
-    kv_refs = refs[2 : 2 + count]
-    mask_refs = refs[2 + count : 2 + 2 * count]
-    keep_ref, send_ref, ke_ref, ve_ref, value_ref, stat_ref = refs[2 + 2 * count :]
+    q_ref = refs[0]
+    kv_refs = refs[1 : 1 + count]
+    mask_refs = refs[1 + count : 1 + 2 * count]
+    keep_ref, send_ref, ke_ref, ve_ref, value_ref, stat_ref = refs[1 + 2 * count :]
     heads, slots = q_ref.shape[:2]
     pairs = heads // 2
     hits = kv_refs[0].shape[0]
@@ -158,13 +158,13 @@
                 top = jnp.max(scores, axis=1, keepdims=True)
                 weights = jnp.exp2(scores - top).astype(BF16)
                 both = mul(weights, ve_ref[pair])
-                outs.append(both[:, :128] / both[:, 128:])
+                outs.append(both[:, :128])
                 stat = jnp.where(slot_lane == head, top, stat)
                 stat = jnp.where(slot_lane == 8 + head, both[:, 128:], stat)
             value = jnp.where(slot_low, outs[0], outs[1])
             value_ref[rows, pair * 128 : (pair + 1) * 128] = value.astype(BF16)
         stat_ref[rows, :] = stat
-    core = where_ref[1]
+    core = lax.axis_index("hit") % 2
     for step in range(slots // block):
         for target, place in ((keep_ref, core), (send_ref, 1 - core)):
             part = pl.ds(pl.multiple_of(step * block + place * half, half), half)
@@ -190,7 +190,7 @@
     return top, total
 
 
-def attend(where, queries, sources, masks):
+def attend(queries, sources, masks):
     heads, slots, _ = queries.shape
     pairs = heads // 2
     count = len(sources)
@@ -200,7 +200,7 @@
     scores = heads * slots * count * hits
     return pl.pallas_call(
         functools.partial(attend_kernel, count),
-        in_specs=[SMEM] + [VMEM] * (1 + 2 * count),
+        in_specs=[VMEM] * (1 + 2 * count),
         out_specs=(VMEM, VMEM),
         out_shape=(message, message),
         scratch_shapes=[
@@ -211,77 +211,103 @@
         ],
         compiler_params=PARAMS,
         cost_estimate=pl.CostEstimate(
-            flops=2 * scores * 512, bytes_accessed=4 << 20, transcendentals=scores
+            flops=scores, bytes_accessed=1 << 20, transcendentals=0
         ),
         name=f"attend{count}",
-    )(where, queries, *sources, *masks)
-
-
-def join(messages, heads):
+    )(queries, *sources, *masks)
+
+
+def spread(count, heads):
+    shape = (256, count * heads * HEAD_DIM)
+    row = lax.broadcasted_iota(jnp.int32, shape, 0) & 127
+    column = lax.broadcasted_iota(jnp.int32, shape, 1) // HEAD_DIM
+    return jnp.where(row == column, 1.0, 0.0).astype(BF16)
+
+
+def join(messages, heads, matrix, final=False):
     slots = messages[0].shape[0] - 4 * heads
+    width = heads * HEAD_DIM
     stats = [unpack(message[slots:, :], heads) for message in messages]
     top = functools.reduce(jnp.maximum, [one for one, _ in stats])
-    shares = [total * jnp.exp2(one - top) for one, total in stats]
-    total = functools.reduce(jnp.add, shares)
-    rows = [share / total for share in shares]
+    rows = [jnp.exp2(one - top) for one, _ in stats]
+    total = functools.reduce(jnp.add, [row * one for row, (_, one) in zip(rows, stats)])
+    if final:
+        rows = [row / total for row in rows]
     rows.append(jnp.zeros((128 - len(messages) * heads, slots), F32))
-    columns = jnp.concatenate(rows, axis=0).T
-    low = lax.broadcasted_iota(jnp.int32, (slots, 128), 1) < HEAD_DIM
-    outs = []
-    for pair in range(heads // 2):
-        value = jnp.zeros((slots, 128), F32)
-        for at, message in enumerate(messages):
-            head = at * heads + 2 * pair
-            factor = jnp.where(low, columns[:, head : head + 1], columns[:, head + 1 : head + 2])
-            value = value + message[:slots, pair * 128 : (pair + 1) * 128].astype(F32) * factor
-        outs.append(value)
-    return jnp.concatenate(outs, axis=1).astype(BF16), top, total
-
-
-def core_kernel(heads, count, where_ref, *refs):
+    factors = jnp.concatenate(split(jnp.concatenate(rows, axis=0).T, 2), axis=1)
+    factors = mul(factors.astype(BF16), matrix)
+    value = jnp.zeros((slots, width), F32)
+    for at, message in enumerate(messages):
+        value = value + message[:slots, :].astype(F32) * factors[:, at * width : (at + 1) * width]
+    return value.astype(BF16), top, total
+
+
+def early_kernel(heads, *refs):
+    given, out = refs[:-1], refs[-1]
+    slots = out.shape[1] - 4 * heads
+    matrix = spread(len(given), heads)
+    for place in range(out.shape[0]):
+        value, top, total = join([one.at[place] for one in given], heads, matrix)
+        out[place, :slots, :] = value
+        out[place, slots:, :] = pack(top, total)
+
+
+def early_join(given, heads):
+    return pl.pallas_call(
+        functools.partial(early_kernel, heads),
+        in_specs=[VMEM] * len(given),
+        out_specs=VMEM,
+        out_shape=struct(given[0].shape),
+        compiler_params=PARAMS,
+        name="early_join",
+    )(*given)
+
+
+def core_kernel(heads, count, *refs):
     given, outs = refs[:count], refs[count:]
     slots = given[0].shape[1] - 4 * heads
+    matrix = spread(count, heads)
     for flip, out in enumerate(outs):
-        place = where_ref[2] ^ flip
-        value, top, total = join([one.at[place] for one in given], heads)
+        place = (lax.axis_index("hit") // 2) ^ flip
+        value, top, total = join([one.at[place] for one in given], heads, matrix)
         out[:slots, :] = value
         out[slots:, :] = pack(top, total)
 
 
-def core_join(where, given, heads):
+def core_join(given, heads):
     chips, rows, width = given[0].shape
     return pl.pallas_call(
         functools.partial(core_kernel, heads, len(given)),
-        in_specs=[SMEM] + [VMEM] * len(given),
+        in_specs=[VMEM] * len(given),
         out_specs=[VMEM] * chips,
         out_shape=[struct((rows, width))] * chips,
         compiler_params=PARAMS,
         name="core_join",
-    )(where, *given)
-
-
-def out_kernel(heads, where_ref, o_ref, m0, m1, m2, m3, own_ref, *refs):
+    )(*given)
+
+
+def out_kernel(heads, o_ref, m0, m1, m2, m3, own_ref, *refs):
     outs, full = refs[:-1], refs[-1]
-    mixed, _, _ = join([m0, m1, m2, m3], heads)
+    mixed, _, _ = join([m0, m1, m2, m3], heads, spread(4, heads), final=True)
     full[...] = mul(mixed, o_ref[...])
     width = own_ref.shape[1]
     for flip, out in enumerate((own_ref, *outs)):
-        start = pl.multiple_of((where_ref[0] ^ flip) * width, width)
+        start = pl.multiple_of((lax.axis_index("head") ^ flip) * width, width)
         out[...] = full[:, pl.ds(start, width)].astype(out.dtype)
 
 
-def out_project(where, o_weight, messages, heads):
+def out_project(o_weight, messages, heads):
     rows = messages[0].shape[0] - 4 * heads
     width = o_weight.shape[1] // 4
     return pl.pallas_call(
         functools.partial(out_kernel, heads),
-        in_specs=[SMEM] + [VMEM] * 5,
+        in_specs=[VMEM] * 5,
         out_specs=[VMEM] * 4,
         out_shape=[struct((rows, width), F32)] + [struct((rows, width))] * 3,
         scratch_shapes=[pltpu.VMEM((rows, o_weight.shape[1]), F32)],
         compiler_params=PARAMS,
         name="out_project",
-    )(where, o_weight, *messages)
+    )(o_weight, *messages)
 
 
 def move(value, hit_flip, head_flip):
@@ -297,31 +323,35 @@
 def local_plane(slots, hits, hit_mask, q_weight, k_weight, v_weight, o_weight):
     width = q_weight.shape[1]
     heads = width // HEAD_DIM
-    hit, head = lax.axis_index("hit"), lax.axis_index("head")
-    where = jnp.stack([head, hit % 2, hit // 2, hit]).astype(jnp.int32)
+    head = lax.axis_index("head")
     masks = hit_mask.reshape(4, 1, hits.shape[0])
 
     def mask_of(flip):
         return lax.dynamic_index_in_dim(masks, head ^ flip, 0, keepdims=False)
 
     ours = {}
-    for flips in ((1, 2), (3, 0)):
-        ours.update(zip(flips, project(flips, where, hits, k_weight, v_weight, width)))
+    for flips in (((1, 1), (2, 1)), ((3, 1), (0, 1))):
+        ours.update(project(flips, hits, k_weight, v_weight, width))
     queries = query(slots, q_weight)
-    theirs = {0: ours[0]}
-    theirs.update((flip, move(ours[flip], 0, flip)) for flip in (1, 2))
+    theirs = {flip: move(ours[flip][0], 0, flip) for flip in (1, 2)}
+    mine = attend(queries, ours[0], [mask_of(0)])
+    later = list(ours[3])
+    later[0], mine, theirs = lax.optimization_barrier((later[0], mine, theirs))
+    later = [move(piece, 0, 3) for piece in later]
+    straight = attend(queries, [theirs[1], theirs[2]], [mask_of(1), mask_of(2)])
     parts = []
-    for flips in ((0,), (1, 2), (3,)):
-        kept, sent = attend(
-            where, queries, [theirs[flip] for flip in flips], [mask_of(flip) for flip in flips]
-        )
+    for kept, sent in (mine, straight):
         parts += [kept, move(sent, 1, 0)]
-        if flips == (0,):
-            ours[3], sent = lax.optimization_barrier((ours[3], sent))
-            theirs[3] = move(ours[3], 0, 3)
-    parts = core_join(where, parts, heads)
+    parts = [early_join(parts, heads)]
+    queries, parts = lax.optimization_barrier((queries, parts))
+    for at, piece in enumerate(later):
+        size = piece.shape[0]
+        mask = mask_of(3)[:, at * size : (at + 1) * size]
+        kept, sent = attend(queries, [piece], [mask])
+        parts += [kept, move(sent, 1, 0)]
+    parts = core_join(parts, heads)
     messages = [parts[0]] + [move(parts[flip], 2 * flip, 0) for flip in (1, 2, 3)]
-    shares = out_project(where, o_weight, messages, heads)
+    shares = out_project(o_weight, messages, heads)
     total = shares[0]
     for flip in (1, 2, 3):
         total = total + move(shares[flip], 0, flip).astype(F32)

time: 61.5 us -> 58.6 us (0.953)
  Pallas kernels: 29.9 us -> 25.1 us
  starting transfers between devices: 12.8 us -> 14.6 us
  waiting for transfers between devices: 17.1 us -> 17.8 us
    pallas_call x6 -> x7, Pallas kernels: 25.3 us -> 22.7 us  [the longest x3 13.9 us: attend(): pl.pallas_call(functools.partial(attend_kernel, count), in_specs=[VMEM] *...]
    pallas_call x1, Pallas kernels: 2.67 us -> 0.45 us  [core_join(): pl.pallas_call(functools.partial(core_kernel, heads, len(given)), in_spec...]
    ppermute x12, starting transfers between devices: 12.8 us -> 14.6 us  [move(): return lax.ppermute(value, AXES, pairs)]
    ppermute x12, waiting for transfers between devices: 17.1 us -> 17.8 us  [move(): return lax.ppermute(value, AXES, pairs)]
  transfers between devices with their start and end apart: 12 -> 12, of which waited for: 7 -> 9; matrix products, arithmetic and copies ran while one was open for 0% -> 0% of each run, Pallas kernels for 35% -> 29%
where the time goes in v3:
time: 58.6 us; the launch traced here: 58.4 us
  Pallas kernels  25.1 us (43%)
  waiting for transfers between devices  17.8 us (30%)
  starting transfers between devices  14.6 us (25%)
  other arithmetic  0.66 us (1%)
    ppermute x12, waiting for transfers between devices, move(): return lax.ppermute(value, AXES, pairs)  17.8 us
    ppermute x12, starting transfers between devices, move(): return lax.ppermute(value, AXES, pairs)  14.6 us
    pallas_call x3, Pallas kernels, attend(): pl.pallas_call(functools.partial(attend_kernel, count), in_specs=[VMEM] *...  13.9 us
    pallas_call x2, Pallas kernels, project(): pl.pallas_call(functools.partial(project_kernel, flips), in_specs=[HBM, H...  7.73 us
    pallas_call x1, Pallas kernels, query(): pl.pallas_call(query_kernel, grid=(rows // block,), in_specs=[pl.BlockSpe...  1.95 us
  transfers between devices with their start and end apart: 12, of which 9 were waited for; matrix products, arithmetic and copies ran while one was open for 0% of the time, Pallas kernels for 29%

profile of v3, /device:TPU:0, one launch (start us, length us, event | category | flops | bytes accessed | tf_op | source)
XLA Modules:
  0.0 58.4 jit_solution(8923930816074611912)
XLA Ops:
  0.0 3.8 %project12.1 = (bf16[512,512]{1,0:T(8,128)(2,1)}, bf16[512,512]{1,0:T(8,128)(2,1)}) custom-call(bf16[512,1024]{1,0:T(8,128)(2,1)} %hits_ref.3, bf16[1024,1024]{1,0:T(8,128)(2,1)} %k_ref.3, bf16[1024,1024]{1,0:T(8,128)(2,1)} %v_ref.3), custom_call_target="tpu_custom_call" | custom-call | tf_op jit(solution)/shard_map/project12/pallas_call | solution.py:69
  3.8 3.0 %collective-permute-start = (bf16[512,512]{1,0:T(8,128)(2,1)}, bf16[512,512]{1,0:T(8,128)(2,1)S(1)}, u32[]{:S(2)}, u32[]{:S(2)}) collective-permute-start(bf16[512,512]{1,0:T(8,128)(2,1)} %get-tuple-element.34), channel_id=1, source_target_pairs={{0,1},{1,0},{2,3},{3,2},{4,5},{5,4},{6,7},{7,6},{8,9},{9,8},{10,11... | collective-permute-start | bytes 1572872 | tf_op jit(solution)/shard_map/ppermute | solution.py:320
  6.8 1.5 %collective-permute-start.1 = (bf16[512,512]{1,0:T(8,128)(2,1)}, bf16[512,512]{1,0:T(8,128)(2,1)}, u32[]{:S(2)}, u32[]{:S(2)}) collective-permute-start(bf16[512,512]{1,0:T(8,128)(2,1)} %get-tuple-element.35), channel_id=1, source_target_pairs={{0,2},{1,3},{2,0},{3,1},{4,6},{5,7},{6,4},{7,5},{8,10},{9,11},{10,... | collective-permute-start | bytes 1572872 | tf_op jit(solution)/shard_map/ppermute | solution.py:320
  8.3 3.9 %project30.1 = (bf16[512,512]{1,0:T(8,128)(2,1)}, bf16[512,512]{1,0:T(8,128)(2,1)}) custom-call(bf16[512,1024]{1,0:T(8,128)(2,1)} %hits_ref.3, bf16[1024,1024]{1,0:T(8,128)(2,1)} %k_ref.3, bf16[1024,1024]{1,0:T(8,128)(2,1)} %v_ref.3), custom_call_target="tpu_custom_call" | custom-call | tf_op jit(solution)/shard_map/project30/pallas_call | solution.py:69
  12.3 2.0 %query.1.refs_0_ = bf16[4,1024,256]{2,1,0:T(8,128)(2,1)S(1)} custom-call(bf16[1024,1024]{1,0:T(8,128)(2,1)S(1)} %copy-done, bf16[1024,256]{1,0:T(8,128)(2,1)S(1)} %copy-done.1), custom_call_target="tpu_custom_call" | custom-call | tf_op jit(solution)/shard_map/query/pallas_call | solution.py:108
  14.4 3.4 %attend1.2 = (bf16[4,144,256]{2,1,0:T(8,128)(2,1)S(1)}, bf16[4,144,256]{2,1,0:T(8,128)(2,1)S(1)}) custom-call(bf16[4,1024,256]{2,1,0:T(8,128)(2,1)S(1)} %query.1.refs_0_, bf16[512,512]{1,0:T(8,128)(2,1)S(1)} %copy-done.3, s32[1,512]{1,0:T(1,128)S(1)} %get-tuple-element.58.refs_2_), custom_call_target="tpu_custom_call" | custom-call | flops 2097152 | bytes 1048576 | tf_op jit(solution)/shard_map/attend1/pallas_call | solution.py:201
  17.7 1.2 %collective-permute-done.refs_1_ = bf16[512,512]{1,0:T(8,128)(2,1)S(1)} collective-permute-done((bf16[512,512]{1,0:T(8,128)(2,1)}, bf16[512,512]{1,0:T(8,128)(2,1)S(1)}, u32[]{:S(2)}, u32[]{:S(2)}) %collective-permute-start) | collective-permute-done | bytes 524320 | tf_op jit(solution)/shard_map/ppermute | solution.py:320
  18.9 1.6 %collective-permute-done.1.refs_2_ = bf16[512,512]{1,0:T(8,128)(2,1)} collective-permute-done((bf16[512,512]{1,0:T(8,128)(2,1)}, bf16[512,512]{1,0:T(8,128)(2,1)}, u32[]{:S(2)}, u32[]{:S(2)}) %collective-permute-start.1) | collective-permute-done | bytes 524320 | tf_op jit(solution)/shard_map/ppermute | solution.py:320
  20.5 1.5 %collective-permute-start.4 = (bf16[512,512]{1,0:T(8,128)(2,1)S(1)}, bf16[512,512]{1,0:T(8,128)(2,1)S(1)}, u32[]{:S(2)}, u32[]{:S(2)}) collective-permute-start(bf16[512,512]{1,0:T(8,128)(2,1)S(1)} %copy-done.5), channel_id=1, source_target_pairs={{0,3},{1,2},{2,1},{3,0},{4,7},{5,6},{6,5},{7,4},{8,11},{9,10},{10,... | collective-permute-start | bytes 1572872 | tf_op jit(solution)/shard_map/ppermute | solution.py:320
  22.0 7.2 %attend2.1 = (bf16[4,144,256]{2,1,0:T(8,128)(2,1)S(1)}, bf16[4,144,256]{2,1,0:T(8,128)(2,1)S(1)}) custom-call(bf16[4,1024,256]{2,1,0:T(8,128)(2,1)S(1)} %query.1.refs_0_, bf16[512,512]{1,0:T(8,128)(2,1)S(1)} %collective-permute-done.refs_1_, bf16[512,512]{1,0:T(8,128)(2,1)} %collective-permute-done.1.refs_2_, s32[1,512]{1,0:T(1,128)S(1)} %get-tuple-element.57.refs_3_, ...), custom_call_target="tpu_custom_call" | custom-call | flops 4194304 | bytes 1048576 | tf_op jit(solution)/shard_map/attend2/pallas_call | solution.py:201
  29.8 1.2 %collective-permute-done.3.refs_3_ = bf16[4,144,256]{2,1,0:T(8,128)(2,1)S(1)} collective-permute-done((bf16[4,144,256]{2,1,0:T(8,128)(2,1)S(1)}, bf16[4,144,256]{2,1,0:T(8,128)(2,1)S(1)}, u32[]{:S(2)}, u32[]{:S(2)}) %collective-permute-start.3) | collective-permute-done | bytes 294944 | tf_op jit(solution)/shard_map/ppermute | solution.py:320
  31.5 2.4 %collective-permute-done.4.refs_1_ = bf16[512,512]{1,0:T(8,128)(2,1)S(1)} collective-permute-done((bf16[512,512]{1,0:T(8,128)(2,1)S(1)}, bf16[512,512]{1,0:T(8,128)(2,1)S(1)}, u32[]{:S(2)}, u32[]{:S(2)}) %collective-permute-start.4) | collective-permute-done | bytes 524320 | tf_op jit(solution)/shard_map/ppermute | solution.py:320
  33.9 3.4 %attend1.3 = (bf16[4,144,256]{2,1,0:T(8,128)(2,1)S(1)}, bf16[4,144,256]{2,1,0:T(8,128)(2,1)S(1)}) custom-call(bf16[4,1024,256]{2,1,0:T(8,128)(2,1)S(1)} %query.1.refs_0_, bf16[512,512]{1,0:T(8,128)(2,1)S(1)} %collective-permute-done.4.refs_1_, s32[1,512]{1,0:T(1,128)S(1)} %get-tuple-element.55.refs_2_), custom_call_target="tpu_custom_call" | custom-call | flops 2097152 | bytes 1048576 | tf_op jit(solution)/shard_map/attend1/pallas_call | solution.py:201
  37.3 1.6 %collective-permute-done.5.refs_2_ = bf16[4,144,256]{2,1,0:T(8,128)(2,1)S(1)} collective-permute-done((bf16[4,144,256]{2,1,0:T(8,128)(2,1)S(1)}, bf16[4,144,256]{2,1,0:T(8,128)(2,1)S(1)}, u32[]{:S(2)}, u32[]{:S(2)}) %collective-permute-start.5) | collective-permute-done | bytes 294944 | tf_op jit(solution)/shard_map/ppermute | solution.py:320
  39.3 1.6 %collective-permute-start.6 = (bf16[144,256]{1,0:T(8,128)(2,1)S(1)}, bf16[144,256]{1,0:T(8,128)(2,1)S(1)}, u32[]{:S(2)}, u32[]{:S(2)}) collective-permute-start(bf16[144,256]{1,0:T(8,128)(2,1)S(1)} %get-tuple-element.48), channel_id=1, source_target_pairs={{0,8},{1,9},{2,10},{3,11},{4,12},{5,13},{6,14},{7,15},{8,0},{9,1},... | collective-permute-start | bytes 221192 | tf_op jit(solution)/shard_map/ppermute | solution.py:320
  41.0 2.6 %collective-permute-start.7 = (bf16[144,256]{1,0:T(8,128)(2,1)S(1)}, bf16[144,256]{1,0:T(8,128)(2,1)S(1)}, u32[]{:S(2)}, u32[]{:S(2)}) collective-permute-start(bf16[144,256]{1,0:T(8,128)(2,1)S(1)} %get-tuple-element.49), channel_id=1, source_target_pairs={{0,16},{1,17},{2,18},{3,19},{4,20},{5,21},{6,22},{7,23},{8,24},{9,... | collective-permute-start | bytes 221192 | tf_op jit(solution)/shard_map/ppermute | solution.py:320
  43.8 6.0 %collective-permute-done.7.m2 = bf16[144,256]{1,0:T(8,128)(2,1)S(1)} collective-permute-done((bf16[144,256]{1,0:T(8,128)(2,1)S(1)}, bf16[144,256]{1,0:T(8,128)(2,1)S(1)}, u32[]{:S(2)}, u32[]{:S(2)}) %collective-permute-start.7) | collective-permute-done | bytes 73760 | tf_op jit(solution)/shard_map/ppermute | solution.py:320
  50.4 0.7 %collective-permute-start.9 = (bf16[128,256]{1,0:T(8,128)(2,1)S(1)}, bf16[128,256]{1,0:T(8,128)(2,1)S(1)}, u32[]{:S(2)}, u32[]{:S(2)}) collective-permute-start(bf16[128,256]{1,0:T(8,128)(2,1)S(1)} %get-tuple-element.52), channel_id=1, source_target_pairs={{0,1},{1,0},{2,3},{3,2},{4,5},{5,4},{6,7},{7,6},{8,9},{9,8},{10,11... | collective-permute-start | bytes 196616 | tf_op jit(solution)/shard_map/ppermute | solution.py:320
  51.1 1.5 %collective-permute-start.10 = (bf16[128,256]{1,0:T(8,128)(2,1)S(1)}, bf16[128,256]{1,0:T(8,128)(2,1)S(1)}, u32[]{:S(2)}, u32[]{:S(2)}) collective-permute-start(bf16[128,256]{1,0:T(8,128)(2,1)S(1)} %get-tuple-element.53), channel_id=1, source_target_pairs={{0,2},{1,3},{2,0},{3,1},{4,6},{5,7},{6,4},{7,5},{8,10},{9,11},{10,... | collective-permute-start | bytes 196616 | tf_op jit(solution)/shard_map/ppermute | solution.py:320
  52.6 1.3 %collective-permute-start.11 = (bf16[128,256]{1,0:T(8,128)(2,1)S(1)}, bf16[128,256]{1,0:T(8,128)(2,1)S(1)}, u32[]{:S(2)}, u32[]{:S(2)}) collective-permute-start(bf16[128,256]{1,0:T(8,128)(2,1)S(1)} %get-tuple-element.54), channel_id=1, source_target_pairs={{0,3},{1,2},{2,1},{3,0},{4,7},{5,6},{6,5},{7,4},{8,11},{9,10},{10,... | collective-permute-start | bytes 196616 | tf_op jit(solution)/shard_map/ppermute | solution.py:320
  53.9 0.8 %collective-permute-done.9 = bf16[128,256]{1,0:T(8,128)(2,1)S(1)} collective-permute-done((bf16[128,256]{1,0:T(8,128)(2,1)S(1)}, bf16[128,256]{1,0:T(8,128)(2,1)S(1)}, u32[]{:S(2)}, u32[]{:S(2)}) %collective-permute-start.9) | collective-permute-done | bytes 65568 | tf_op jit(solution)/shard_map/ppermute | solution.py:320
  54.7 0.6 %collective-permute-done.10 = bf16[128,256]{1,0:T(8,128)(2,1)S(1)} collective-permute-done((bf16[128,256]{1,0:T(8,128)(2,1)S(1)}, bf16[128,256]{1,0:T(8,128)(2,1)S(1)}, u32[]{:S(2)}, u32[]{:S(2)}) %collective-permute-start.10) | collective-permute-done | bytes 65568 | tf_op jit(solution)/shard_map/ppermute | solution.py:320
  55.3 2.4 %collective-permute-done.11 = bf16[128,256]{1,0:T(8,128)(2,1)S(1)} collective-permute-done((bf16[128,256]{1,0:T(8,128)(2,1)S(1)}, bf16[128,256]{1,0:T(8,128)(2,1)S(1)}, u32[]{:S(2)}, u32[]{:S(2)}) %collective-permute-start.11) | collective-permute-done | bytes 65568 | tf_op jit(solution)/shard_map/ppermute | solution.py:320
  57.8 0.7 %add_convert_fusion = bf16[128,256]{1,0:T(8,128)(2,1)} fusion(bf16[128,256]{1,0:T(8,128)(2,1)S(1)} %collective-permute-done.11, bf16[128,256]{1,0:T(8,128)(2,1)S(1)} %collective-permute-done.10, f32[128,256]{1,0:T(8,128)S(1)} %get-tuple-element.51, bf16[128,256]{1,0:T(8,128)(2,1)S(1)} %collective-permute-done.9), kind=kLoop, calls=%fused_computation | loop fusion | flops 229376 | bytes 393216 | tf_op jit(solution)/shard_map/convert_element_type | solution.py:358
  (23 shorter events, 2.4 us)
Async XLA Ops:
  3.8 15.1 %collective-permute-start = (bf16[512,512]{1,0:T(8,128)(2,1)}, bf16[512,512]{1,0:T(8,128)(2,1)S(1)}, u32[]{:S(2)}, u32[]{:S(2)}) collective-permute-start(bf16[512,512]{1,0:T(8,128)(2,1)} %get-tuple-element.34), channel_id=1, source_target_pairs={{0,1},{1,0},{2,3},{3,2},{4,5},{5,4},{6,7},{7,6},{8,9},{9,8},{10,11... | collective-permute-start | bytes 1572872 | tf_op jit(solution)/shard_map/ppermute | solution.py:320
  6.8 13.7 %collective-permute-start.1 = (bf16[512,512]{1,0:T(8,128)(2,1)}, bf16[512,512]{1,0:T(8,128)(2,1)}, u32[]{:S(2)}, u32[]{:S(2)}) collective-permute-start(bf16[512,512]{1,0:T(8,128)(2,1)} %get-tuple-element.35), channel_id=1, source_target_pairs={{0,2},{1,3},{2,0},{3,1},{4,6},{5,7},{6,4},{7,5},{8,10},{9,11},{10,... | collective-permute-start | bytes 1572872 | tf_op jit(solution)/shard_map/ppermute | solution.py:320
  8.3 4.0 %copy-start = (bf16[1024,1024]{1,0:T(8,128)(2,1)S(1)}, bf16[1024,1024]{1,0:T(8,128)(2,1)}, u32[]{:S(2)}) copy-start(bf16[1024,1024]{1,0:T(8,128)(2,1)} %slots_ref.1) | copy-start | bytes 6291460
  8.3 4.0 %copy-start.1 = (bf16[1024,256]{1,0:T(8,128)(2,1)S(1)}, bf16[1024,256]{1,0:T(8,128)(2,1)}, u32[]{:S(2)}) copy-start(bf16[1024,256]{1,0:T(8,128)(2,1)} %q_ref.1) | copy-start | bytes 1572868
  12.3 2.0 %copy-start.4 = (s32[2048]{0:T(1024)S(1)}, s32[2048]{0:T(1024)}, u32[]{:S(2)}) copy-start(s32[2048]{0:T(1024)} %param.9) | copy-start | bytes 24580
  12.3 2.0 %copy-start.3 = (bf16[512,512]{1,0:T(8,128)(2,1)S(1)}, bf16[512,512]{1,0:T(8,128)(2,1)}, u32[]{:S(2)}) copy-start(bf16[512,512]{1,0:T(8,128)(2,1)} %get-tuple-element.31.refs_1_) | copy-start | bytes 1572868
  14.3 6.2 %copy-start.5 = (bf16[512,512]{1,0:T(8,128)(2,1)S(1)}, bf16[512,512]{1,0:T(8,128)(2,1)}, u32[]{:S(2)}) copy-start(bf16[512,512]{1,0:T(8,128)(2,1)} %get-tuple-element.44) | copy-start | bytes 1572868
  20.5 13.4 %collective-permute-start.4 = (bf16[512,512]{1,0:T(8,128)(2,1)S(1)}, bf16[512,512]{1,0:T(8,128)(2,1)S(1)}, u32[]{:S(2)}, u32[]{:S(2)}) collective-permute-start(bf16[512,512]{1,0:T(8,128)(2,1)S(1)} %copy-done.5), channel_id=1, source_target_pairs={{0,3},{1,2},{2,1},{3,0},{4,7},{5,6},{6,5},{7,4},{8,11},{9,10},{10,... | collective-permute-start | bytes 1572872 | tf_op jit(solution)/shard_map/ppermute | solution.py:320
  22.0 7.8 %collective-permute-start.2 = (bf16[4,144,256]{2,1,0:T(8,128)(2,1)S(1)}, bf16[4,144,256]{2,1,0:T(8,128)(2,1)S(1)}, u32[]{:S(2)}, u32[]{:S(2)}) collective-permute-start(bf16[4,144,256]{2,1,0:T(8,128)(2,1)S(1)} %get-tuple-element.37), channel_id=1, source_target_pairs={{0,4},{1,5},{2,6},{3,7},{4,0},{5,1},{6,2},{7,3},{8,12},{9,13},{10,... | collective-permute-start | bytes 884744 | tf_op jit(solution)/shard_map/ppermute | solution.py:320
  29.2 1.8 %collective-permute-start.3 = (bf16[4,144,256]{2,1,0:T(8,128)(2,1)S(1)}, bf16[4,144,256]{2,1,0:T(8,128)(2,1)S(1)}, u32[]{:S(2)}, u32[]{:S(2)}) collective-permute-start(bf16[4,144,256]{2,1,0:T(8,128)(2,1)S(1)} %get-tuple-element.41), channel_id=1, source_target_pairs={{0,4},{1,5},{2,6},{3,7},{4,0},{5,1},{6,2},{7,3},{8,12},{9,13},{10,... | collective-permute-start | bytes 884744 | tf_op jit(solution)/shard_map/ppermute | solution.py:320
  31.5 18.3 %copy-start.2 = (bf16[256,1024]{1,0:T(8,128)(2,1)S(1)}, bf16[256,1024]{1,0:T(8,128)(2,1)}, u32[]{:S(2)}) copy-start(bf16[256,1024]{1,0:T(8,128)(2,1)} %o_ref.1) | copy-start | bytes 1572868
  37.2 1.6 %collective-permute-start.5 = (bf16[4,144,256]{2,1,0:T(8,128)(2,1)S(1)}, bf16[4,144,256]{2,1,0:T(8,128)(2,1)S(1)}, u32[]{:S(2)}, u32[]{:S(2)}) collective-permute-start(bf16[4,144,256]{2,1,0:T(8,128)(2,1)S(1)} %get-tuple-element.46), channel_id=1, source_target_pairs={{0,4},{1,5},{2,6},{3,7},{4,0},{5,1},{6,2},{7,3},{8,12},{9,13},{10,... | collective-permute-start | bytes 884744 | tf_op jit(solution)/shard_map/ppermute | solution.py:320
  39.3 4.5 %collective-permute-start.6 = (bf16[144,256]{1,0:T(8,128)(2,1)S(1)}, bf16[144,256]{1,0:T(8,128)(2,1)S(1)}, u32[]{:S(2)}, u32[]{:S(2)}) collective-permute-start(bf16[144,256]{1,0:T(8,128)(2,1)S(1)} %get-tuple-element.48), channel_id=1, source_target_pairs={{0,8},{1,9},{2,10},{3,11},{4,12},{5,13},{6,14},{7,15},{8,0},{9,1},... | collective-permute-start | bytes 221192 | tf_op jit(solution)/shard_map/ppermute | solution.py:320
  41.0 8.9 %collective-permute-start.7 = (bf16[144,256]{1,0:T(8,128)(2,1)S(1)}, bf16[144,256]{1,0:T(8,128)(2,1)S(1)}, u32[]{:S(2)}, u32[]{:S(2)}) collective-permute-start(bf16[144,256]{1,0:T(8,128)(2,1)S(1)} %get-tuple-element.49), channel_id=1, source_target_pairs={{0,16},{1,17},{2,18},{3,19},{4,20},{5,21},{6,22},{7,23},{8,24},{9,... | collective-permute-start | bytes 221192 | tf_op jit(solution)/shard_map/ppermute | solution.py:320
  43.6 6.3 %collective-permute-start.8 = (bf16[144,256]{1,0:T(8,128)(2,1)S(1)}, bf16[144,256]{1,0:T(8,128)(2,1)S(1)}, u32[]{:S(2)}, u32[]{:S(2)}) collective-permute-start(bf16[144,256]{1,0:T(8,128)(2,1)S(1)} %get-tuple-element.50), channel_id=1, source_target_pairs={{0,24},{1,25},{2,26},{3,27},{4,28},{5,29},{6,30},{7,31},{8,16},{9,... | collective-permute-start | bytes 221192 | tf_op jit(solution)/shard_map/ppermute | solution.py:320
  50.4 4.3 %collective-permute-start.9 = (bf16[128,256]{1,0:T(8,128)(2,1)S(1)}, bf16[128,256]{1,0:T(8,128)(2,1)S(1)}, u32[]{:S(2)}, u32[]{:S(2)}) collective-permute-start(bf16[128,256]{1,0:T(8,128)(2,1)S(1)} %get-tuple-element.52), channel_id=1, source_target_pairs={{0,1},{1,0},{2,3},{3,2},{4,5},{5,4},{6,7},{7,6},{8,9},{9,8},{10,11... | collective-permute-start | bytes 196616 | tf_op jit(solution)/shard_map/ppermute | solution.py:320
  51.1 4.3 %collective-permute-start.10 = (bf16[128,256]{1,0:T(8,128)(2,1)S(1)}, bf16[128,256]{1,0:T(8,128)(2,1)S(1)}, u32[]{:S(2)}, u32[]{:S(2)}) collective-permute-start(bf16[128,256]{1,0:T(8,128)(2,1)S(1)} %get-tuple-element.53), channel_id=1, source_target_pairs={{0,2},{1,3},{2,0},{3,1},{4,6},{5,7},{6,4},{7,5},{8,10},{9,11},{10,... | collective-permute-start | bytes 196616 | tf_op jit(solution)/shard_map/ppermute | solution.py:320
  52.6 5.2 %collective-permute-start.11 = (bf16[128,256]{1,0:T(8,128)(2,1)S(1)}, bf16[128,256]{1,0:T(8,128)(2,1)S(1)}, u32[]{:S(2)}, u32[]{:S(2)}) collective-permute-start(bf16[128,256]{1,0:T(8,128)(2,1)S(1)} %get-tuple-element.54), channel_id=1, source_target_pairs={{0,3},{1,2},{2,1},{3,0},{4,7},{5,6},{6,5},{7,4},{8,11},{9,10},{10,... | collective-permute-start | bytes 196616 | tf_op jit(solution)/shard_map/ppermute | solution.py:320

commit v4 on v3

--- a/solution.py
+++ b/solution.py
@@ -53,10 +53,15 @@
             )
             copies[-1].start()
     hits_copy.wait()
-    for at, out in enumerate(outs):
+    place = 0
+    for at, (_, pieces) in enumerate(flips):
         copies[2 * at].wait()
         copies[2 * at + 1].wait()
-        out[...] = mul(hits_here[...], weights[at]).astype(BF16)
+        both = mul(hits_here[...], weights[at]).astype(BF16)
+        rows = both.shape[0] // pieces
+        for piece in range(pieces):
+            outs[place][...] = both[piece * rows : (piece + 1) * rows]
+            place += 1
 
 
 PROJECT_SCRATCH = ("hits", "weights", "in")
@@ -119,12 +124,13 @@
     )(slots, q_weight)
 
 
-def attend_kernel(count, *refs):
+def attend_kernel(count, sides, *refs):
     q_ref = refs[0]
     kv_refs = refs[1 : 1 + count]
     mask_refs = refs[1 + count : 1 + 2 * count]
-    keep_ref, send_ref, ke_ref, ve_ref, value_ref, stat_ref = refs[1 + 2 * count :]
-    heads, slots = q_ref.shape[:2]
+    targets = refs[1 + 2 * count : -2]
+    ke_ref, ve_ref = refs[-2:]
+    heads = q_ref.shape[0]
     pairs = heads // 2
     hits = kv_refs[0].shape[0]
     lane = lax.broadcasted_iota(jnp.int32, (hits, 128), 1)
@@ -144,33 +150,38 @@
             start = (pairs + pair) * 128
             ve_ref[pair, rows, :128] = kv_refs[at][:, start : start + 128]
             ve_ref[pair, rows, 128:] = jnp.ones((hits, 128), BF16)
-    block = 256
-    half = block // 2
-    slot_lane = lax.broadcasted_iota(jnp.int32, (block, 128), 1)
+    core = lax.axis_index("hit") % 2
+    blocks = targets[0].shape[0]
+    half = targets[0].shape[1] - 4 * heads
+    slot_lane = lax.broadcasted_iota(jnp.int32, (2 * half, 128), 1)
     slot_low = slot_lane < HEAD_DIM
-    for step in range(slots // block):
-        rows = pl.ds(step * block, block)
-        stat = jnp.zeros((block, 128), F32)
-        for pair in range(pairs):
-            outs = []
-            for head in (2 * pair, 2 * pair + 1):
-                scores = mul(q_ref[head, rows, :], ke_ref[head], NT)
-                top = jnp.max(scores, axis=1, keepdims=True)
-                weights = jnp.exp2(scores - top).astype(BF16)
-                both = mul(weights, ve_ref[pair])
-                outs.append(both[:, :128])
-                stat = jnp.where(slot_lane == head, top, stat)
-                stat = jnp.where(slot_lane == 8 + head, both[:, 128:], stat)
-            value = jnp.where(slot_low, outs[0], outs[1])
-            value_ref[rows, pair * 128 : (pair + 1) * 128] = value.astype(BF16)
-        stat_ref[rows, :] = stat
-    core = lax.axis_index("hit") % 2
-    for step in range(slots // block):
-        for target, place in ((keep_ref, core), (send_ref, 1 - core)):
-            part = pl.ds(pl.multiple_of(step * block + place * half, half), half)
-            target[step, :half, :] = value_ref[part, :]
-            flat = stat_ref[part, :].T
-            target[step, half:, :] = pack(flat[:heads], flat[8 : 8 + heads])
+    for side, target in zip(sides, targets):
+        place = core if side == "keep" else 1 - core
+        for block in range(0, blocks, 2):
+            rows = [
+                pl.ds(pl.multiple_of((2 * (block + one) + place) * half, half), half)
+                for one in range(2)
+            ]
+            stat = jnp.zeros((2 * half, 128), F32)
+            for pair in range(pairs):
+                outs = []
+                for head in (2 * pair, 2 * pair + 1):
+                    queries = jnp.concatenate([q_ref[head, one, :] for one in rows], axis=0)
+                    scores = mul(queries, ke_ref[head], NT)
+                    top = jnp.max(scores, axis=1, keepdims=True)
+                    weights = jnp.exp2(scores - top).astype(BF16)
+                    both = mul(weights, ve_ref[pair])
+                    outs.append(both[:, :128])
+                    stat = jnp.where(slot_lane == head, top, stat)
+                    stat = jnp.where(slot_lane == 8 + head, both[:, 128:], stat)
+                value = jnp.where(slot_low, outs[0], outs[1]).astype(BF16)
+                for one in range(2):
+                    target[block + one, :half, pair * 128 : (pair + 1) * 128] = value[
+                        one * half : (one + 1) * half
+                    ]
+            for one in range(2):
+                flat = stat[one * half : (one + 1) * half].T
+                target[block + one, half:, :] = pack(flat[:heads], flat[8 : 8 + heads])
 
 
 def pack(top, total):
@@ -190,30 +201,25 @@
     return top, total
 
 
-def attend(queries, sources, masks):
+def attend(queries, sources, masks, sides=("keep", "send")):
     heads, slots, _ = queries.shape
-    pairs = heads // 2
     count = len(sources)
     hits = sources[0].shape[0]
-    block = 256
-    message = struct((slots // block, block // 2 + 4 * heads, heads * HEAD_DIM))
-    scores = heads * slots * count * hits
+    half = slots // (lax.axis_size("hit"))
+    message = struct((lax.axis_size("hit") // 2, half + 4 * heads, heads * HEAD_DIM))
+    scores = heads * slots * count * hits * len(sides) // 2
     return pl.pallas_call(
-        functools.partial(attend_kernel, count),
+        functools.partial(attend_kernel, count, sides),
         in_specs=[VMEM] * (1 + 2 * count),
-        out_specs=(VMEM, VMEM),
-        out_shape=(message, message),
+        out_specs=[VMEM] * len(sides),
+        out_shape=[message] * len(sides),
         scratch_shapes=[
             pltpu.VMEM((heads, count * hits, 256), BF16),
-            pltpu.VMEM((pairs, count * hits, 256), BF16),
-            pltpu.VMEM((slots, heads * HEAD_DIM), BF16),
-            pltpu.VMEM((slots, 128), F32),
+            pltpu.VMEM((heads // 2, count * hits, 256), BF16),
         ],
         compiler_params=PARAMS,
-        cost_estimate=pl.CostEstimate(
-            flops=scores, bytes_accessed=1 << 20, transcendentals=0
-        ),
-        name=f"attend{count}",
+        cost_estimate=pl.CostEstimate(flops=scores, bytes_accessed=1 << 20, transcendentals=0),
+        name=f"attend{count}_" + "_".join(sides),
     )(queries, *sources, *masks)
 
 
@@ -336,9 +342,10 @@
     theirs = {flip: move(ours[flip][0], 0, flip) for flip in (1, 2)}
     mine = attend(queries, ours[0], [mask_of(0)])
     later = list(ours[3])
-    later[0], mine, theirs = lax.optimization_barrier((later[0], mine, theirs))
+    later[0], mine = lax.optimization_barrier((later[0], mine))
     later = [move(piece, 0, 3) for piece in later]
-    straight = attend(queries, [theirs[1], theirs[2]], [mask_of(1), mask_of(2)])
+    theirs[2], theirs[1] = lax.optimization_barrier((theirs[2], theirs[1]))
+    straight = attend(queries, [theirs[2], theirs[1]], [mask_of(2), mask_of(1)])
     parts = []
     for kept, sent in (mine, straight):
         parts += [kept, move(sent, 1, 0)]
@@ -347,8 +354,9 @@
     for at, piece in enumerate(later):
         size = piece.shape[0]
         mask = mask_of(3)[:, at * size : (at + 1) * size]
-        kept, sent = attend(queries, [piece], [mask])
-        parts += [kept, move(sent, 1, 0)]
+        (sent,) = attend(queries, [piece], [mask], ("send",))
+        parts.append(move(sent, 1, 0))
+        parts += attend(queries, [piece], [mask], ("keep",))
     parts = core_join(parts, heads)
     messages = [parts[0]] + [move(parts[flip], 2 * flip, 0) for flip in (1, 2, 3)]
     shares = out_project(o_weight, messages, heads)

time: 58.6 us -> 55.2 us (0.942)
  starting transfers between devices: 14.6 us -> 12.8 us
  waiting for transfers between devices: 17.8 us -> 16.1 us
    ppermute x12, starting transfers between devices: 14.6 us -> 12.8 us  [move(): return lax.ppermute(value, AXES, pairs)]
    ppermute x12, waiting for transfers between devices: 17.8 us -> 16.1 us  [move(): return lax.ppermute(value, AXES, pairs)]
    pallas_call x3 -> x4, Pallas kernels: 13.9 us -> 14.1 us  [attend(): pl.pallas_call(functools.partial(attend_kernel, count, sides), in_specs=[...]
  transfers between devices with their start and end apart: 12 -> 12, of which waited for: 9 -> 9; matrix products, arithmetic and copies ran while one was open for 0% -> 0% of each run, Pallas kernels for 29% -> 34%
where the time goes in v4:
time: 55.2 us; the launch traced here: 55.1 us
  Pallas kernels  25.3 us (46%)
  waiting for transfers between devices  16.1 us (29%)
  starting transfers between devices  12.8 us (23%)
  other arithmetic  0.67 us (1%)
    ppermute x12, waiting for transfers between devices, move(): return lax.ppermute(value, AXES, pairs)  16.1 us
    pallas_call x4, Pallas kernels, attend(): pl.pallas_call(functools.partial(attend_kernel, count, sides), in_specs=[...  14.1 us
    ppermute x12, starting transfers between devices, move(): return lax.ppermute(value, AXES, pairs)  12.8 us
    pallas_call x2, Pallas kernels, project(): pl.pallas_call(functools.partial(project_kernel, flips), in_specs=[HBM, H...  7.75 us
    pallas_call x1, Pallas kernels, query(): pl.pallas_call(query_kernel, grid=(rows // block,), in_specs=[pl.BlockSpe...  1.95 us
  transfers between devices with their start and end apart: 12, of which 9 were waited for; matrix products, arithmetic and copies ran while one was open for 0% of the time, Pallas kernels for 34%

profile of v4, /device:TPU:0, one launch (start us, length us, event | category | flops | bytes accessed | tf_op | source)
XLA Modules:
  0.0 55.1 jit_solution(5578162702333795170)
XLA Ops:
  0.0 3.8 %project12.1 = (bf16[512,512]{1,0:T(8,128)(2,1)}, bf16[512,512]{1,0:T(8,128)(2,1)}) custom-call(bf16[512,1024]{1,0:T(8,128)(2,1)} %hits_ref.3, bf16[1024,1024]{1,0:T(8,128)(2,1)} %k_ref.3, bf16[1024,1024]{1,0:T(8,128)(2,1)} %v_ref.3), custom_call_target="tpu_custom_call" | custom-call | tf_op jit(solution)/shard_map/project12/pallas_call | solution.py:74
  3.8 3.0 %collective-permute-start.1 = (bf16[512,512]{1,0:T(8,128)(2,1)}, bf16[512,512]{1,0:T(8,128)(2,1)S(1)}, u32[]{:S(2)}, u32[]{:S(2)}) collective-permute-start(bf16[512,512]{1,0:T(8,128)(2,1)} %get-tuple-element.34), channel_id=1, source_target_pairs={{0,2},{1,3},{2,0},{3,1},{4,6},{5,7},{6,4},{7,5},{8,10},{9,11},{10,... | collective-permute-start | bytes 1572872 | tf_op jit(solution)/shard_map/ppermute | solution.py:326
  6.8 1.5 %collective-permute-start.2 = (bf16[512,512]{1,0:T(8,128)(2,1)}, bf16[512,512]{1,0:T(8,128)(2,1)}, u32[]{:S(2)}, u32[]{:S(2)}) collective-permute-start(bf16[512,512]{1,0:T(8,128)(2,1)} %get-tuple-element.35), channel_id=1, source_target_pairs={{0,1},{1,0},{2,3},{3,2},{4,5},{5,4},{6,7},{7,6},{8,9},{9,8},{10,11... | collective-permute-start | bytes 1572872 | tf_op jit(solution)/shard_map/ppermute | solution.py:326
  8.3 3.9 %project30.1 = (bf16[512,512]{1,0:T(8,128)(2,1)}, bf16[512,512]{1,0:T(8,128)(2,1)}) custom-call(bf16[512,1024]{1,0:T(8,128)(2,1)} %hits_ref.3, bf16[1024,1024]{1,0:T(8,128)(2,1)} %k_ref.3, bf16[1024,1024]{1,0:T(8,128)(2,1)} %v_ref.3), custom_call_target="tpu_custom_call" | custom-call | tf_op jit(solution)/shard_map/project30/pallas_call | solution.py:74
  12.4 2.0 %query.1.refs_0_ = bf16[4,1024,256]{2,1,0:T(8,128)(2,1)S(1)} custom-call(bf16[1024,1024]{1,0:T(8,128)(2,1)S(1)} %copy-done, bf16[1024,256]{1,0:T(8,128)(2,1)S(1)} %copy-done.1), custom_call_target="tpu_custom_call" | custom-call | tf_op jit(solution)/shard_map/query/pallas_call | solution.py:113
  14.4 3.2 %attend1_keep_send.1 = (bf16[4,144,256]{2,1,0:T(8,128)(2,1)S(1)}, bf16[4,144,256]{2,1,0:T(8,128)(2,1)S(1)}) custom-call(bf16[4,1024,256]{2,1,0:T(8,128)(2,1)S(1)} %query.1.refs_0_, bf16[512,512]{1,0:T(8,128)(2,1)S(1)} %copy-done.3, s32[1,512]{1,0:T(1,128)S(1)} %get-tuple-element.54.refs_2_), custom_call_target="tpu_custom_call" | custom-call | flops 2097152 | bytes 1048576 | tf_op jit(solution)/shard_map/attend1_keep_send/pallas_call | solution.py:211
  17.7 1.3 %collective-permute-done.1.refs_1_ = bf16[512,512]{1,0:T(8,128)(2,1)S(1)} collective-permute-done((bf16[512,512]{1,0:T(8,128)(2,1)}, bf16[512,512]{1,0:T(8,128)(2,1)S(1)}, u32[]{:S(2)}, u32[]{:S(2)}) %collective-permute-start.1) | collective-permute-done | bytes 524320 | tf_op jit(solution)/shard_map/ppermute | solution.py:326
  19.0 2.5 %collective-permute-done.2.refs_2_ = bf16[512,512]{1,0:T(8,128)(2,1)} collective-permute-done((bf16[512,512]{1,0:T(8,128)(2,1)}, bf16[512,512]{1,0:T(8,128)(2,1)}, u32[]{:S(2)}, u32[]{:S(2)}) %collective-permute-start.2) | collective-permute-done | bytes 524320 | tf_op jit(solution)/shard_map/ppermute | solution.py:326
  21.5 7.1 %attend2_keep_send.1 = (bf16[4,144,256]{2,1,0:T(8,128)(2,1)S(1)}, bf16[4,144,256]{2,1,0:T(8,128)(2,1)S(1)}) custom-call(bf16[4,1024,256]{2,1,0:T(8,128)(2,1)S(1)} %query.1.refs_0_, bf16[512,512]{1,0:T(8,128)(2,1)S(1)} %collective-permute-done.1.refs_1_, bf16[512,512]{1,0:T(8,128)(2,1)} %collective-permute-done.2.refs_2_, ...), custom_call_target="tpu_custom_call" | custom-call | flops 4194304 | bytes 1048576 | tf_op jit(solution)/shard_map/attend2_keep_send/pallas_call | solution.py:211
  28.6 1.6 %collective-permute-done.3.refs_3_ = bf16[4,144,256]{2,1,0:T(8,128)(2,1)S(1)} collective-permute-done((bf16[4,144,256]{2,1,0:T(8,128)(2,1)S(1)}, bf16[4,144,256]{2,1,0:T(8,128)(2,1)S(1)}, u32[]{:S(2)}, u32[]{:S(2)}) %collective-permute-start.3) | collective-permute-done | bytes 294944 | tf_op jit(solution)/shard_map/ppermute | solution.py:326
  30.7 0.9 %collective-permute-done.4.refs_1_ = bf16[512,512]{1,0:T(8,128)(2,1)S(1)} collective-permute-done((bf16[512,512]{1,0:T(8,128)(2,1)S(1)}, bf16[512,512]{1,0:T(8,128)(2,1)S(1)}, u32[]{:S(2)}, u32[]{:S(2)}) %collective-permute-start.4) | collective-permute-done | bytes 524320 | tf_op jit(solution)/shard_map/ppermute | solution.py:326
  31.6 1.9 %attend1_send.1 = bf16[4,144,256]{2,1,0:T(8,128)(2,1)S(1)} custom-call(bf16[4,1024,256]{2,1,0:T(8,128)(2,1)S(1)} %query.1.refs_0_, bf16[512,512]{1,0:T(8,128)(2,1)S(1)} %collective-permute-done.4.refs_1_, s32[1,512]{1,0:T(1,128)S(1)} %get-tuple-element.51.refs_2_), custom_call_target="tpu_custom_call" | custom-call | flops 1048576 | bytes 1048576 | tf_op jit(solution)/shard_map/attend1_send/pallas_call | solution.py:211
  33.6 1.9 %attend1_keep.1.refs_2_ = bf16[4,144,256]{2,1,0:T(8,128)(2,1)S(1)} custom-call(bf16[4,1024,256]{2,1,0:T(8,128)(2,1)S(1)} %query.1.refs_0_, bf16[512,512]{1,0:T(8,128)(2,1)S(1)} %collective-permute-done.4.refs_1_, s32[1,512]{1,0:T(1,128)S(1)} %get-tuple-element.51.refs_2_), custom_call_target="tpu_custom_call" | custom-call | flops 1048576 | bytes 1048576 | tf_op jit(solution)/shard_map/attend1_keep/pallas_call | solution.py:211
  36.0 1.7 %collective-permute-start.6 = (bf16[144,256]{1,0:T(8,128)(2,1)S(1)}, bf16[144,256]{1,0:T(8,128)(2,1)S(1)}, u32[]{:S(2)}, u32[]{:S(2)}) collective-permute-start(bf16[144,256]{1,0:T(8,128)(2,1)S(1)} %get-tuple-element.44), channel_id=1, source_target_pairs={{0,8},{1,9},{2,10},{3,11},{4,12},{5,13},{6,14},{7,15},{8,0},{9,1},... | collective-permute-start | bytes 221192 | tf_op jit(solution)/shard_map/ppermute | solution.py:326
  37.6 2.6 %collective-permute-start.7 = (bf16[144,256]{1,0:T(8,128)(2,1)S(1)}, bf16[144,256]{1,0:T(8,128)(2,1)S(1)}, u32[]{:S(2)}, u32[]{:S(2)}) collective-permute-start(bf16[144,256]{1,0:T(8,128)(2,1)S(1)} %get-tuple-element.45), channel_id=1, source_target_pairs={{0,16},{1,17},{2,18},{3,19},{4,20},{5,21},{6,22},{7,23},{8,24},{9,... | collective-permute-start | bytes 221192 | tf_op jit(solution)/shard_map/ppermute | solution.py:326
  40.7 5.9 %collective-permute-done.7.m2 = bf16[144,256]{1,0:T(8,128)(2,1)S(1)} collective-permute-done((bf16[144,256]{1,0:T(8,128)(2,1)S(1)}, bf16[144,256]{1,0:T(8,128)(2,1)S(1)}, u32[]{:S(2)}, u32[]{:S(2)}) %collective-permute-start.7) | collective-permute-done | bytes 73760 | tf_op jit(solution)/shard_map/ppermute | solution.py:326
  46.6 0.5 out_project.1
  47.1 1.6 %collective-permute-start.10 = (bf16[128,256]{1,0:T(8,128)(2,1)S(1)}, bf16[128,256]{1,0:T(8,128)(2,1)S(1)}, u32[]{:S(2)}, u32[]{:S(2)}) collective-permute-start(bf16[128,256]{1,0:T(8,128)(2,1)S(1)} %get-tuple-element.49), channel_id=1, source_target_pairs={{0,2},{1,3},{2,0},{3,1},{4,6},{5,7},{6,4},{7,5},{8,10},{9,11},{10,... | collective-permute-start | bytes 196616 | tf_op jit(solution)/shard_map/ppermute | solution.py:326
  48.7 1.4 %collective-permute-start.11 = (bf16[128,256]{1,0:T(8,128)(2,1)S(1)}, bf16[128,256]{1,0:T(8,128)(2,1)S(1)}, u32[]{:S(2)}, u32[]{:S(2)}) collective-permute-start(bf16[128,256]{1,0:T(8,128)(2,1)S(1)} %get-tuple-element.50), channel_id=1, source_target_pairs={{0,3},{1,2},{2,1},{3,0},{4,7},{5,6},{6,5},{7,4},{8,11},{9,10},{10,... | collective-permute-start | bytes 196616 | tf_op jit(solution)/shard_map/ppermute | solution.py:326
  50.1 0.5 collective-permute-start.9
  50.7 1.2 %collective-permute-done.10 = bf16[128,256]{1,0:T(8,128)(2,1)S(1)} collective-permute-done((bf16[128,256]{1,0:T(8,128)(2,1)S(1)}, bf16[128,256]{1,0:T(8,128)(2,1)S(1)}, u32[]{:S(2)}, u32[]{:S(2)}) %collective-permute-start.10) | collective-permute-done | bytes 65568 | tf_op jit(solution)/shard_map/ppermute | solution.py:326
  51.9 2.0 %collective-permute-done.11 = bf16[128,256]{1,0:T(8,128)(2,1)S(1)} collective-permute-done((bf16[128,256]{1,0:T(8,128)(2,1)S(1)}, bf16[128,256]{1,0:T(8,128)(2,1)S(1)}, u32[]{:S(2)}, u32[]{:S(2)}) %collective-permute-start.11) | collective-permute-done | bytes 65568 | tf_op jit(solution)/shard_map/ppermute | solution.py:326
  53.9 0.5 collective-permute-done.9
  54.4 0.7 %add_convert_fusion = bf16[128,256]{1,0:T(8,128)(2,1)} fusion(bf16[128,256]{1,0:T(8,128)(2,1)S(1)} %collective-permute-done.11, bf16[128,256]{1,0:T(8,128)(2,1)S(1)} %collective-permute-done.10, f32[128,256]{1,0:T(8,128)S(1)} %get-tuple-element.47, bf16[128,256]{1,0:T(8,128)(2,1)S(1)} %collective-permute-done.9), kind=kLoop, calls=%fused_computation | loop fusion | flops 229376 | bytes 393216 | tf_op jit(solution)/shard_map/convert_element_type | solution.py:366
  (24 shorter events, 1.7 us)
Async XLA Ops:
  3.8 15.2 %collective-permute-start.1 = (bf16[512,512]{1,0:T(8,128)(2,1)}, bf16[512,512]{1,0:T(8,128)(2,1)S(1)}, u32[]{:S(2)}, u32[]{:S(2)}) collective-permute-start(bf16[512,512]{1,0:T(8,128)(2,1)} %get-tuple-element.34), channel_id=1, source_target_pairs={{0,2},{1,3},{2,0},{3,1},{4,6},{5,7},{6,4},{7,5},{8,10},{9,11},{10,... | collective-permute-start | bytes 1572872 | tf_op jit(solution)/shard_map/ppermute | solution.py:326
  6.8 14.7 %collective-permute-start.2 = (bf16[512,512]{1,0:T(8,128)(2,1)}, bf16[512,512]{1,0:T(8,128)(2,1)}, u32[]{:S(2)}, u32[]{:S(2)}) collective-permute-start(bf16[512,512]{1,0:T(8,128)(2,1)} %get-tuple-element.35), channel_id=1, source_target_pairs={{0,1},{1,0},{2,3},{3,2},{4,5},{5,4},{6,7},{7,6},{8,9},{9,8},{10,11... | collective-permute-start | bytes 1572872 | tf_op jit(solution)/shard_map/ppermute | solution.py:326
  8.3 4.0 %copy-start = (bf16[1024,1024]{1,0:T(8,128)(2,1)S(1)}, bf16[1024,1024]{1,0:T(8,128)(2,1)}, u32[]{:S(2)}) copy-start(bf16[1024,1024]{1,0:T(8,128)(2,1)} %slots_ref.1) | copy-start | bytes 6291460
  8.3 4.0 %copy-start.1 = (bf16[1024,256]{1,0:T(8,128)(2,1)S(1)}, bf16[1024,256]{1,0:T(8,128)(2,1)}, u32[]{:S(2)}) copy-start(bf16[1024,256]{1,0:T(8,128)(2,1)} %q_ref.1) | copy-start | bytes 1572868
  12.3 2.0 %copy-start.4 = (s32[2048]{0:T(1024)S(1)}, s32[2048]{0:T(1024)}, u32[]{:S(2)}) copy-start(s32[2048]{0:T(1024)} %param.9) | copy-start | bytes 24580
  12.3 2.0 %copy-start.3 = (bf16[512,512]{1,0:T(8,128)(2,1)S(1)}, bf16[512,512]{1,0:T(8,128)(2,1)}, u32[]{:S(2)}) copy-start(bf16[512,512]{1,0:T(8,128)(2,1)} %get-tuple-element.29.refs_1_) | copy-start | bytes 1572868
  14.3 3.2 %copy-start.5 = (bf16[512,512]{1,0:T(8,128)(2,1)S(1)}, bf16[512,512]{1,0:T(8,128)(2,1)}, u32[]{:S(2)}) copy-start(bf16[512,512]{1,0:T(8,128)(2,1)} %get-tuple-element.42) | copy-start | bytes 1572868
  17.5 14.1 %collective-permute-start.4 = (bf16[512,512]{1,0:T(8,128)(2,1)S(1)}, bf16[512,512]{1,0:T(8,128)(2,1)S(1)}, u32[]{:S(2)}, u32[]{:S(2)}) collective-permute-start(bf16[512,512]{1,0:T(8,128)(2,1)S(1)} %copy-done.5), channel_id=1, source_target_pairs={{0,3},{1,2},{2,1},{3,0},{4,7},{5,6},{6,5},{7,4},{8,11},{9,10},{10,... | collective-permute-start | bytes 1572872 | tf_op jit(solution)/shard_map/ppermute | solution.py:326
  17.6 11.0 %collective-permute-start = (bf16[4,144,256]{2,1,0:T(8,128)(2,1)S(1)}, bf16[4,144,256]{2,1,0:T(8,128)(2,1)S(1)}, u32[]{:S(2)}, u32[]{:S(2)}) collective-permute-start(bf16[4,144,256]{2,1,0:T(8,128)(2,1)S(1)} %get-tuple-element.33), channel_id=1, source_target_pairs={{0,4},{1,5},{2,6},{3,7},{4,0},{5,1},{6,2},{7,3},{8,12},{9,13},{10,... | collective-permute-start | bytes 884744 | tf_op jit(solution)/shard_map/ppermute | solution.py:326
  28.6 1.6 %collective-permute-start.3 = (bf16[4,144,256]{2,1,0:T(8,128)(2,1)S(1)}, bf16[4,144,256]{2,1,0:T(8,128)(2,1)S(1)}, u32[]{:S(2)}, u32[]{:S(2)}) collective-permute-start(bf16[4,144,256]{2,1,0:T(8,128)(2,1)S(1)} %get-tuple-element.39), channel_id=1, source_target_pairs={{0,4},{1,5},{2,6},{3,7},{4,0},{5,1},{6,2},{7,3},{8,12},{9,13},{10,... | collective-permute-start | bytes 884744 | tf_op jit(solution)/shard_map/ppermute | solution.py:326
  33.5 13.0 %copy-start.2 = (bf16[256,1024]{1,0:T(8,128)(2,1)S(1)}, bf16[256,1024]{1,0:T(8,128)(2,1)}, u32[]{:S(2)}) copy-start(bf16[256,1024]{1,0:T(8,128)(2,1)} %o_ref.1) | copy-start | bytes 1572868
  33.5 2.0 %collective-permute-start.5 = (bf16[4,144,256]{2,1,0:T(8,128)(2,1)S(1)}, bf16[4,144,256]{2,1,0:T(8,128)(2,1)S(1)}, u32[]{:S(2)}, u32[]{:S(2)}) collective-permute-start(bf16[4,144,256]{2,1,0:T(8,128)(2,1)S(1)} %attend1_send.1), channel_id=1, source_target_pairs={{0,4},{1,5},{2,6},{3,7},{4,0},{5,1},{6,2},{7,3},{8,12},{9,13},{10,... | collective-permute-start | bytes 884744 | tf_op jit(solution)/shard_map/ppermute | solution.py:326
  36.0 4.7 %collective-permute-start.6 = (bf16[144,256]{1,0:T(8,128)(2,1)S(1)}, bf16[144,256]{1,0:T(8,128)(2,1)S(1)}, u32[]{:S(2)}, u32[]{:S(2)}) collective-permute-start(bf16[144,256]{1,0:T(8,128)(2,1)S(1)} %get-tuple-element.44), channel_id=1, source_target_pairs={{0,8},{1,9},{2,10},{3,11},{4,12},{5,13},{6,14},{7,15},{8,0},{9,1},... | collective-permute-start | bytes 221192 | tf_op jit(solution)/shard_map/ppermute | solution.py:326
  37.6 8.9 %collective-permute-start.7 = (bf16[144,256]{1,0:T(8,128)(2,1)S(1)}, bf16[144,256]{1,0:T(8,128)(2,1)S(1)}, u32[]{:S(2)}, u32[]{:S(2)}) collective-permute-start(bf16[144,256]{1,0:T(8,128)(2,1)S(1)} %get-tuple-element.45), channel_id=1, source_target_pairs={{0,16},{1,17},{2,18},{3,19},{4,20},{5,21},{6,22},{7,23},{8,24},{9,... | collective-permute-start | bytes 221192 | tf_op jit(solution)/shard_map/ppermute | solution.py:326
  40.2 6.3 %collective-permute-start.8 = (bf16[144,256]{1,0:T(8,128)(2,1)S(1)}, bf16[144,256]{1,0:T(8,128)(2,1)S(1)}, u32[]{:S(2)}, u32[]{:S(2)}) collective-permute-start(bf16[144,256]{1,0:T(8,128)(2,1)S(1)} %get-tuple-element.46), channel_id=1, source_target_pairs={{0,24},{1,25},{2,26},{3,27},{4,28},{5,29},{6,30},{7,31},{8,16},{9,... | collective-permute-start | bytes 221192 | tf_op jit(solution)/shard_map/ppermute | solution.py:326
  47.1 4.8 %collective-permute-start.10 = (bf16[128,256]{1,0:T(8,128)(2,1)S(1)}, bf16[128,256]{1,0:T(8,128)(2,1)S(1)}, u32[]{:S(2)}, u32[]{:S(2)}) collective-permute-start(bf16[128,256]{1,0:T(8,128)(2,1)S(1)} %get-tuple-element.49), channel_id=1, source_target_pairs={{0,2},{1,3},{2,0},{3,1},{4,6},{5,7},{6,4},{7,5},{8,10},{9,11},{10,... | collective-permute-start | bytes 196616 | tf_op jit(solution)/shard_map/ppermute | solution.py:326
  48.7 5.2 %collective-permute-start.11 = (bf16[128,256]{1,0:T(8,128)(2,1)S(1)}, bf16[128,256]{1,0:T(8,128)(2,1)S(1)}, u32[]{:S(2)}, u32[]{:S(2)}) collective-permute-start(bf16[128,256]{1,0:T(8,128)(2,1)S(1)} %get-tuple-element.50), channel_id=1, source_target_pairs={{0,3},{1,2},{2,1},{3,0},{4,7},{5,6},{6,5},{7,4},{8,11},{9,10},{10,... | collective-permute-start | bytes 196616 | tf_op jit(solution)/shard_map/ppermute | solution.py:326
  50.1 4.3 %collective-permute-start.9 = (bf16[128,256]{1,0:T(8,128)(2,1)S(1)}, bf16[128,256]{1,0:T(8,128)(2,1)S(1)}, u32[]{:S(2)}, u32[]{:S(2)}) collective-permute-start(bf16[128,256]{1,0:T(8,128)(2,1)S(1)} %get-tuple-element.48), channel_id=1, source_target_pairs={{0,1},{1,0},{2,3},{3,2},{4,5},{5,4},{6,7},{7,6},{8,9},{9,8},{10,11... | collective-permute-start | bytes 196616 | tf_op jit(solution)/shard_map/ppermute | solution.py:326

commit v5 on v4

--- a/solution.py
+++ b/solution.py
@@ -17,7 +17,7 @@
 AXES = ("hit", "head")
 VMEM = pl.BlockSpec(memory_space=pltpu.VMEM)
 HBM = pl.BlockSpec(memory_space=pltpu.HBM)
-PARAMS = pltpu.CompilerParams(vmem_limit_bytes=40 << 20)
+PARAMS = pltpu.CompilerParams(vmem_limit_bytes=24 << 20)
 
 
 def mul(left, right, dims=NN):
@@ -38,14 +38,15 @@
 
 
 def project_kernel(flips, hits_ref, k_ref, v_ref, *refs):
-    outs = refs[: -len(PROJECT_SCRATCH)]
-    hits_here, weights, in_sems = refs[-len(PROJECT_SCRATCH) :]
+    outs = refs[: len(flips)]
+    hits_here, weights, both, in_sems, out_sems = refs[len(flips) :]
     width = weights.shape[2] // 2
     hits_copy = pltpu.make_async_copy(hits_ref, hits_here, in_sems.at[0, 0])
     hits_copy.start()
     copies = []
-    for at, (flip, _) in enumerate(flips):
-        columns = pl.ds(pl.multiple_of((lax.axis_index("head") ^ flip) * width, width), width)
+    for at, flip in enumerate(flips):
+        start = (lax.axis_index("head") ^ flip) * width
+        columns = pl.ds(pl.multiple_of(start, width), width)
         for side, source in enumerate((k_ref, v_ref)):
             target = weights.at[at, :, pl.ds(side * width, width)]
             copies.append(
@@ -53,41 +54,38 @@
             )
             copies[-1].start()
     hits_copy.wait()
-    place = 0
-    for at, (_, pieces) in enumerate(flips):
+    leaving = []
+    for at in range(len(flips)):
         copies[2 * at].wait()
         copies[2 * at + 1].wait()
-        both = mul(hits_here[...], weights[at]).astype(BF16)
-        rows = both.shape[0] // pieces
-        for piece in range(pieces):
-            outs[place][...] = both[piece * rows : (piece + 1) * rows]
-            place += 1
-
-
-PROJECT_SCRATCH = ("hits", "weights", "in")
+        block = mul(hits_here[...], weights[at]).astype(BF16)
+        both[at] = block
+        leaving.append(pltpu.make_async_copy(both.at[at], outs[at], out_sems.at[at]))
+        leaving[-1].start()
+    for copy in leaving:
+        copy.wait()
 
 
 def project(flips, hits, k_weight, v_weight, width):
     rows, depth = hits.shape
     count = len(flips)
-    shapes = [struct((rows // pieces, 2 * width)) for _, pieces in flips for _ in range(pieces)]
+    block = (rows, 2 * width)
     outs = pl.pallas_call(
         functools.partial(project_kernel, flips),
         in_specs=[HBM, HBM, HBM],
-        out_specs=[VMEM] * len(shapes),
-        out_shape=shapes,
+        out_specs=[HBM] * count,
+        out_shape=[struct(block)] * count,
         scratch_shapes=[
             pltpu.VMEM((rows, depth), BF16),
             pltpu.VMEM((count, depth, 2 * width), BF16),
+            pltpu.VMEM((count, *block), BF16),
             pltpu.SemaphoreType.DMA((count + 1, 2)),
+            pltpu.SemaphoreType.DMA((count,)),
         ],
         compiler_params=pltpu.CompilerParams(vmem_limit_bytes=58 << 20),
-        name="project" + "".join(str(flip) for flip, _ in flips),
+        name="project" + "".join(map(str, flips)),
     )(hits, k_weight, v_weight)
-    taken = {}
-    for flip, pieces in flips:
-        taken[flip], outs = outs[:pieces], outs[pieces:]
-    return taken
+    return dict(zip(flips, outs))
 
 
 def query_kernel(slots_ref, q_ref, out_ref):
@@ -124,18 +122,12 @@
     )(slots, q_weight)
 
 
-def attend_kernel(count, sides, *refs):
-    q_ref = refs[0]
-    kv_refs = refs[1 : 1 + count]
-    mask_refs = refs[1 + count : 1 + 2 * count]
-    targets = refs[1 + 2 * count : -2]
-    ke_ref, ve_ref = refs[-2:]
-    heads = q_ref.shape[0]
-    pairs = heads // 2
+def extend(kv_refs, mask_refs, ke_ref, ve_ref):
+    pairs = ve_ref.shape[0]
     hits = kv_refs[0].shape[0]
     lane = lax.broadcasted_iota(jnp.int32, (hits, 128), 1)
     low = lane < HEAD_DIM
-    for at in range(count):
+    for at in range(len(kv_refs)):
         rows = pl.ds(at * hits, hits)
         off = jnp.where(mask_refs[at][...] > 0, 0.0, -1e30)
         column = jnp.broadcast_to(off, (128, hits)).T
@@ -150,6 +142,19 @@
             start = (pairs + pair) * 128
             ve_ref[pair, rows, :128] = kv_refs[at][:, start : start + 128]
             ve_ref[pair, rows, 128:] = jnp.ones((hits, 128), BF16)
+
+
+def attend_kernel(count, sides, given, *refs):
+    q_ref = refs[0]
+    heads = q_ref.shape[0]
+    pairs = heads // 2
+    if given:
+        ke_ref, ve_ref, *targets = refs[1:]
+    else:
+        kv_refs = refs[1 : 1 + count]
+        mask_refs = refs[1 + count : 1 + 2 * count]
+        *targets, ke_ref, ve_ref = refs[1 + 2 * count :]
+        extend(kv_refs, mask_refs, ke_ref, ve_ref)
     core = lax.axis_index("hit") % 2
     blocks = targets[0].shape[0]
     half = targets[0].shape[1] - 4 * heads
@@ -201,26 +206,31 @@
     return top, total
 
 
-def attend(queries, sources, masks, sides=("keep", "send")):
+def attend(queries, sources, masks, sides=("keep", "send"), given=(), give=False):
     heads, slots, _ = queries.shape
     count = len(sources)
-    hits = sources[0].shape[0]
-    half = slots // (lax.axis_size("hit"))
+    half = slots // lax.axis_size("hit")
     message = struct((lax.axis_size("hit") // 2, half + 4 * heads, heads * HEAD_DIM))
-    scores = heads * slots * count * hits * len(sides) // 2
+    outs = [message] * len(sides)
+    scratch = []
+    if not given:
+        hits = sum(source.shape[0] for source in sources)
+        scratch = [pltpu.VMEM((heads, hits, 256), BF16), pltpu.VMEM((heads // 2, hits, 256), BF16)]
+    if give:
+        outs, scratch = outs + scratch, []
+    operands = given if given else (*sources, *masks)
     return pl.pallas_call(
-        functools.partial(attend_kernel, count, sides),
-        in_specs=[VMEM] * (1 + 2 * count),
-        out_specs=[VMEM] * len(sides),
-        out_shape=[message] * len(sides),
-        scratch_shapes=[
-            pltpu.VMEM((heads, count * hits, 256), BF16),
-            pltpu.VMEM((heads // 2, count * hits, 256), BF16),
-        ],
+        functools.partial(attend_kernel, count, sides, bool(given)),
+        in_specs=[VMEM] * (1 + len(operands)),
+        out_specs=[VMEM] * len(outs),
+        out_shape=outs,
+        scratch_shapes=scratch,
         compiler_params=PARAMS,
-        cost_estimate=pl.CostEstimate(flops=scores, bytes_accessed=1 << 20, transcendentals=0),
+        cost_estimate=pl.CostEstimate(
+            flops=heads * slots * 1024, bytes_accessed=1 << 20, transcendentals=0
+        ),
         name=f"attend{count}_" + "_".join(sides),
-    )(queries, *sources, *masks)
+    )(queries, *operands)
 
 
 def spread(count, heads):
@@ -336,12 +346,12 @@
         return lax.dynamic_index_in_dim(masks, head ^ flip, 0, keepdims=False)
 
     ours = {}
-    for flips in (((1, 1), (2, 1)), ((3, 1), (0, 1))):
+    for flips in ((1, 2), (3, 0)):
         ours.update(project(flips, hits, k_weight, v_weight, width))
     queries = query(slots, q_weight)
-    theirs = {flip: move(ours[flip][0], 0, flip) for flip in (1, 2)}
-    mine = attend(queries, ours[0], [mask_of(0)])
-    later = list(ours[3])
+    theirs = {flip: move(ours[flip], 0, flip) for flip in (1, 2)}
+    mine = attend(queries, [ours[0]], [mask_of(0)])
+    later = [ours[3]]
     later[0], mine = lax.optimization_barrier((later[0], mine))
     later = [move(piece, 0, 3) for piece in later]
     theirs[2], theirs[1] = lax.optimization_barrier((theirs[2], theirs[1]))
@@ -354,9 +364,9 @@
     for at, piece in enumerate(later):
         size = piece.shape[0]
         mask = mask_of(3)[:, at * size : (at + 1) * size]
-        (sent,) = attend(queries, [piece], [mask], ("send",))
+        sent, *rows = attend(queries, [piece], [mask], ("send",), give=True)
         parts.append(move(sent, 1, 0))
-        parts += attend(queries, [piece], [mask], ("keep",))
+        parts += attend(queries, (), (), ("keep",), given=rows)
     parts = core_join(parts, heads)
     messages = [parts[0]] + [move(parts[flip], 2 * flip, 0) for flip in (1, 2, 3)]
     shares = out_project(o_weight, messages, heads)

time: 55.2 us -> 55.1 us (level)
  transfers between devices with their start and end apart: 12 -> 12, of which waited for: 9 -> 9; matrix products, arithmetic and copies ran while one was open for 0% -> 0% of each run, Pallas kernels for 34% -> 33%
where the time goes in v5:
time: 55.1 us; the launch traced here: 54.9 us
  Pallas kernels  24.9 us (45%)
  waiting for transfers between devices  16.3 us (30%)
  starting transfers between devices  12.8 us (23%)
  other arithmetic  0.66 us (1%)
    ppermute x12, waiting for transfers between devices, move(): return lax.ppermute(value, AXES, pairs)  16.3 us
    pallas_call x4, Pallas kernels, attend(): pl.pallas_call(functools.partial(attend_kernel, count, sides, bool(given)...  13.7 us
    ppermute x12, starting transfers between devices, move(): return lax.ppermute(value, AXES, pairs)  12.8 us
    pallas_call x2, Pallas kernels, project(): pl.pallas_call(functools.partial(project_kernel, flips), in_specs=[HBM, H...  7.76 us
    pallas_call x1, Pallas kernels, query(): pl.pallas_call(query_kernel, grid=(rows // block,), in_specs=[pl.BlockSpe...  1.95 us
  transfers between devices with their start and end apart: 12, of which 9 were waited for; matrix products, arithmetic and copies ran while one was open for 0% of the time, Pallas kernels for 33%

profile of v5, /device:TPU:0, one launch (start us, length us, event | category | flops | bytes accessed | tf_op | source)
XLA Modules:
  0.0 54.9 jit_solution(12717322056312621149)
XLA Ops:
  0.0 3.8 %project12.1 = (bf16[512,512]{1,0:T(8,128)(2,1)}, bf16[512,512]{1,0:T(8,128)(2,1)}) custom-call(bf16[512,1024]{1,0:T(8,128)(2,1)} %hits_ref.3, bf16[1024,1024]{1,0:T(8,128)(2,1)} %k_ref.3, bf16[1024,1024]{1,0:T(8,128)(2,1)} %v_ref.3), custom_call_target="tpu_custom_call" | custom-call | tf_op jit(solution)/shard_map/project12/pallas_call | solution.py:73
  3.8 3.0 %collective-permute-start.1 = (bf16[512,512]{1,0:T(8,128)(2,1)}, bf16[512,512]{1,0:T(8,128)(2,1)S(1)}, u32[]{:S(2)}, u32[]{:S(2)}) collective-permute-start(bf16[512,512]{1,0:T(8,128)(2,1)} %get-tuple-element.37), channel_id=1, source_target_pairs={{0,2},{1,3},{2,0},{3,1},{4,6},{5,7},{6,4},{7,5},{8,10},{9,11},{10,... | collective-permute-start | bytes 1572872 | tf_op jit(solution)/shard_map/ppermute | solution.py:336
  6.9 1.5 %collective-permute-start.2 = (bf16[512,512]{1,0:T(8,128)(2,1)}, bf16[512,512]{1,0:T(8,128)(2,1)}, u32[]{:S(2)}, u32[]{:S(2)}) collective-permute-start(bf16[512,512]{1,0:T(8,128)(2,1)} %get-tuple-element.38), channel_id=1, source_target_pairs={{0,1},{1,0},{2,3},{3,2},{4,5},{5,4},{6,7},{7,6},{8,9},{9,8},{10,11... | collective-permute-start | bytes 1572872 | tf_op jit(solution)/shard_map/ppermute | solution.py:336
  8.3 4.0 %project30.1 = (bf16[512,512]{1,0:T(8,128)(2,1)}, bf16[512,512]{1,0:T(8,128)(2,1)}) custom-call(bf16[512,1024]{1,0:T(8,128)(2,1)} %hits_ref.3, bf16[1024,1024]{1,0:T(8,128)(2,1)} %k_ref.3, bf16[1024,1024]{1,0:T(8,128)(2,1)} %v_ref.3), custom_call_target="tpu_custom_call" | custom-call | tf_op jit(solution)/shard_map/project30/pallas_call | solution.py:73
  12.4 2.0 %query.1.refs_0_ = bf16[4,1024,256]{2,1,0:T(8,128)(2,1)S(1)} custom-call(bf16[1024,1024]{1,0:T(8,128)(2,1)S(1)} %copy-done, bf16[1024,256]{1,0:T(8,128)(2,1)S(1)} %copy-done.1), custom_call_target="tpu_custom_call" | custom-call | tf_op jit(solution)/shard_map/query/pallas_call | solution.py:111
  14.4 3.1 %attend1_keep_send.1 = (bf16[4,144,256]{2,1,0:T(8,128)(2,1)S(1)}, bf16[4,144,256]{2,1,0:T(8,128)(2,1)S(1)}) custom-call(bf16[4,1024,256]{2,1,0:T(8,128)(2,1)S(1)} %query.1.refs_0_, bf16[512,512]{1,0:T(8,128)(2,1)S(1)} %copy-done.3, s32[1,512]{1,0:T(1,128)S(1)} %get-tuple-element.60.refs_2_), custom_call_target="tpu_custom_call" | custom-call | flops 4194304 | bytes 1048576 | tf_op jit(solution)/shard_map/attend1_keep_send/pallas_call | solution.py:222
  17.6 1.3 %collective-permute-done.1.refs_1_ = bf16[512,512]{1,0:T(8,128)(2,1)S(1)} collective-permute-done((bf16[512,512]{1,0:T(8,128)(2,1)}, bf16[512,512]{1,0:T(8,128)(2,1)S(1)}, u32[]{:S(2)}, u32[]{:S(2)}) %collective-permute-start.1) | collective-permute-done | bytes 524320 | tf_op jit(solution)/shard_map/ppermute | solution.py:336
  19.0 2.6 %collective-permute-done.2.refs_2_ = bf16[512,512]{1,0:T(8,128)(2,1)} collective-permute-done((bf16[512,512]{1,0:T(8,128)(2,1)}, bf16[512,512]{1,0:T(8,128)(2,1)}, u32[]{:S(2)}, u32[]{:S(2)}) %collective-permute-start.2) | collective-permute-done | bytes 524320 | tf_op jit(solution)/shard_map/ppermute | solution.py:336
  21.6 6.9 %attend2_keep_send.1 = (bf16[4,144,256]{2,1,0:T(8,128)(2,1)S(1)}, bf16[4,144,256]{2,1,0:T(8,128)(2,1)S(1)}) custom-call(bf16[4,1024,256]{2,1,0:T(8,128)(2,1)S(1)} %query.1.refs_0_, bf16[512,512]{1,0:T(8,128)(2,1)S(1)} %collective-permute-done.1.refs_1_, bf16[512,512]{1,0:T(8,128)(2,1)} %collective-permute-done.2.refs_2_, ...), custom_call_target="tpu_custom_call" | custom-call | flops 4194304 | bytes 1048576 | tf_op jit(solution)/shard_map/attend2_keep_send/pallas_call | solution.py:222
  28.6 1.6 %collective-permute-done.3.refs_3_ = bf16[4,144,256]{2,1,0:T(8,128)(2,1)S(1)} collective-permute-done((bf16[4,144,256]{2,1,0:T(8,128)(2,1)S(1)}, bf16[4,144,256]{2,1,0:T(8,128)(2,1)S(1)}, u32[]{:S(2)}, u32[]{:S(2)}) %collective-permute-start.3) | collective-permute-done | bytes 294944 | tf_op jit(solution)/shard_map/ppermute | solution.py:336
  30.6 0.9 %collective-permute-done.4.refs_1_ = bf16[512,512]{1,0:T(8,128)(2,1)S(1)} collective-permute-done((bf16[512,512]{1,0:T(8,128)(2,1)S(1)}, bf16[512,512]{1,0:T(8,128)(2,1)S(1)}, u32[]{:S(2)}, u32[]{:S(2)}) %collective-permute-start.4) | collective-permute-done | bytes 524320 | tf_op jit(solution)/shard_map/ppermute | solution.py:336
  31.6 2.0 %attend1_send.1 = (bf16[4,144,256]{2,1,0:T(8,128)(2,1)S(1)}, bf16[4,512,256]{2,1,0:T(8,128)(2,1)S(1)}, bf16[2,512,256]{2,1,0:T(8,128)(2,1)S(1)}) custom-call(bf16[4,1024,256]{2,1,0:T(8,128)(2,1)S(1)} %query.1.refs_0_, bf16[512,512]{1,0:T(8,128)(2,1)S(1)} %collective-permute-done.4.refs_1_, s32[1,512]{1,0:T(1,128)S(1)} %get-tuple-element.57.refs_2_), custom_call_target="tpu_custom_call" | custom-call | flops 4194304 | bytes 1048576 | tf_op jit(solution)/shard_map/attend1_send/pallas_call | solution.py:222
  33.6 1.7 %attend0_keep.1.refs_2_ = bf16[4,144,256]{2,1,0:T(8,128)(2,1)S(1)} custom-call(bf16[4,1024,256]{2,1,0:T(8,128)(2,1)S(1)} %query.1.refs_0_, bf16[4,512,256]{2,1,0:T(8,128)(2,1)S(1)} %get-tuple-element.47.refs_1_, bf16[2,512,256]{2,1,0:T(8,128)(2,1)S(1)} %get-tuple-element.48.refs_2_), custom_call_target="tpu_custom_call" | custom-call | flops 4194304 | bytes 1048576 | tf_op jit(solution)/shard_map/attend0_keep/pallas_call | solution.py:222
  35.8 1.7 %collective-permute-start.6 = (bf16[144,256]{1,0:T(8,128)(2,1)S(1)}, bf16[144,256]{1,0:T(8,128)(2,1)S(1)}, u32[]{:S(2)}, u32[]{:S(2)}) collective-permute-start(bf16[144,256]{1,0:T(8,128)(2,1)S(1)} %get-tuple-element.50), channel_id=1, source_target_pairs={{0,8},{1,9},{2,10},{3,11},{4,12},{5,13},{6,14},{7,15},{8,0},{9,1},... | collective-permute-start | bytes 221192 | tf_op jit(solution)/shard_map/ppermute | solution.py:336
  37.5 2.6 %collective-permute-start.7 = (bf16[144,256]{1,0:T(8,128)(2,1)S(1)}, bf16[144,256]{1,0:T(8,128)(2,1)S(1)}, u32[]{:S(2)}, u32[]{:S(2)}) collective-permute-start(bf16[144,256]{1,0:T(8,128)(2,1)S(1)} %get-tuple-element.51), channel_id=1, source_target_pairs={{0,16},{1,17},{2,18},{3,19},{4,20},{5,21},{6,22},{7,23},{8,24},{9,... | collective-permute-start | bytes 221192 | tf_op jit(solution)/shard_map/ppermute | solution.py:336
  40.5 5.9 %collective-permute-done.7.m2 = bf16[144,256]{1,0:T(8,128)(2,1)S(1)} collective-permute-done((bf16[144,256]{1,0:T(8,128)(2,1)S(1)}, bf16[144,256]{1,0:T(8,128)(2,1)S(1)}, u32[]{:S(2)}, u32[]{:S(2)}) %collective-permute-start.7) | collective-permute-done | bytes 73760 | tf_op jit(solution)/shard_map/ppermute | solution.py:336
  46.4 0.5 out_project.1
  47.0 1.6 %collective-permute-start.10 = (bf16[128,256]{1,0:T(8,128)(2,1)S(1)}, bf16[128,256]{1,0:T(8,128)(2,1)S(1)}, u32[]{:S(2)}, u32[]{:S(2)}) collective-permute-start(bf16[128,256]{1,0:T(8,128)(2,1)S(1)} %get-tuple-element.55), channel_id=1, source_target_pairs={{0,2},{1,3},{2,0},{3,1},{4,6},{5,7},{6,4},{7,5},{8,10},{9,11},{10,... | collective-permute-start | bytes 196616 | tf_op jit(solution)/shard_map/ppermute | solution.py:336
  48.6 1.4 %collective-permute-start.11 = (bf16[128,256]{1,0:T(8,128)(2,1)S(1)}, bf16[128,256]{1,0:T(8,128)(2,1)S(1)}, u32[]{:S(2)}, u32[]{:S(2)}) collective-permute-start(bf16[128,256]{1,0:T(8,128)(2,1)S(1)} %get-tuple-element.56), channel_id=1, source_target_pairs={{0,3},{1,2},{2,1},{3,0},{4,7},{5,6},{6,5},{7,4},{8,11},{9,10},{10,... | collective-permute-start | bytes 196616 | tf_op jit(solution)/shard_map/ppermute | solution.py:336
  50.0 0.5 collective-permute-start.9
  50.5 1.2 %collective-permute-done.10 = bf16[128,256]{1,0:T(8,128)(2,1)S(1)} collective-permute-done((bf16[128,256]{1,0:T(8,128)(2,1)S(1)}, bf16[128,256]{1,0:T(8,128)(2,1)S(1)}, u32[]{:S(2)}, u32[]{:S(2)}) %collective-permute-start.10) | collective-permute-done | bytes 65568 | tf_op jit(solution)/shard_map/ppermute | solution.py:336
  51.8 2.0 %collective-permute-done.11 = bf16[128,256]{1,0:T(8,128)(2,1)S(1)} collective-permute-done((bf16[128,256]{1,0:T(8,128)(2,1)S(1)}, bf16[128,256]{1,0:T(8,128)(2,1)S(1)}, u32[]{:S(2)}, u32[]{:S(2)}) %collective-permute-start.11) | collective-permute-done | bytes 65568 | tf_op jit(solution)/shard_map/ppermute | solution.py:336
  53.7 0.5 collective-permute-done.9
  54.3 0.7 %add_convert_fusion = bf16[128,256]{1,0:T(8,128)(2,1)} fusion(bf16[128,256]{1,0:T(8,128)(2,1)S(1)} %collective-permute-done.11, bf16[128,256]{1,0:T(8,128)(2,1)S(1)} %collective-permute-done.10, f32[128,256]{1,0:T(8,128)S(1)} %get-tuple-element.53, bf16[128,256]{1,0:T(8,128)(2,1)S(1)} %collective-permute-done.9), kind=kLoop, calls=%fused_computation | loop fusion | flops 229376 | bytes 393216 | tf_op jit(solution)/shard_map/convert_element_type | solution.py:376
  (24 shorter events, 1.7 us)
Async XLA Ops:
  3.8 15.2 %collective-permute-start.1 = (bf16[512,512]{1,0:T(8,128)(2,1)}, bf16[512,512]{1,0:T(8,128)(2,1)S(1)}, u32[]{:S(2)}, u32[]{:S(2)}) collective-permute-start(bf16[512,512]{1,0:T(8,128)(2,1)} %get-tuple-element.37), channel_id=1, source_target_pairs={{0,2},{1,3},{2,0},{3,1},{4,6},{5,7},{6,4},{7,5},{8,10},{9,11},{10,... | collective-permute-start | bytes 1572872 | tf_op jit(solution)/shard_map/ppermute | solution.py:336
  6.9 14.7 %collective-permute-start.2 = (bf16[512,512]{1,0:T(8,128)(2,1)}, bf16[512,512]{1,0:T(8,128)(2,1)}, u32[]{:S(2)}, u32[]{:S(2)}) collective-permute-start(bf16[512,512]{1,0:T(8,128)(2,1)} %get-tuple-element.38), channel_id=1, source_target_pairs={{0,1},{1,0},{2,3},{3,2},{4,5},{5,4},{6,7},{7,6},{8,9},{9,8},{10,11... | collective-permute-start | bytes 1572872 | tf_op jit(solution)/shard_map/ppermute | solution.py:336
  8.3 4.0 %copy-start = (bf16[1024,1024]{1,0:T(8,128)(2,1)S(1)}, bf16[1024,1024]{1,0:T(8,128)(2,1)}, u32[]{:S(2)}) copy-start(bf16[1024,1024]{1,0:T(8,128)(2,1)} %slots_ref.1) | copy-start | bytes 6291460
  8.3 4.0 %copy-start.1 = (bf16[1024,256]{1,0:T(8,128)(2,1)S(1)}, bf16[1024,256]{1,0:T(8,128)(2,1)}, u32[]{:S(2)}) copy-start(bf16[1024,256]{1,0:T(8,128)(2,1)} %q_ref.1) | copy-start | bytes 1572868
  12.3 2.0 %copy-start.4 = (s32[2048]{0:T(1024)S(1)}, s32[2048]{0:T(1024)}, u32[]{:S(2)}) copy-start(s32[2048]{0:T(1024)} %param.9) | copy-start | bytes 24580
  12.4 2.0 %copy-start.3 = (bf16[512,512]{1,0:T(8,128)(2,1)S(1)}, bf16[512,512]{1,0:T(8,128)(2,1)}, u32[]{:S(2)}) copy-start(bf16[512,512]{1,0:T(8,128)(2,1)} %get-tuple-element.32.refs_1_) | copy-start | bytes 1572868
  14.3 3.2 %copy-start.5 = (bf16[512,512]{1,0:T(8,128)(2,1)S(1)}, bf16[512,512]{1,0:T(8,128)(2,1)}, u32[]{:S(2)}) copy-start(bf16[512,512]{1,0:T(8,128)(2,1)} %get-tuple-element.45) | copy-start | bytes 1572868
  17.5 14.1 %collective-permute-start.4 = (bf16[512,512]{1,0:T(8,128)(2,1)S(1)}, bf16[512,512]{1,0:T(8,128)(2,1)S(1)}, u32[]{:S(2)}, u32[]{:S(2)}) collective-permute-start(bf16[512,512]{1,0:T(8,128)(2,1)S(1)} %copy-done.5), channel_id=1, source_target_pairs={{0,3},{1,2},{2,1},{3,0},{4,7},{5,6},{6,5},{7,4},{8,11},{9,10},{10,... | collective-permute-start | bytes 1572872 | tf_op jit(solution)/shard_map/ppermute | solution.py:336
  17.6 11.0 %collective-permute-start = (bf16[4,144,256]{2,1,0:T(8,128)(2,1)S(1)}, bf16[4,144,256]{2,1,0:T(8,128)(2,1)S(1)}, u32[]{:S(2)}, u32[]{:S(2)}) collective-permute-start(bf16[4,144,256]{2,1,0:T(8,128)(2,1)S(1)} %get-tuple-element.36), channel_id=1, source_target_pairs={{0,4},{1,5},{2,6},{3,7},{4,0},{5,1},{6,2},{7,3},{8,12},{9,13},{10,... | collective-permute-start | bytes 884744 | tf_op jit(solution)/shard_map/ppermute | solution.py:336
  28.5 1.6 %collective-permute-start.3 = (bf16[4,144,256]{2,1,0:T(8,128)(2,1)S(1)}, bf16[4,144,256]{2,1,0:T(8,128)(2,1)S(1)}, u32[]{:S(2)}, u32[]{:S(2)}) collective-permute-start(bf16[4,144,256]{2,1,0:T(8,128)(2,1)S(1)} %get-tuple-element.42), channel_id=1, source_target_pairs={{0,4},{1,5},{2,6},{3,7},{4,0},{5,1},{6,2},{7,3},{8,12},{9,13},{10,... | collective-permute-start | bytes 884744 | tf_op jit(solution)/shard_map/ppermute | solution.py:336
  33.5 1.8 %collective-permute-start.5 = (bf16[4,144,256]{2,1,0:T(8,128)(2,1)S(1)}, bf16[4,144,256]{2,1,0:T(8,128)(2,1)S(1)}, u32[]{:S(2)}, u32[]{:S(2)}) collective-permute-start(bf16[4,144,256]{2,1,0:T(8,128)(2,1)S(1)} %get-tuple-element.46), channel_id=1, source_target_pairs={{0,4},{1,5},{2,6},{3,7},{4,0},{5,1},{6,2},{7,3},{8,12},{9,13},{10,... | collective-permute-start | bytes 884744 | tf_op jit(solution)/shard_map/ppermute | solution.py:336
  33.6 12.8 %copy-start.2 = (bf16[256,1024]{1,0:T(8,128)(2,1)S(1)}, bf16[256,1024]{1,0:T(8,128)(2,1)}, u32[]{:S(2)}) copy-start(bf16[256,1024]{1,0:T(8,128)(2,1)} %o_ref.1) | copy-start | bytes 1572868
  35.8 4.7 %collective-permute-start.6 = (bf16[144,256]{1,0:T(8,128)(2,1)S(1)}, bf16[144,256]{1,0:T(8,128)(2,1)S(1)}, u32[]{:S(2)}, u32[]{:S(2)}) collective-permute-start(bf16[144,256]{1,0:T(8,128)(2,1)S(1)} %get-tuple-element.50), channel_id=1, source_target_pairs={{0,8},{1,9},{2,10},{3,11},{4,12},{5,13},{6,14},{7,15},{8,0},{9,1},... | collective-permute-start | bytes 221192 | tf_op jit(solution)/shard_map/ppermute | solution.py:336
  37.5 8.9 %collective-permute-start.7 = (bf16[144,256]{1,0:T(8,128)(2,1)S(1)}, bf16[144,256]{1,0:T(8,128)(2,1)S(1)}, u32[]{:S(2)}, u32[]{:S(2)}) collective-permute-start(bf16[144,256]{1,0:T(8,128)(2,1)S(1)} %get-tuple-element.51), channel_id=1, source_target_pairs={{0,16},{1,17},{2,18},{3,19},{4,20},{5,21},{6,22},{7,23},{8,24},{9,... | collective-permute-start | bytes 221192 | tf_op jit(solution)/shard_map/ppermute | solution.py:336
  40.1 6.3 %collective-permute-start.8 = (bf16[144,256]{1,0:T(8,128)(2,1)S(1)}, bf16[144,256]{1,0:T(8,128)(2,1)S(1)}, u32[]{:S(2)}, u32[]{:S(2)}) collective-permute-start(bf16[144,256]{1,0:T(8,128)(2,1)S(1)} %get-tuple-element.52), channel_id=1, source_target_pairs={{0,24},{1,25},{2,26},{3,27},{4,28},{5,29},{6,30},{7,31},{8,16},{9,... | collective-permute-start | bytes 221192 | tf_op jit(solution)/shard_map/ppermute | solution.py:336
  47.0 4.8 %collective-permute-start.10 = (bf16[128,256]{1,0:T(8,128)(2,1)S(1)}, bf16[128,256]{1,0:T(8,128)(2,1)S(1)}, u32[]{:S(2)}, u32[]{:S(2)}) collective-permute-start(bf16[128,256]{1,0:T(8,128)(2,1)S(1)} %get-tuple-element.55), channel_id=1, source_target_pairs={{0,2},{1,3},{2,0},{3,1},{4,6},{5,7},{6,4},{7,5},{8,10},{9,11},{10,... | collective-permute-start | bytes 196616 | tf_op jit(solution)/shard_map/ppermute | solution.py:336
  48.6 5.2 %collective-permute-start.11 = (bf16[128,256]{1,0:T(8,128)(2,1)S(1)}, bf16[128,256]{1,0:T(8,128)(2,1)S(1)}, u32[]{:S(2)}, u32[]{:S(2)}) collective-permute-start(bf16[128,256]{1,0:T(8,128)(2,1)S(1)} %get-tuple-element.56), channel_id=1, source_target_pairs={{0,3},{1,2},{2,1},{3,0},{4,7},{5,6},{6,5},{7,4},{8,11},{9,10},{10,... | collective-permute-start | bytes 196616 | tf_op jit(solution)/shard_map/ppermute | solution.py:336
  50.0 4.3 %collective-permute-start.9 = (bf16[128,256]{1,0:T(8,128)(2,1)S(1)}, bf16[128,256]{1,0:T(8,128)(2,1)S(1)}, u32[]{:S(2)}, u32[]{:S(2)}) collective-permute-start(bf16[128,256]{1,0:T(8,128)(2,1)S(1)} %get-tuple-element.54), channel_id=1, source_target_pairs={{0,1},{1,0},{2,3},{3,2},{4,5},{5,4},{6,7},{7,6},{8,9},{9,8},{10,11... | collective-permute-start | bytes 196616 | tf_op jit(solution)/shard_map/ppermute | solution.py:336
